TPU v7x, 32 devices: a whole 2x2x4 slice. The times are simulated.
32 devices in a mesh: head: 4 (over y, x), tok: 8 (over z, core).
Axes of the slice: x: 2, y: 2, z: 4, core: 2. Of those that a mesh axis runs over, the one named last changes fastest.
Arguments:
- stream_one: bfloat16 [16384, 1024], P('tok', 'head'), may hold values from -6 to 6
- stream_two: bfloat16 [16384, 1024], P('tok', 'head'), may hold values from -6 to 6
- buckets: int32 [16384, 4], P('tok'), may hold values from 0 to 703, all different within a row; in each aligned block of 2048 rows (0 to 2047, 2048 to 4095, ...) at most 16 rows name the same one
- lengths: int32 [2], replicated, may hold values from 1024 to 15360, as said below
- gain_attn: bfloat16 [1024], P('head'), may hold values from 0.25 to 1.75
- bias_attn: bfloat16 [1024], P('head'), may hold values from -1.75 to 1.75
- qk_weight: bfloat16 [1024, 1024], P('tok', 'head'), may hold values from -0.25 to 0.25
- value_weight: bfloat16 [1024, 1024], P('tok', 'head'), may hold values from -0.1875 to 0.1875
- out_weight: bfloat16 [1024, 1024], P('head', 'tok'), may hold values from -1.5 to 1.5
- gain_ffn: bfloat16 [1024], P('head'), may hold values from 0.25 to 1.75
- bias_ffn: bfloat16 [1024], P('head'), may hold values from -1.75 to 1.75
- in_weight: bfloat16 [1024, 4096], P('tok', 'head'), may hold values from -0.1875 to 0.1875
- in_bias: bfloat16 [4096], P('head'), may hold values from -3 to 3
- down_weight: bfloat16 [4096, 1024], P('head', 'tok'), may hold values from -0.125 to 0.125
- down_bias: bfloat16 [1024], P('head'), may hold values from -1.75 to 1.75
- cotangent_one: bfloat16 [16384, 1024], P('tok', 'head'), may hold values from -6 to 6
- cotangent_two: bfloat16 [16384, 1024], P('tok', 'head'), may hold values from -6 to 6
Outputs:
- result_one: bfloat16 [16384, 1024], P('tok', 'head')
- result_two: bfloat16 [16384, 1024], P('tok', 'head')
- grad_one: bfloat16 [16384, 1024], P('tok', 'head')
- grad_two: bfloat16 [16384, 1024], P('tok', 'head')
- grad_gain_attn: float32 [1024], P(('head', 'tok'))
- grad_bias_attn: float32 [1024], P(('head', 'tok'))
- grad_qk: float32 [1024, 1024], P('tok', 'head')
- grad_value: float32 [1024, 1024], P('tok', 'head')
- grad_out: float32 [1024, 1024], P('head', 'tok')
- grad_gain_ffn: float32 [1024], P(('head', 'tok'))
- grad_bias_ffn: float32 [1024], P(('head', 'tok'))
- grad_in_weight: float32 [1024, 4096], P('tok', 'head')
- grad_in_bias: float32 [4096], P(('head', 'tok'))
- grad_down_weight: float32 [4096, 1024], P('head', 'tok')
- grad_down_bias: float32 [1024], P(('head', 'tok'))
- bucket_counts: int32 [704], P('tok')
Inputs may be any that keep to these rules, and one draw needn't show every extreme that they name: Each token names 4 different buckets; in each aligned block of 2048 tokens no bucket is named by more than 16 tokens. Two sequences packed in order, lengths summing to 16384; the shorter has fewer than 2048 tokens.
All inputs are finite; a program needn't handle non-finite values.
Results may differ from a plain program's by a relative error of at most 0.012.
The roundings to bfloat16 on the way count: a program that leaves them out, or rounds other values in their place, can miss the bound.
Values may be sent and summed in bfloat16 or wider, within the bound.
No kernel may reach another device: no remote copies, remote signals or barrier semaphores. Data moves between devices by JAX's collectives and lax.ppermute only.
A program may use at most 256 MiB of HBM per device.

v0:
```python
import jax
import jax.numpy as jnp
from jax import lax
from jax.sharding import PartitionSpec as P

DH = 128
CAP = 128
BPD = 88


SELF_SCORE = -10000.0
MASKED = -1000000000.0


def block_ranks(chosen):
    flat_ids = chosen.reshape(-1)
    length_all = flat_ids.shape[0]
    positions = jnp.arange(length_all, dtype=jnp.int32)
    sorted_at = jnp.argsort(flat_ids * length_all + positions)
    ordered = flat_ids[sorted_at]
    starts = jnp.concatenate([jnp.ones((1,), dtype=bool), ordered[1:] != ordered[:-1]])
    run_start = lax.cummax(jnp.where(starts, positions, 0), axis=0)
    rank_of = jnp.zeros((length_all,), jnp.int32).at[sorted_at].set(positions - run_start)
    return rank_of.reshape(chosen.shape)


def norm_rows(row_block, gain_vec, bias_vec):
    row_mean = jnp.mean(row_block, axis=1, keepdims=True)
    centred = row_block - row_mean
    row_scale = lax.rsqrt(jnp.mean(centred * centred, axis=1, keepdims=True) + 1e-05)
    unit_rows = centred * row_scale
    return (unit_rows * gain_vec + bias_vec, unit_rows, row_scale)


def contract_rows(left_side, right_side):
    return lax.dot_general(
        left_side, right_side, (((0,), (0,)), ((), ())), preferred_element_type=jnp.float32
    )


def contract_cols(left_side, right_side):
    return lax.dot_general(
        left_side, right_side, (((1,), (1,)), ((), ())), preferred_element_type=jnp.float32
    )


def smooth_gate(value_in):
    return jax.nn.gelu(value_in, approximate=True)


def score_mask(places, boundary):
    query_place = places[:, :, None]
    key_place = places[:, None, :]
    same_seq = (query_place >= boundary) == (key_place >= boundary)
    allowed = (key_place >= 0) & same_seq & (key_place < query_place)
    itself = key_place == query_place
    return (allowed[:, None], itself[:, None])


def bucket_scores(shared, places, boundary):
    queries = shared.astype(jnp.float32)
    inverse = lax.rsqrt(jnp.sum(queries * queries, axis=3, keepdims=True) + 1e-06)
    unit_keys = queries * inverse
    key_low = unit_keys.astype(jnp.bfloat16)
    scores = jnp.einsum("gqhd,gkhd->ghqk", shared, key_low, preferred_element_type=jnp.float32)
    allowed, itself = score_mask(places, boundary)
    scores = jnp.where(allowed, scores, jnp.where(itself, SELF_SCORE, MASKED))
    return (scores, allowed, inverse, unit_keys, key_low)


def bucket_forward(pieces, boundary):
    shared, values, places = pieces
    groups, capacity, columns = shared.shape
    shared = shared.reshape(groups, capacity, columns // DH, DH)
    values = values.reshape(groups, capacity, columns // DH, DH)
    scores, allowed, inverse, unit_keys, key_low = bucket_scores(shared, places, boundary)
    highest = jnp.max(scores, axis=3, keepdims=True)
    totals = highest + jnp.log(jnp.sum(jnp.exp(scores - highest), axis=3, keepdims=True))
    weights_low = jnp.exp(scores - totals).astype(jnp.bfloat16)
    mixture = jnp.einsum("ghqk,gkhd->gqhd", weights_low, values, preferred_element_type=jnp.float32)
    return (mixture.reshape(groups, capacity, columns), jnp.transpose(totals[..., 0], (0, 2, 1)))


def bucket_backward(pieces, boundary):
    shared, values, places, totals, grad_mix, grad_totals = pieces
    groups, capacity, columns = shared.shape
    head_count = columns // DH
    shared = shared.reshape(groups, capacity, head_count, DH)
    values = values.reshape(groups, capacity, head_count, DH)
    scores, allowed, inverse, unit_keys, key_low = bucket_scores(shared, places, boundary)
    probability = jnp.exp(scores - jnp.transpose(totals, (0, 2, 1))[..., None])
    grad_low = grad_mix.reshape(groups, capacity, head_count, DH).astype(jnp.bfloat16)
    grad_prob = jnp.einsum("gqhd,gkhd->ghqk", grad_low, values, preferred_element_type=jnp.float32)
    grad_values = jnp.einsum(
        "ghqk,gqhd->gkhd",
        probability.astype(jnp.bfloat16),
        grad_low,
        preferred_element_type=jnp.float32,
    )
    inner_sum = jnp.sum(probability * grad_prob, axis=3, keepdims=True)
    lse_term = jnp.transpose(grad_totals, (0, 2, 1))[..., None]
    grad_scores = jnp.where(allowed, probability * (grad_prob - inner_sum + lse_term), 0.0).astype(
        jnp.bfloat16
    )
    grad_query = jnp.einsum(
        "ghqk,gkhd->gqhd", grad_scores, key_low, preferred_element_type=jnp.float32
    )
    grad_keys = jnp.einsum(
        "ghqk,gqhd->gkhd", grad_scores, shared, preferred_element_type=jnp.float32
    )
    along_key = jnp.sum(unit_keys * grad_keys, axis=3, keepdims=True)
    grad_shared = grad_query + inverse * (grad_keys - unit_keys * along_key)
    return (
        grad_shared.reshape(groups, capacity, columns),
        grad_values.reshape(groups, capacity, columns),
    )


def shards(
    stream_one,
    stream_two,
    buckets,
    lengths,
    gain_attn,
    bias_attn,
    qk_weight,
    value_weight,
    out_weight,
    gain_ffn,
    bias_ffn,
    in_weight,
    in_bias,
    down_weight,
    down_bias,
    cotangent_one,
    cotangent_two,
):
    tok_count = lax.axis_size("tok")
    tok_rows = stream_one.shape[0]
    shard_width = stream_one.shape[1]
    full_width = shard_width * lax.axis_size("head")
    rounds = buckets.shape[1]
    slot_most = CAP // tok_count
    group_size = max(1, 512 // CAP)
    boundary = lengths[0]
    feature_start = lax.axis_index("head") * shard_width
    whole_qk, whole_value, whole_out, whole_in, whole_down = (
        lax.all_gather(qk_weight, "tok", axis=0, tiled=True),
        lax.all_gather(value_weight, "tok", axis=0, tiled=True),
        lax.all_gather(out_weight, "tok", axis=1, tiled=True),
        lax.all_gather(in_weight, "tok", axis=0, tiled=True),
        lax.all_gather(down_weight, "tok", axis=1, tiled=True),
    )
    columns = whole_qk.shape[1]
    head_count = columns // DH

    def full_rows(shard_in, gain_vec, bias_vec):
        return (
            lax.all_gather(shard_in, "head", axis=1, tiled=True),
            lax.all_gather(gain_vec, "head", axis=0, tiled=True),
            lax.all_gather(bias_vec, "head", axis=0, tiled=True),
        )

    def grad_rows(shard_in):
        return lax.all_gather(shard_in, "head", axis=1, tiled=True)

    def grad_total(grad_pairs):
        summed = jnp.zeros((shard_width * lax.axis_size("head"), tok_rows), jnp.float32)
        for grad_low, weight_full in grad_pairs:
            summed = summed + contract_cols(weight_full, grad_low)
        return jnp.transpose(lax.psum_scatter(summed, "head", scatter_dimension=0, tiled=True))

    def norm_back(grad_norm, unit_part, row_scale, gain_vec):
        grad_unit = grad_norm * gain_vec.astype(jnp.float32)
        sums_one, sums_two = lax.psum(
            (jnp.sum(grad_unit, axis=1), jnp.sum(grad_unit * unit_part, axis=1)), "head"
        )
        grad_in_rows = row_scale * (
            grad_unit
            - sums_one[:, None] / full_width
            - unit_part * (sums_two[:, None] / full_width)
        )
        return (grad_in_rows, jnp.sum(grad_norm * unit_part, axis=0), jnp.sum(grad_norm, axis=0))

    rank_of = block_ranks(buckets)
    slot_of = (buckets * slot_most + rank_of).reshape(-1)
    entries = tok_rows * rounds
    bucket_total = BPD * CAP // slot_most
    sources = (
        jnp.full((bucket_total * slot_most,), entries, jnp.int32)
        .at[slot_of]
        .set(jnp.arange(entries, dtype=jnp.int32))
    )
    source_rows = sources // rounds
    places_out = jnp.where(
        sources < entries, source_rows + lax.axis_index("tok") * tok_rows, -1
    ).reshape(bucket_total, slot_most)

    def token_slots(row_block):
        padded = jnp.concatenate(
            [row_block, jnp.zeros((1, row_block.shape[1]), row_block.dtype)], axis=0
        )
        return padded[source_rows].reshape(bucket_total, slot_most, row_block.shape[1])

    def entry_slots(entry_block):
        padded = jnp.concatenate(
            [entry_block, jnp.zeros((1, entry_block.shape[1]), entry_block.dtype)], axis=0
        )
        return padded[sources].reshape(bucket_total, slot_most, entry_block.shape[1])

    def send_buckets(shared_tok, value_tok):
        return (
            lax.all_to_all(token_slots(shared_tok), "tok", split_axis=0, concat_axis=1, tiled=True),
            lax.all_to_all(token_slots(value_tok), "tok", split_axis=0, concat_axis=1, tiled=True),
        )

    def grouped(array_in):
        return array_in.reshape((array_in.shape[0] // group_size, group_size) + array_in.shape[1:])

    def forward_group(pieces):
        return bucket_forward(pieces, boundary)

    def backward_group(pieces):
        return bucket_backward(pieces, boundary)

    rows_two, gain_full, bias_full = full_rows(stream_two, gain_attn, bias_attn)
    normed_full, unit_full, scale_one = norm_rows(
        rows_two.astype(jnp.float32), gain_full.astype(jnp.float32), bias_full.astype(jnp.float32)
    )
    unit_one = lax.dynamic_slice_in_dim(unit_full, feature_start, shard_width, 1)
    normed = normed_full.astype(jnp.bfloat16)
    shared_tok = jnp.dot(normed, whole_qk, preferred_element_type=jnp.float32).astype(jnp.bfloat16)
    value_tok = jnp.dot(normed, whole_value, preferred_element_type=jnp.float32).astype(
        jnp.bfloat16
    )
    shared_slots, value_slots = send_buckets(shared_tok, value_tok)
    place_slots = lax.all_to_all(places_out, "tok", split_axis=0, concat_axis=1, tiled=True)
    bucket_counts = jnp.sum((place_slots >= 0).astype(jnp.int32), axis=1)
    slot_buckets = shared_slots.shape[0]
    mix_slots, total_slots = lax.map(
        forward_group, (grouped(shared_slots), grouped(value_slots), grouped(place_slots))
    )
    back_mix, back_total = (
        lax.all_to_all(
            mix_slots.reshape(slot_buckets, CAP, columns),
            "tok",
            split_axis=1,
            concat_axis=0,
            tiled=True,
        ),
        lax.all_to_all(
            total_slots.reshape(slot_buckets, CAP, head_count),
            "tok",
            split_axis=1,
            concat_axis=0,
            tiled=True,
        ),
    )
    round_mix = back_mix.reshape(bucket_total * slot_most, columns)[slot_of].reshape(
        tok_rows, rounds, head_count, DH
    )
    round_total = back_total.reshape(bucket_total * slot_most, head_count)[slot_of].reshape(
        tok_rows, rounds, head_count
    )
    round_weight = jax.nn.softmax(round_total, axis=1)
    attended = (
        jnp.sum(round_weight[..., None] * round_mix, axis=1)
        .reshape(tok_rows, columns)
        .astype(jnp.bfloat16)
    )
    attended_full = lax.all_gather(attended, "head", axis=1, tiled=True)
    out_full = lax.all_gather(whole_out, "head", axis=0, tiled=True)
    out_columns = lax.dynamic_slice_in_dim(out_full, feature_start, shard_width, 1)
    attn_term = jnp.dot(attended_full, out_columns, preferred_element_type=jnp.float32)
    result_one = (stream_one.astype(jnp.float32) + attn_term).astype(jnp.bfloat16)
    rows_one, gain_two, bias_two = full_rows(result_one, gain_ffn, bias_ffn)
    normed_two_full, unit_two_full, scale_two = norm_rows(
        rows_one.astype(jnp.float32), gain_two.astype(jnp.float32), bias_two.astype(jnp.float32)
    )
    unit_two = lax.dynamic_slice_in_dim(unit_two_full, feature_start, shard_width, 1)
    normed_two = normed_two_full.astype(jnp.bfloat16)
    pre_act = jnp.dot(normed_two, whole_in, preferred_element_type=jnp.float32) + in_bias.astype(
        jnp.float32
    )
    hidden, gate_back = jax.vjp(smooth_gate, pre_act)
    hidden_low = hidden.astype(jnp.bfloat16)
    result_two = (
        stream_two.astype(jnp.float32)
        + jnp.transpose(
            lax.psum_scatter(
                lax.dot_general(
                    whole_down,
                    hidden_low,
                    (((0,), (1,)), ((), ())),
                    preferred_element_type=jnp.float32,
                ),
                "head",
                scatter_dimension=0,
                tiled=True,
            )
        )
        + down_bias.astype(jnp.float32)
    ).astype(jnp.bfloat16)
    rows_grad_two = grad_rows(cotangent_two)
    grad_down_part = contract_rows(hidden_low, rows_grad_two)
    grad_hidden = contract_cols(rows_grad_two, whole_down)
    grad_pre = gate_back(grad_hidden)[0].astype(jnp.bfloat16)
    grad_in_bias_part = jnp.sum(grad_pre.astype(jnp.float32), axis=0)
    grad_in_part = contract_rows(normed_two, grad_pre)
    grad_norm_two = grad_total(((grad_pre, whole_in),))
    grad_from_ffn, grad_gain_two, grad_bias_two = norm_back(
        grad_norm_two, unit_two, scale_two, gain_ffn
    )
    grad_down_bias_part = jnp.sum(cotangent_two.astype(jnp.float32), axis=0)
    carried = cotangent_one.astype(jnp.float32) + grad_from_ffn
    grad_one = carried.astype(jnp.bfloat16)
    rows_grad_one = grad_rows(grad_one)
    grad_out_part = contract_rows(attended, rows_grad_one)
    grad_attended = contract_cols(rows_grad_one, whole_out)
    grad_view = grad_attended.reshape(tok_rows, 1, head_count, DH)
    grad_mix_tok = round_weight[..., None] * grad_view
    mix_dot = jnp.sum(grad_view * round_mix, axis=3)
    grad_total_tok = round_weight * (
        mix_dot - jnp.sum(round_weight * mix_dot, axis=1, keepdims=True)
    )
    grad_mix_slots, grad_total_slots = (
        lax.all_to_all(
            entry_slots(grad_mix_tok.reshape(entries, columns)),
            "tok",
            split_axis=0,
            concat_axis=1,
            tiled=True,
        ),
        lax.all_to_all(
            entry_slots(grad_total_tok.reshape(entries, head_count)),
            "tok",
            split_axis=0,
            concat_axis=1,
            tiled=True,
        ),
    )
    again_shared, again_value = send_buckets(shared_tok, value_tok)
    grad_shared_slots, grad_value_slots = lax.map(
        backward_group,
        (
            grouped(again_shared),
            grouped(again_value),
            grouped(place_slots),
            total_slots,
            grouped(grad_mix_slots),
            grouped(grad_total_slots),
        ),
    )
    back_shared, back_value = (
        lax.all_to_all(
            grad_shared_slots.reshape(slot_buckets, CAP, columns),
            "tok",
            split_axis=1,
            concat_axis=0,
            tiled=True,
        ),
        lax.all_to_all(
            grad_value_slots.reshape(slot_buckets, CAP, columns),
            "tok",
            split_axis=1,
            concat_axis=0,
            tiled=True,
        ),
    )
    grad_shared_tok = jnp.sum(
        back_shared.reshape(bucket_total * slot_most, columns)[slot_of].reshape(
            tok_rows, rounds, columns
        ),
        axis=1,
    ).astype(jnp.bfloat16)
    grad_value_tok = jnp.sum(
        back_value.reshape(bucket_total * slot_most, columns)[slot_of].reshape(
            tok_rows, rounds, columns
        ),
        axis=1,
    ).astype(jnp.bfloat16)
    grad_qk_part = contract_rows(normed, grad_shared_tok)
    grad_value_part = contract_rows(normed, grad_value_tok)
    grad_norm_one = grad_total(((grad_shared_tok, whole_qk), (grad_value_tok, whole_value)))
    grad_from_attn, grad_gain_one, grad_bias_one = norm_back(
        grad_norm_one, unit_one, scale_one, gain_attn
    )
    grad_two = (cotangent_two.astype(jnp.float32) + grad_from_attn).astype(jnp.bfloat16)
    all_sums = (
        lax.psum_scatter(grad_gain_one, "tok", scatter_dimension=0, tiled=True),
        lax.psum_scatter(grad_bias_one, "tok", scatter_dimension=0, tiled=True),
        lax.psum_scatter(grad_qk_part, "tok", scatter_dimension=0, tiled=True),
        lax.psum_scatter(grad_value_part, "tok", scatter_dimension=0, tiled=True),
        lax.psum_scatter(grad_out_part, "tok", scatter_dimension=1, tiled=True),
        lax.psum_scatter(grad_gain_two, "tok", scatter_dimension=0, tiled=True),
        lax.psum_scatter(grad_bias_two, "tok", scatter_dimension=0, tiled=True),
        lax.psum_scatter(grad_in_part, "tok", scatter_dimension=0, tiled=True),
        lax.psum_scatter(grad_in_bias_part, "tok", scatter_dimension=0, tiled=True),
        lax.psum_scatter(grad_down_part, "tok", scatter_dimension=1, tiled=True),
        lax.psum_scatter(grad_down_bias_part, "tok", scatter_dimension=0, tiled=True),
    )
    return (
        result_one,
        result_two,
        grad_one,
        grad_two,
        all_sums[0],
        all_sums[1],
        all_sums[2],
        all_sums[3],
        all_sums[4],
        all_sums[5],
        all_sums[6],
        all_sums[7],
        all_sums[8],
        all_sums[9],
        all_sums[10],
        bucket_counts,
    )


def solution(mesh):
    placed = (
        P("tok", "head"),
        P("tok", "head"),
        P("tok", None),
        P(),
        P("head"),
        P("head"),
        P("tok", "head"),
        P("tok", "head"),
        P("head", "tok"),
        P("head"),
        P("head"),
        P("tok", "head"),
        P("head"),
        P("head", "tok"),
        P("head"),
        P("tok", "head"),
        P("tok", "head"),
    )
    return jax.shard_map(
        shards,
        mesh=mesh,
        in_specs=placed,
        out_specs=(
            P("tok", "head"),
            P("tok", "head"),
            P("tok", "head"),
            P("tok", "head"),
            P(("head", "tok")),
            P(("head", "tok")),
            P("tok", "head"),
            P("tok", "head"),
            P("head", "tok"),
            P(("head", "tok")),
            P(("head", "tok")),
            P("tok", "head"),
            P(("head", "tok")),
            P("head", "tok"),
            P(("head", "tok")),
            P("tok"),
        ),
        check_vma=False,
    )
```

profile of v0, /device:TPU:0, one launch (start us, length us, event | category | flops | bytes accessed | tf_op | source)
XLA Modules:
  0.0 2846.3 jit_solution(17365873935538855249)
XLA Ops:
  16.5 45.5 %gather_fusion = s32[8192]{0:T(1024)S(1)} fusion(s32[8192]{0:T(1024)S(1)} %reshape.344, s32[8192]{0:T(1024)S(1)} %get-tuple-element.271), kind=kCustom, calls=%fused_computation | custom fusion | bytes 98304 | tf_op jit(solution)/shard_map/gather | solution.py:20
  62.9 30.5 %scatter_custom_fusion = s32[8192]{0:T(1024)S(1)} fusion(s32[8192]{0:T(1024)S(1)} %get-tuple-element.272, s32[8192]{0:T(1024)S(1)} %bitcast_subtract_fusion, s32[]{:T(128)} %copy.282), kind=kCustom, calls=%fused_computation.180 | custom fusion | bytes 32772 | tf_op jit(solution)/shard_map/scatter | solution.py:23
  96.0 30.5 %scatter_custom_fusion.1 = s32[11264]{0:T(1024)S(1)} fusion(s32[8192]{0:T(1024)S(1)} %bitcast.265, s32[8192]{0:T(1024)S(1)} %iota.33, s32[]{:T(128)} %constant.70.clone.1), kind=kCustom, calls=%fused_computation.176 | custom fusion | bytes 45060 | tf_op jit(solution)/shard_map/scatter | solution.py:192
  150.6 15.9 all_gather.48
  179.0 44.9 %gather_fusion.1 = bf16[11264,256]{1,0:T(8,128)(2,1)} fusion(bf16[2049,256]{1,0:T(8,128)(2,1)S(1)} %concatenate.19, s32[11264]{0:T(1024)S(1)} %get-tuple-element.270), kind=kCustom, calls=%fused_computation.1 | custom fusion | bytes 11579392 | tf_op jit(solution)/shard_map/gather | solution.py:203
  228.8 135.8 %all_gather.49 = bf16[1024,256]{1,0:T(8,128)(2,1)S(1)} all-gather(bf16[128,256]{1,0:T(8,128)(2,1)S(1)} %copy-done.34), channel_id=1, replica_groups=mesh['head'=4,'tok'=8] {'tok'}, dimensions={0}, use_global_device_ids=true | all-gather | bytes 589824 | tf_op jit(solution)/shard_map/all_gather | solution.py:148
  368.8 44.9 %gather_fusion.2 = bf16[11264,256]{1,0:T(8,128)(2,1)} fusion(bf16[2049,256]{1,0:T(8,128)(2,1)S(1)} %concatenate.22, s32[11264]{0:T(1024)S(1)} %get-tuple-element.270), kind=kCustom, calls=%fused_computation.2 | custom fusion | bytes 11579392 | tf_op jit(solution)/shard_map/gather | solution.py:203
  433.1 113.0 %all-to-all-done.2 = bf16[704,16,256]{2,1,0:T(8,128)(2,1)} async-done(((bf16[704,16,256]{2,1,0:T(8,128)(2,1)}), bf16[704,16,256]{2,1,0:T(8,128)(2,1)}, u32[]{:S(2)}, u32[]{:S(2)}) %all-to-all-start.2) | async-done | bytes 5767200 | tf_op jit(solution)/shard_map/all_to_all | solution.py:213
  566.2 69.2 %while.24 = (s32[]{:T(128)}, f32[22,4,128,256]{2,3,1,0:T(8,128)}, f32[22,4,128,2]{2,3,1,0:T(2,128)S(1)}, bf16[22,4,128,256]{2,3,1,0:T(8,128)(2,1)}, s32[22,4,128...) while((s32[]{:T(128)}, f32[22,4,128,256]{2,3,1,0:T(8,128)}, ...), condition=%wide.region_11.12_spmd, body=%wide.region_7.11_spmd.sunk | while | flops 69074944 | bytes 5697649 | solution.py:240
  657.2 259.7 %all_gather.51 = bf16[256,1024]{1,0:T(8,128)(2,1)} all-gather(bf16[256,128]{1,0:T(8,128)(2,1)S(1)} %copy-done.35), channel_id=1, replica_groups=mesh['head'=4,'tok'=8] {'tok'}, dimensions={1}, use_global_device_ids=true | all-gather | bytes 589824 | tf_op jit(solution)/shard_map/all_gather | solution.py:150
  921.0 30.6 %gather_fusion.3 = f32[8192,2]{1,0:T(8,128)} fusion(f32[11264,2]{1,0:T(8,128)} %bitcast.222, s32[8192]{0:T(1024)S(1)} %broadcast_clamp_fusion), kind=kCustom, calls=%fused_computation.3 | custom fusion | bytes 163840 | tf_op jit(solution)/shard_map/gather | solution.py:262
  991.3 35.7 %gather_fusion.4 = f32[8192,256]{1,0:T(8,128)} fusion(f32[11264,256]{1,0:T(8,128)} %bitcast.220, s32[8192]{0:T(1024)S(1)} %broadcast_clamp_fusion), kind=kCustom, calls=%fused_computation.4 | custom fusion | bytes 16809984 | tf_op jit(solution)/shard_map/gather | solution.py:259
  1053.3 51.3 %all-gather.15.cloned.1.call-done = bf16[2048,1024]{1,0:T(8,128)(2,1)} async-done(((bf16[2048,256]{1,0:T(8,128)(2,1)}), bf16[2048,1024]{1,0:T(8,128)(2,1)}) %all-gather.15.cloned.1.call-update) | async-done | bytes 4194320 | tf_op jit(solution)/shard_map/all_gather | solution.py:271
  1126.4 35.5 %all-gather.19.cloned.1.call-done = bf16[2048,1024]{1,0:T(8,128)(2,1)} async-done(((bf16[2048,256]{1,0:T(8,128)(2,1)}), bf16[2048,1024]{1,0:T(8,128)(2,1)}) %all-gather.19.cloned.1.call-update) | async-done | bytes 4194320 | tf_op jit(solution)/shard_map/all_gather | solution.py:159
  1167.2 25.3 all-gather.21.cloned.1.call-done
  1203.5 20.8 all-gather.23.cloned.1.call-done
  1224.3 53.5 %all-gather.25.cloned.1.call-done = bf16[2048,1024]{1,0:T(8,128)(2,1)} async-done(((bf16[2048,256]{1,0:T(8,128)(2,1)}), bf16[2048,1024]{1,0:T(8,128)(2,1)}) %all-gather.25.cloned.1.call-update) | async-done | bytes 4194320 | tf_op jit(solution)/shard_map/all_gather | solution.py:165
  1308.1 80.9 %reduce-scatter.11.cloned.1.call-done = f32[256,2048]{0,1:T(8,128)} async-done(((f32[1024,2048]{0,1:T(8,128)}), f32[256,2048]{0,1:T(8,128)}) %reduce-scatter.11.cloned.1.call-update) | async-done | bytes 2097168 | tf_op jit(solution)/shard_map/reduce_scatter | solution.py:171
  1411.1 52.6 %all-gather.27.cloned.1.call-done = bf16[2048,1024]{1,0:T(8,128)(2,1)} async-done(((bf16[2048,256]{1,0:T(8,128)(2,1)}), bf16[2048,1024]{1,0:T(8,128)(2,1)}) %all-gather.27.cloned.1.call-update) | async-done | bytes 4194320 | tf_op jit(solution)/shard_map/all_gather | solution.py:165
  1502.1 40.0 %gather_fusion.6 = f32[11264,2]{1,0:T(8,128)} fusion(f32[8193,2]{1,0:T(8,128)} %concatenate.24, s32[11264]{0:T(1024)S(1)} %copy-done.23), kind=kCustom, calls=%fused_computation.6 | custom fusion | bytes 225280 | tf_op jit(solution)/shard_map/gather | solution.py:209
  1569.0 44.9 %gather_fusion.5 = bf16[11264,256]{1,0:T(8,128)(2,1)} fusion(bf16[8193,256]{1,0:T(8,128)(2,1)} %concatenate.23, s32[11264]{0:T(1024)S(1)} %copy-done.23), kind=kCustom, calls=%fused_computation.5 | custom fusion | bytes 11579392 | tf_op jit(solution)/shard_map/gather | solution.py:209
  1621.9 124.9 %all-to-all-done.5 = bf16[704,16,256]{2,1,0:T(8,128)(2,1)} async-done(((bf16[704,16,256]{2,1,0:T(8,128)(2,1)}), bf16[704,16,256]{2,1,0:T(8,128)(2,1)}, u32[]{:S(2)}, u32[]{:S(2)}) %all-to-all-start.5) | async-done | bytes 5767200 | tf_op jit(solution)/shard_map/all_to_all | solution.py:327
  1764.1 171.3 %while.25 = (s32[]{:T(128)}, f32[22,4,128,256]{2,3,1,0:T(8,128)}, f32[22,4,128,256]{2,3,1,0:T(8,128)}, bf16[22,4,128,256]{2,3,1,0:T(8,128)(2,1)}, s32[22,4,128]{...) while((s32[]{:T(128)}, f32[22,4,128,256]{2,3,1,0:T(8,128)}, ...), condition=%wide.region_29.30_spmd, body=%wide.region_25.29_spmd.sunk | while | flops 172495232 | bytes 13959313 | solution.py:343
  1965.2 239.0 %all-to-all-done.7 = f32[88,128,256]{2,0,1:T(8,128)} async-done(((f32[88,128,256]{2,0,1:T(8,128)}), f32[88,128,256]{2,0,1:T(8,128)}, u32[]{:S(2)}, u32[]{:S(2)}) %all-to-all-start.7) | async-done | bytes 11534368 | tf_op jit(solution)/shard_map/all_to_all | solution.py:355
  2234.2 36.0 %gather_fusion.7 = f32[8192,256]{1,0:T(8,128)} fusion(f32[11264,256]{1,0:T(8,128)} %bitcast.221, s32[8192]{0:T(1024)S(1)} %copy-done.20), kind=kCustom, calls=%fused_computation.7 | custom fusion | bytes 16809984 | tf_op jit(solution)/shard_map/gather | solution.py:371
  2280.0 180.8 %all-to-all-done.8 = f32[88,128,256]{2,0,1:T(8,128)} async-done(((f32[88,128,256]{2,0,1:T(8,128)}), f32[88,128,256]{2,0,1:T(8,128)}, u32[]{:S(2)}, u32[]{:S(2)}) %all-to-all-start.8) | async-done | bytes 11534368 | tf_op jit(solution)/shard_map/all_to_all | solution.py:362
  2472.9 35.6 %gather_fusion.8 = f32[8192,256]{1,0:T(8,128)} fusion(f32[11264,256]{1,0:T(8,128)} %bitcast.219, s32[8192]{0:T(1024)S(1)} %copy-done.20), kind=kCustom, calls=%fused_computation.8 | custom fusion | bytes 16809984 | tf_op jit(solution)/shard_map/gather | solution.py:377
  2593.7 40.4 %reduce-scatter.13.cloned.1.call-done = f32[256,2048]{0,1:T(8,128)} async-done(((f32[1024,2048]{0,1:T(8,128)}), f32[256,2048]{0,1:T(8,128)}) %reduce-scatter.13.cloned.1.call-update) | async-done | bytes 2097168 | tf_op jit(solution)/shard_map/reduce_scatter | solution.py:171
  2687.8 51.2 %reduce-scatter.21.cloned.1.call-done = f32[128,1024]{1,0:T(8,128)} async-done(((f32[1024,1024]{1,0:T(8,128)}), f32[128,1024]{1,0:T(8,128)}) %reduce-scatter.21.cloned.1.call-update) | async-done | bytes 524304 | tf_op jit(solution)/shard_map/reduce_scatter | solution.py:397
  2739.0 33.3 %reduce-scatter.19.cloned.1.call-done = f32[256,128]{1,0:T(8,128)} async-done(((f32[256,1024]{1,0:T(8,128)}), f32[256,128]{1,0:T(8,128)}) %reduce-scatter.19.cloned.1.call-update) | async-done | bytes 131088 | tf_op jit(solution)/shard_map/reduce_scatter | solution.py:394
  2772.3 33.5 %reduce-scatter.15.cloned.1.call-done = f32[128,256]{1,0:T(8,128)} async-done(((f32[1024,256]{1,0:T(8,128)}), f32[128,256]{1,0:T(8,128)}) %reduce-scatter.15.cloned.1.call-update) | async-done | bytes 131088 | tf_op jit(solution)/shard_map/reduce_scatter | solution.py:392
  2805.8 33.5 %reduce-scatter.17.cloned.1.call-done = f32[128,256]{1,0:T(8,128)} async-done(((f32[1024,256]{1,0:T(8,128)}), f32[128,256]{1,0:T(8,128)}) %reduce-scatter.17.cloned.1.call-update) | async-done | bytes 131088 | tf_op jit(solution)/shard_map/reduce_scatter | solution.py:393
  (955 shorter events, 826.7 us)
Async XLA Ops:
  7.2 159.3 %all-gather.13.cloned.1.call-start = ((), (), s32[]{:S(2)}) async-start(), calls=%async_computation.17 | async-start | bytes 5242880 | tf_op jit(solution)/shard_map/all_gather | solution.py:159
  62.1 88.5 %copy-start.33 = (bf16[128,256]{1,0:T(8,128)(2,1)S(1)}, bf16[128,256]{1,0:T(8,128)(2,1)}, u32[]{:S(2)}) copy-start(bf16[128,256]{1,0:T(8,128)(2,1)} %param.28) | copy-start | bytes 196612
  128.1 95.8 %all-to-all-start.1 = ((s32[8,88,16]{1,2,0:T(8,128)}), s32[8,88,16]{1,2,0:T(8,128)S(1)}, u32[]{:S(2)}, u32[]{:S(2)}) async-start(s32[8,88,16]{1,2,0:T(8,128)} %copy.195), calls=%async_computation.1 | async-start | bytes 131072 | tf_op jit(solution)/shard_map/all_to_all | solution.py:237
  223.9 194.6 %copy-start.21 = (s32[8,88,16]{1,2,0:T(8,128)}, s32[8,88,16]{1,2,0:T(8,128)S(1)}, u32[]{:S(2)}) copy-start(s32[8,88,16]{1,2,0:T(8,128)S(1)} %all-to-all-done.1) | copy-start | bytes 135172
  223.9 189.8 %all-to-all-start = ((bf16[704,16,256]{2,1,0:T(8,128)(2,1)}), bf16[704,16,256]{2,1,0:T(8,128)(2,1)}, u32[]{:S(2)}, u32[]{:S(2)}) async-start(bf16[704,16,256]{2,1,0:T(8,128)(2,1)} %bitcast.244), calls=%async_computation | async-start | bytes 11534336 | tf_op jit(solution)/shard_map/all_to_all | solution.py:214
  413.7 132.4 %all-to-all-start.2 = ((bf16[704,16,256]{2,1,0:T(8,128)(2,1)}), bf16[704,16,256]{2,1,0:T(8,128)(2,1)}, u32[]{:S(2)}, u32[]{:S(2)}) async-start(bf16[704,16,256]{2,1,0:T(8,128)(2,1)} %bitcast.243), calls=%async_computation.2 | async-start | bytes 11534336 | tf_op jit(solution)/shard_map/all_to_all | solution.py:213
  636.1 15.6 all-to-all-start.3
  651.8 327.6 %all-to-all-start.4 = ((f32[88,128,256]{2,0,1:T(8,128)}), f32[88,128,256]{2,0,1:T(8,128)}, u32[]{:S(2)}, u32[]{:S(2)}) async-start(f32[88,128,256]{2,0,1:T(8,128)} %copy.233), calls=%async_computation.4 | async-start | bytes 23068672 | tf_op jit(solution)/shard_map/all_to_all | solution.py:244
  657.2 396.1 %all-gather.17.cloned.1.call-start = ((), (), s32[]{:S(2)}) async-start(), calls=%async_computation.19 | async-start | bytes 2621440 | tf_op jit(solution)/shard_map/all_gather | solution.py:272
  917.0 187.7 %all-gather.15.cloned.1.call-start = ((), (), s32[]{:S(2)}) async-start(), calls=%async_computation.18 | async-start | bytes 5242880 | tf_op jit(solution)/shard_map/all_gather | solution.py:271
  1053.2 108.8 %all-gather.19.cloned.1.call-start = ((), (), s32[]{:S(2)}) async-start(), calls=%async_computation.20 | async-start | bytes 5242880 | tf_op jit(solution)/shard_map/all_gather | solution.py:159
  1109.2 83.3 %all-gather.21.cloned.1.call-start = ((), (), s32[]{:S(2)}) async-start(), calls=%async_computation.21 | async-start | bytes 2359296 | tf_op jit(solution)/shard_map/all_gather | solution.py:151
  1109.8 114.5 %all-gather.23.cloned.1.call-start = ((), (), s32[]{:S(2)}) async-start(), calls=%async_computation.22 | async-start | bytes 2359296 | tf_op jit(solution)/shard_map/all_gather | solution.py:152
  1110.4 167.5 %all-gather.25.cloned.1.call-start = ((), (), s32[]{:S(2)}) async-start(), calls=%async_computation.24 | async-start | bytes 5242880 | tf_op jit(solution)/shard_map/all_gather | solution.py:165
  1111.1 277.8 %reduce-scatter.11.cloned.1.call-start = ((), (), s32[]{:S(2)}) async-start(), calls=%async_computation.25 | async-start | bytes 10485760 | tf_op jit(solution)/shard_map/reduce_scatter | solution.py:171
  1165.4 137.1 %copy-start.29 = (f32[2048]{0:T(1024)}, f32[2048]{0:T(1024)S(1)}, u32[]{:S(2)}) copy-start(f32[2048]{0:T(1024)S(1)} %broadcast_multiply_fusion.5) | copy-start | bytes 24580
  1167.2 240.4 %copy-start.31 = (f32[2048]{0:T(1024)}, f32[2048]{0:T(1024)S(1)}, u32[]{:S(2)}) copy-start(f32[2048]{0:T(1024)S(1)} %add_rsqrt_fusion.2) | copy-start | bytes 24580
  1302.4 161.2 %all-gather.27.cloned.1.call-start = ((), (), s32[]{:S(2)}) async-start(), calls=%async_computation.26 | async-start | bytes 5242880 | tf_op jit(solution)/shard_map/all_gather | solution.py:165
  1302.5 105.1 %copy-start.18 = (bf16[2048,256]{1,0:T(8,128)(2,1)S(1)}, bf16[2048,256]{1,0:T(8,128)(2,1)}, u32[]{:S(2)}) copy-start(bf16[2048,256]{1,0:T(8,128)(2,1)} %param.36) | copy-start | bytes 3145732
  1308.1 155.6 %copy-start.17 = (bf16[256,1024]{1,0:T(8,128)(2,1)S(1)}, bf16[256,1024]{1,0:T(8,128)(2,1)}, u32[]{:S(2)}) copy-start(bf16[256,1024]{1,0:T(8,128)(2,1)} %all_gather.51) | copy-start | bytes 1572868
  1550.5 63.4 %all-to-all-start.6 = ((f32[8,1,2816]{2,1,0:T(1,128)}), f32[8,1,2816]{2,1,0:T(1,128)S(1)}, u32[]{:S(2)}, u32[]{:S(2)}) async-start(f32[8,1,2816]{2,1,0:T(1,128)} %reshape.486), calls=%async_computation.8 | async-start | bytes 180224 | tf_op jit(solution)/shard_map/all_to_all | solution.py:334
  1613.9 132.9 %all-to-all-start.5 = ((bf16[704,16,256]{2,1,0:T(8,128)(2,1)}), bf16[704,16,256]{2,1,0:T(8,128)(2,1)}, u32[]{:S(2)}, u32[]{:S(2)}) async-start(bf16[704,16,256]{2,1,0:T(8,128)(2,1)} %bitcast.242), calls=%async_computation.7 | async-start | bytes 11534336 | tf_op jit(solution)/shard_map/all_to_all | solution.py:327
  1947.7 256.6 %all-to-all-start.7 = ((f32[88,128,256]{2,0,1:T(8,128)}), f32[88,128,256]{2,0,1:T(8,128)}, u32[]{:S(2)}, u32[]{:S(2)}) async-start(f32[88,128,256]{2,0,1:T(8,128)} %copy.237), calls=%async_computation.9 | async-start | bytes 23068672 | tf_op jit(solution)/shard_map/all_to_all | solution.py:355
  1965.2 244.8 %copy-start.45 = (bf16[1024,1024]{1,0:T(8,128)(2,1)S(1)}, bf16[1024,1024]{1,0:T(8,128)(2,1)}, u32[]{:S(2)}) copy-start(bf16[1024,1024]{1,0:T(8,128)(2,1)} %all-gather.23.cloned.1.call-done) | copy-start | bytes 6291460
  2204.2 256.6 %all-to-all-start.8 = ((f32[88,128,256]{2,0,1:T(8,128)}), f32[88,128,256]{2,0,1:T(8,128)}, u32[]{:S(2)}, u32[]{:S(2)}) async-start(f32[88,128,256]{2,0,1:T(8,128)} %copy.239), calls=%async_computation.10 | async-start | bytes 23068672 | tf_op jit(solution)/shard_map/all_to_all | solution.py:362
  2209.5 380.7 %reduce-scatter.9.cloned.1.call-start = ((), (), s32[]{:S(2)}) async-start(), calls=%async_computation.23 | async-start | bytes 10485760 | tf_op jit(solution)/shard_map/reduce_scatter | solution.py:290
  2222.3 411.8 %reduce-scatter.13.cloned.1.call-start = ((), (), s32[]{:S(2)}) async-start(), calls=%async_computation.27 | async-start | bytes 10485760 | tf_op jit(solution)/shard_map/reduce_scatter | solution.py:171
  2549.6 138.2 %reduce-scatter.23.cloned.1.call-start = ((), (), s32[]{:S(2)}) async-start(), calls=%async_computation.32 | async-start | bytes 4718592 | tf_op jit(solution)/shard_map/reduce_scatter | solution.py:399
  2562.3 176.7 %reduce-scatter.21.cloned.1.call-start = ((), (), s32[]{:S(2)}) async-start(), calls=%async_computation.31 | async-start | bytes 4718592 | tf_op jit(solution)/shard_map/reduce_scatter | solution.py:397
  2573.2 199.1 %reduce-scatter.19.cloned.1.call-start = ((), (), s32[]{:S(2)}) async-start(), calls=%async_computation.30 | async-start | bytes 1179648 | tf_op jit(solution)/shard_map/reduce_scatter | solution.py:394
  2578.0 227.8 %reduce-scatter.15.cloned.1.call-start = ((), (), s32[]{:S(2)}) async-start(), calls=%async_computation.28 | async-start | bytes 1179648 | tf_op jit(solution)/shard_map/reduce_scatter | solution.py:392
  2582.5 256.7 %reduce-scatter.17.cloned.1.call-start = ((), (), s32[]{:S(2)}) async-start(), calls=%async_computation.29 | async-start | bytes 1179648 | tf_op jit(solution)/shard_map/reduce_scatter | solution.py:393
  (48 other events, 1140.9 us)
Sparse Core Ops, SparseCore 0:
  9.8 55.2 all-gather.12
  917.1 34.3 all-gather.16
  1053.3 51.2 all-gather.14
  1109.3 52.5 all-gather.18
  1163.4 29.0 all-gather.20
  1194.0 30.3 all-gather.22
  1226.2 51.6 all-gather.24
  1302.6 86.3 reduce-scatter.10
  1411.2 52.4 all-gather.26
  2222.4 86.7 reduce-scatter.8
  2549.7 84.2 reduce-scatter.12
  2636.9 50.9 reduce-scatter.22
  2690.8 48.1 reduce-scatter.20
  2741.8 30.4 reduce-scatter.18
  2775.1 30.6 reduce-scatter.14
  2808.6 30.6 reduce-scatter.16
where the time goes:
time: 2860 us; the launch traced here: 2850 us
  waiting for transfers between devices  1180 us (41%)
  local copies, waits for them, and re-layouts  764 us (27%)
  blocking collectives  488 us (17%)
  other arithmetic  195 us (7%)
  matrix products  149 us (5%)
  starting transfers between devices  46.6 us (2%)
    all_gather x1, blocking collectives, shards(): lax.all_gather(out_weight, 'tok', axis=1, tiled=True)  260 us
    all_to_all x1, waiting for transfers between devices, shards(): lax.all_to_all(grad_shared_slots.reshape(slot_buckets, CAP, columns), 'to...  239 us
    all_to_all x1, waiting for transfers between devices, shards(): lax.all_to_all(grad_value_slots.reshape(slot_buckets, CAP, columns), 'tok...  181 us
    all_gather x1, blocking collectives, shards(): lax.all_gather(qk_weight, 'tok', axis=0, tiled=True)  136 us
    all_to_all x1, waiting for transfers between devices, shards(): lax.all_to_all(entry_slots(grad_mix_tok.reshape(entries, columns)), 'tok'...  125 us
    reduce_scatter x2, waiting for transfers between devices, grad_total(): lax.psum_scatter(summed, 'head', scatter_dimension=0, tiled=True)  121 us
    all_to_all x1, waiting for transfers between devices, send_buckets(): lax.all_to_all(token_slots(shared_tok), 'tok', split_axis=0, concat_axis=...  113 us
    all_gather x2, waiting for transfers between devices, grad_rows(): return lax.all_gather(shard_in, 'head', axis=1, tiled=True)  106 us
  transfers between devices with their start and end apart: 25, of which 17 were waited for; matrix products, arithmetic and copies ran while one was open for 24% of the time, Pallas kernels for 0%

commit v1 on v0

v1 whole, which is shorter than its diff:
```python
import jax
import jax.numpy as jnp
from jax import lax
from jax.experimental import pallas as pl
from jax.experimental.pallas import tpu as pltpu
from jax.sharding import PartitionSpec as P

DH = 128
CAP = 128
HALF = 64
GROUP = 128
ROWS = 256

SELF_SCORE = -10000.0
MASKED = -1000000000.0
NOTHING = -1e30
LOWEST = -3e38
PENALTY = 1048576.0
F32 = jnp.float32
BF16 = jnp.bfloat16
VMEM_BYTES = 60 * 1024 * 1024


def round_up(value, multiple):
    return -(-value // multiple) * multiple


def iota(shape, axis):
    return lax.broadcasted_iota(jnp.int32, shape, axis)


def dot_nt(left, right):
    return lax.dot_general(left, right, (((1,), (1,)), ((), ())), preferred_element_type=F32)


def dot_tn(left, right):
    return lax.dot_general(left, right, (((0,), (0,)), ((), ())), preferred_element_type=F32)


def dot_nn(left, right):
    return jnp.dot(left, right, preferred_element_type=F32)


def split_three(value):
    high = value.astype(BF16)
    rest = value - high.astype(F32)
    middle = rest.astype(BF16)
    return high, middle, (rest - middle.astype(F32)).astype(BF16)


def column_to_row(column):
    spread = jnp.broadcast_to(column, (GROUP, GROUP))
    same = iota((GROUP, GROUP), 0) == iota((GROUP, GROUP), 1)
    return jnp.sum(jnp.where(same, spread, 0.0), axis=0, keepdims=True)


def row_to_column(row):
    spread = jnp.broadcast_to(row, (GROUP, GROUP))
    same = iota((GROUP, GROUP), 0) == iota((GROUP, GROUP), 1)
    return jnp.sum(jnp.where(same, spread, 0.0), axis=1, keepdims=True)


class Plan:
    def __init__(self, blocks, tokens, most, buckets):
        self.blocks, self.tokens, self.most, self.buckets = blocks, tokens, most, buckets
        self.rows = round_up(buckets, 16)
        self.tiles = -(-buckets // HALF)
        self.pitch = self.tiles * HALF
        self.per_step = next(n for n in (16, 8, 4, 2, 1) if buckets % n == 0)
        self.steps = buckets // self.per_step
        self.deep = self.tiles * most * HALF
        self.together = next(n for n in (4, 2, 1) if most % n == 0)
        self.chunk = min(tokens, 512)


def ranks_by_bucket(plan, named_ref, base, block, boundary, rank_ref):
    wide = ROWS
    row = iota((plan.rows, 1), 0)
    ids = jnp.where(row < plan.buckets, (row + base).astype(F32), -100.0)
    earlier = jnp.where(iota((wide, wide), 0) < iota((wide, wide), 1), 1.0, 0.0).astype(BF16)
    count = jnp.zeros((plan.rows, 1), F32)
    below = jnp.zeros((plan.rows, 1), F32)
    for part in range(plan.tokens // wide):
        cols = slice(part * wide, (part + 1) * wide)
        member = ids == named_ref[0, 0:1, cols]
        for r in range(1, 4):
            member = member | (ids == named_ref[0, r : r + 1, cols])
        ones = jnp.where(member, 1.0, 0.0)
        before = dot_nn(ones.astype(BF16), earlier)
        rank_ref[:, cols] = jnp.where(member, before + count, -1.0)
        place = block * plan.tokens + part * wide + iota((1, wide), 1)
        below = below + jnp.sum(jnp.where(place < boundary, ones, 0.0), axis=1, keepdims=True)
        count = count + jnp.sum(ones, axis=1, keepdims=True)
    return count, below


def ranks_by_token(plan, named_ref, base, rank_ref):
    wide = ROWS
    lane = iota((1, GROUP), 1) % HALF
    later = jnp.where(iota((wide, wide), 1) < iota((wide, wide), 0), 1.0, 0.0).astype(BF16)
    names = jnp.transpose(named_ref[0])
    count = [jnp.zeros((1, GROUP), F32) for _ in range(plan.tiles)]
    for part in range(plan.tokens // wide):
        rows = slice(part * wide, (part + 1) * wide)
        named = [jnp.broadcast_to(names[rows, r : r + 1], (wide, GROUP)) for r in range(4)]
        for tile in range(plan.tiles):
            bucket = lane + tile * HALF
            ids = jnp.where(bucket < plan.buckets, (bucket + base).astype(F32), -100.0)
            member = ids == named[0]
            for r in range(1, 4):
                member = member | (ids == named[r])
            ones = jnp.where(member, 1.0, 0.0)
            before = dot_nn(later, ones.astype(BF16))
            rank_ref[rows, tile * GROUP : (tile + 1) * GROUP] = jnp.where(
                member, before + count[tile], -1.0
            )
            count[tile] = count[tile] + jnp.sum(ones, axis=0, keepdims=True)


def gather_rows(plan, rank_ref, table, block, left_ref, right_ref):
    def some(turn, _):
        ranks = rank_ref[...]
        picks = [
            jnp.where(ranks == (turn * plan.together + n).astype(F32), 1.0, 0.0).astype(BF16)
            for n in range(plan.together)
        ]
        found = dot_nn(jnp.concatenate(picks, axis=0), table)
        for n in range(plan.together):
            start = pl.multiple_of((block * plan.most + turn * plan.together + n) * plan.pitch, 8)
            part = found[n * plan.rows : (n + 1) * plan.rows]
            left_ref[pl.ds(start, plan.rows), :] = part[:, :DH]
            right_ref[pl.ds(start, plan.rows), :] = part[:, DH:]
        return 0

    lax.fori_loop(0, plan.most // plan.together, some, 0)


def clear_padding(plan, refs):
    extra = plan.pitch - plan.rows
    if extra == 0:
        return

    def one(slot, _):
        start = pl.multiple_of(slot * plan.pitch + plan.rows, 8)
        for ref in refs:
            ref[pl.ds(start, extra), :] = jnp.zeros((extra, DH), F32)
        return 0

    lax.fori_loop(0, CAP, one, 0)


def block_rows(plan, slot_ref, block, out_ref, cols):
    for tile in range(plan.tiles):
        for k in range(plan.most):
            start = pl.multiple_of((block * plan.most + k) * plan.pitch + tile * HALF, 8)
            to = (tile * plan.most + k) * HALF
            out_ref[to : to + HALF, cols] = slot_ref[pl.ds(start, HALF), :].astype(BF16)


def pair_values(j):
    return jnp.where(iota((1, GROUP), 1) < HALF, 2.0 * j, 2.0 * j + 1.0)


def forward_body(
    plan, scal, named_ref, shared_ref, value_ref, slot_shared, slot_value, out_ref,
    left_ref, right_ref, rank_ref, token_rank, code_ref, total_ref, lhs_ref, rhs_ref, lse_ref,
):
    step = pl.program_id(0)
    boundary, base = scal[0], scal[1]
    first_scatter = plan.blocks + plan.steps

    @pl.when(step == 0)
    def _():
        code_ref[...] = jnp.zeros_like(code_ref)
        clear_padding(plan, (left_ref, right_ref))

    @pl.when(step < plan.blocks)
    def _():
        block = scal[2 + jnp.minimum(step, plan.blocks - 1)]
        count, below = ranks_by_bucket(plan, named_ref, base, block, boundary, rank_ref)
        nth = iota((plan.rows, CAP), 1) - block * plan.most
        valid = (nth >= 0) & (nth < plan.most) & (nth.astype(F32) < count)
        code_ref[...] = jnp.where(
            valid, jnp.where(nth.astype(F32) < below, 1.0, 2.0), code_ref[...]
        )
        table = jnp.concatenate([shared_ref[0], value_ref[0]], axis=1)
        gather_rows(plan, rank_ref, table, block, left_ref, right_ref)

    @pl.when(step == plan.blocks)
    def _():
        code = code_ref[...]
        slot = iota((plan.rows, CAP), 1).astype(F32)
        change = jnp.min(jnp.where(code == 2.0, slot, 1.0 * CAP), axis=1, keepdims=True)
        code_ref[...] = jnp.where(
            code == 0.0, 0.0, jnp.where(code == 1.0, change, 1.0 * CAP)
        )

    @pl.when((step >= plan.blocks) & (step < first_scatter))
    def _():
        first = (step - plan.blocks) * plan.per_step
        row = iota((CAP, CAP), 0)
        col = iota((CAP, CAP), 1)
        batch = 2 if plan.per_step % 2 == 0 else 1

        def some(turn, _):
            at = [first + turn * batch + n for n in range(batch)]
            queries = [left_ref[pl.ds(b, CAP, stride=plan.pitch), :] for b in at]
            values = [right_ref[pl.ds(b, CAP, stride=plan.pitch), :] for b in at]
            limits = [code_ref[pl.ds(b, 1), :] for b in at]
            results = []
            for n in range(batch):
                query = queries[n]
                inverse = lax.rsqrt(jnp.sum(query * query, axis=1, keepdims=True) + 1e-06)
                query_low = query.astype(BF16)
                value_low = values[n].astype(BF16)
                key_low = (query * inverse).astype(BF16)
                scores = dot_nt(query_low, key_low)
                allowed = (row > col) & (row.astype(F32) < limits[n])
                scores = jnp.where(allowed, scores, jnp.where(row == col, SELF_SCORE, MASKED))
                highest = jnp.max(scores, axis=1, keepdims=True)
                raised = jnp.exp(scores - highest)
                summed = jnp.sum(raised, axis=1, keepdims=True)
                weight = (raised * (1.0 / summed)).astype(BF16)
                mixture = dot_nn(weight, value_low)
                results.append((query_low, value_low, mixture, highest + jnp.log(summed)))
            for n in range(batch):
                query_low, value_low, mixture, total = results[n]
                slot_shared[turn * batch + n] = query_low
                slot_value[turn * batch + n] = value_low
                right_ref[pl.ds(at[n], CAP, stride=plan.pitch), :] = mixture
                tile = at[n] // HALF
                mine = (col % HALF) == (at[n] - tile * HALF)
                total_ref[tile] = jnp.where(mine, total, total_ref[tile])
            return 0

        lax.fori_loop(0, plan.per_step // batch, some, 0)

    @pl.when(step >= first_scatter)
    def _():
        block = scal[2 + jnp.maximum(step - first_scatter, 0)]
        ranks_by_token(plan, named_ref, base, token_rank)
        block_rows(plan, right_ref, block, rhs_ref, slice(0, DH))
        pairs = plan.most // 2
        left_half = iota((1, GROUP), 1) < HALF

        def vector(tile, j):
            rows = [
                total_ref[tile, pl.ds(block * plan.most + 2 * j + n, 1), :] for n in range(2)
            ]
            return jnp.where(left_half, rows[0], rows[1])

        def chunk(part, _):
            start = part * plan.chunk
            for sub in range(plan.chunk // GROUP):
                rows = pl.ds(pl.multiple_of(start + sub * GROUP, GROUP), GROUP)
                here = slice(sub * GROUP, (sub + 1) * GROUP)
                totals = []
                for tile in range(plan.tiles):
                    ranks = token_rank[rows, tile * GROUP : (tile + 1) * GROUP]
                    found = jnp.full((GROUP, GROUP), LOWEST, F32)
                    for j in range(pairs):
                        found = jnp.where(ranks == pair_values(j), vector(tile, j), found)
                    totals.append(jnp.maximum(found, pltpu.roll(found, HALF, 1)))
                highest = totals[0]
                for tile in range(1, plan.tiles):
                    highest = jnp.maximum(highest, totals[tile])
                highest = jnp.max(highest, axis=1, keepdims=True)
                weights = [
                    jnp.where(one > 0.1 * LOWEST, jnp.exp(one - highest), 0.0) for one in totals
                ]
                summed = weights[0]
                for tile in range(1, plan.tiles):
                    summed = summed + weights[tile]
                summed = 0.5 * jnp.sum(summed, axis=1, keepdims=True)
                some_here = summed > 0.0
                scale = jnp.where(some_here, 1.0 / jnp.where(some_here, summed, 1.0), 0.0)
                lse = jnp.where(
                    some_here, highest + jnp.log(jnp.where(some_here, summed, 1.0)), NOTHING
                )
                lse_ref[pl.ds(part * (plan.chunk // GROUP) + sub, 1), :] = column_to_row(lse)
                for tile in range(plan.tiles):
                    ranks = token_rank[rows, tile * GROUP : (tile + 1) * GROUP]
                    weight = weights[tile] * scale
                    for j in range(pairs):
                        to = (tile * pairs + j) * GROUP
                        lhs_ref[here, to : to + GROUP] = jnp.where(
                            ranks == pair_values(j), weight, 0.0
                        ).astype(BF16)
            mixed = dot_nn(lhs_ref[...], rhs_ref[...])
            out_ref[0, pl.ds(pl.multiple_of(start, GROUP), plan.chunk), :] = mixed.astype(BF16)
            return 0

        lax.fori_loop(0, plan.tokens // plan.chunk, chunk, 0)
        extra = plan.tokens // GROUP
        for n, piece in enumerate(split_three(lse_ref[...])):
            out_ref[0, plan.tokens + n * extra : plan.tokens + (n + 1) * extra, :] = piece


def forward_call(plan, scal, named, shared, values):
    first_scatter = plan.blocks + plan.steps

    def named_at(i, scal):
        here = jnp.where(i < plan.blocks, i, jnp.maximum(i - first_scatter, 0))
        return (scal[2 + here], 0, 0)

    def table_at(i, scal):
        return (jnp.minimum(i, plan.blocks - 1), 0, 0)

    def slots_at(i, scal):
        return (jnp.clip(i - plan.blocks, 0, plan.steps - 1), 0, 0)

    def out_at(i, scal):
        return (jnp.maximum(i - first_scatter, 0), 0, 0)

    packed = plan.tokens + 3 * (plan.tokens // GROUP)
    slots = jax.ShapeDtypeStruct((plan.buckets, CAP, DH), BF16)
    return pl.pallas_call(
        lambda *refs: forward_body(plan, *refs),
        grid_spec=pltpu.PrefetchScalarGridSpec(
            num_scalar_prefetch=1,
            grid=(plan.blocks + plan.steps + plan.blocks,),
            in_specs=[
                pl.BlockSpec((1, 8, plan.tokens), named_at),
                pl.BlockSpec((1, plan.tokens, DH), table_at),
                pl.BlockSpec((1, plan.tokens, DH), table_at),
            ],
            out_specs=[
                pl.BlockSpec((plan.per_step, CAP, DH), slots_at),
                pl.BlockSpec((plan.per_step, CAP, DH), slots_at),
                pl.BlockSpec((1, packed, DH), out_at),
            ],
            scratch_shapes=[
                pltpu.VMEM((CAP * plan.pitch, DH), F32),
                pltpu.VMEM((CAP * plan.pitch, DH), F32),
                pltpu.VMEM((plan.rows, plan.tokens), F32),
                pltpu.VMEM((plan.tokens, plan.tiles * GROUP), F32),
                pltpu.VMEM((plan.rows, CAP), F32),
                pltpu.VMEM((plan.tiles, CAP, GROUP), F32),
                pltpu.VMEM((plan.chunk, plan.deep), BF16),
                pltpu.VMEM((plan.deep, DH), BF16),
                pltpu.VMEM((plan.tokens // GROUP, GROUP), F32),
            ],
        ),
        out_shape=[slots, slots, jax.ShapeDtypeStruct((plan.blocks, packed, DH), BF16)],
        compiler_params=pltpu.CompilerParams(vmem_limit_bytes=VMEM_BYTES),
        name="bucket_forward",
    )(scal, named, shared, values)


def merge_call(parts):
    count, packed, _ = parts[0].shape
    extra = packed // (GROUP + 3)
    tokens = extra * GROUP

    def body(*refs):
        ins, out_ref = refs[:-1], refs[-1]
        lses = []
        for ref in ins:
            pieces = [
                ref[0, tokens + n * extra : tokens + (n + 1) * extra, :].astype(F32)
                for n in range(3)
            ]
            lses.append(pieces[0] + pieces[1] + pieces[2])
        highest = lses[0]
        for lse in lses[1:]:
            highest = jnp.maximum(highest, lse)
        raised = [jnp.exp(lse - highest) for lse in lses]
        summed = raised[0]
        for one in raised[1:]:
            summed = summed + one
        shares = [one / summed for one in raised]
        for n, piece in enumerate(split_three(highest + jnp.log(summed))):
            out_ref[0, tokens + n * extra : tokens + (n + 1) * extra, :] = piece
        for g in range(extra):
            rows = slice(g * GROUP, (g + 1) * GROUP)
            total = jnp.zeros((GROUP, DH), F32)
            for ref, share in zip(ins, shares):
                total = total + row_to_column(share[g : g + 1, :]) * ref[0, rows, :].astype(F32)
            out_ref[0, rows, :] = total.astype(BF16)

    spec = pl.BlockSpec((1, packed, DH), lambda i: (i, 0, 0))
    return pl.pallas_call(
        body,
        grid=(count,),
        in_specs=[spec] * len(parts),
        out_specs=spec,
        out_shape=jax.ShapeDtypeStruct((count, packed, DH), BF16),
        compiler_params=pltpu.CompilerParams(vmem_limit_bytes=VMEM_BYTES),
        name="merge_rounds",
    )(*parts)


def pack_call(grads, mixed):
    count, tokens, _ = grads.shape
    packed = mixed.shape[1]
    extra = tokens // GROUP

    def body(grad_ref, mixed_ref, out_ref):
        out_ref[0, :tokens, :] = grad_ref[0]
        out_ref[0, tokens:packed, :] = mixed_ref[0, tokens:packed, :]
        rows = []
        for g in range(extra):
            here = slice(g * GROUP, (g + 1) * GROUP)
            product = grad_ref[0, here, :].astype(F32) * mixed_ref[0, here, :].astype(F32)
            rows.append(column_to_row(jnp.sum(product, axis=1, keepdims=True)))
        dots = jnp.concatenate(rows, axis=0)
        high = dots.astype(BF16)
        out_ref[0, packed : packed + extra, :] = high
        out_ref[0, packed + extra : packed + 2 * extra, :] = (dots - high.astype(F32)).astype(BF16)

    full = packed + 2 * extra
    return pl.pallas_call(
        body,
        grid=(count,),
        in_specs=[
            pl.BlockSpec((1, tokens, DH), lambda i: (i, 0, 0)),
            pl.BlockSpec((1, packed, DH), lambda i: (i, 0, 0)),
        ],
        out_specs=pl.BlockSpec((1, full, DH), lambda i: (i, 0, 0)),
        out_shape=jax.ShapeDtypeStruct((count, full, DH), BF16),
        compiler_params=pltpu.CompilerParams(vmem_limit_bytes=VMEM_BYTES),
        name="pack_gradient",
    )(grads, mixed)


def backward_body(
    plan, scal, named_ref, grad_ref, slot_shared, slot_value, shared_out, value_out,
    left_ref, right_ref, rank_ref, token_rank, extra_ref, lhs_ref, rhs_ref,
):
    step = pl.program_id(0)
    boundary, base = scal[0], scal[1]
    first_scatter = plan.blocks + plan.steps
    lane = iota((1, GROUP), 1)

    @pl.when(step == 0)
    def _():
        clear_padding(plan, (left_ref, right_ref))

    @pl.when(step < plan.blocks)
    def _():
        block = scal[2 + jnp.minimum(step, plan.blocks - 1)]
        ranks_by_bucket(plan, named_ref, base, block, boundary, rank_ref)
        groups = plan.tokens // GROUP
        pieces = [
            grad_ref[0, plan.tokens + n * groups : plan.tokens + (n + 1) * groups, :].astype(F32)
            for n in range(5)
        ]
        spread = jnp.where(iota((8, GROUP), 0) == iota((8, GROUP), 1), 1.0, 0.0)
        for g in range(groups):
            place = block * plan.tokens + g * GROUP + lane
            rows = [piece[g : g + 1, :] for piece in pieces]
            rows.append(jnp.where(place < boundary, 1.0, 0.0))
            rows.append(jnp.zeros((2, GROUP), F32))
            columns = jnp.transpose(jnp.concatenate(rows, axis=0))
            extra_ref[g * GROUP : (g + 1) * GROUP, :] = dot_nn(
                columns.astype(BF16), spread.astype(BF16)
            ).astype(BF16)
        table = jnp.concatenate([grad_ref[0, : plan.tokens, :], extra_ref[...]], axis=1)
        gather_rows(plan, rank_ref, table, block, left_ref, right_ref)

    @pl.when((step >= plan.blocks) & (step < first_scatter))
    def _():
        first = (step - plan.blocks) * plan.per_step
        key_slot = iota((CAP, CAP), 0)
        query_slot = iota((CAP, CAP), 1)
        earlier = key_slot < query_slot
        itself = key_slot == query_slot
        query_scale = jnp.where(lane == 5, PENALTY, 1.0)
        query_shift = jnp.where(lane == 5, -PENALTY, 0.0)
        key_scale = jnp.where(lane == 5, 1.0, 0.0)
        key_shift = jnp.where(lane < 3, -1.0, 0.0)
        value_extra = jnp.broadcast_to(
            jnp.where((lane == 3) | (lane == 4), -1.0, 0.0), (CAP, GROUP)
        ).astype(BF16)
        minus_total = jnp.broadcast_to(key_shift, (16, GROUP)).astype(BF16)
        batch = 2 if plan.per_step % 2 == 0 else 1

        def some(turn, _):
            at = [first + turn * batch + n for n in range(batch)]
            grads = [left_ref[pl.ds(b, CAP, stride=plan.pitch), :] for b in at]
            extras = [right_ref[pl.ds(b, CAP, stride=plan.pitch), :] for b in at]
            results = []
            for n in range(batch):
                query = slot_shared[turn * batch + n]
                value = slot_value[turn * batch + n]
                grad, extra = grads[n].astype(BF16), extras[n]
                wide = query.astype(F32)
                inverse = lax.rsqrt(jnp.sum(wide * wide, axis=1, keepdims=True) + 1e-06)
                unit = wide * inverse
                key = unit.astype(BF16)
                extra_low = extra.astype(BF16)
                query_extra = (extra * query_scale + query_shift).astype(BF16)
                key_extra = (extra * key_scale + key_shift).astype(BF16)
                scores = dot_nt(
                    jnp.concatenate([key, key_extra], axis=1),
                    jnp.concatenate([query, query_extra], axis=1),
                )
                slope = dot_nt(
                    jnp.concatenate([value, value_extra], axis=1),
                    jnp.concatenate([grad, extra_low], axis=1),
                )
                own = dot_nt(minus_total, extra_low)[0:1, :] + SELF_SCORE
                scores = jnp.where(earlier, scores, jnp.where(itself, own, MASKED))
                share = jnp.exp(jnp.minimum(scores, 0.0))
                grad_value = dot_nn(share.astype(BF16), grad)
                grad_scores = jnp.where(earlier, share * slope, 0.0).astype(BF16)
                grad_key = dot_nn(grad_scores, query)
                grad_query = dot_tn(grad_scores, key)
                along = jnp.sum(unit * grad_key, axis=1, keepdims=True)
                results.append((grad_query + inverse * (grad_key - unit * along), grad_value))
            for n in range(batch):
                left_ref[pl.ds(at[n], CAP, stride=plan.pitch), :] = results[n][0]
                right_ref[pl.ds(at[n], CAP, stride=plan.pitch), :] = results[n][1]
            return 0

        lax.fori_loop(0, plan.per_step // batch, some, 0)

    @pl.when(step >= first_scatter)
    def _():
        block = scal[2 + jnp.maximum(step - first_scatter, 0)]
        ranks_by_token(plan, named_ref, base, token_rank)
        block_rows(plan, left_ref, block, rhs_ref, slice(0, DH))
        block_rows(plan, right_ref, block, rhs_ref, slice(DH, 2 * DH))
        pairs = plan.most // 2

        def chunk(part, _):
            start = pl.multiple_of(part * plan.chunk, GROUP)
            for sub in range(plan.chunk // GROUP):
                rows = pl.ds(pl.multiple_of(start + sub * GROUP, GROUP), GROUP)
                here = slice(sub * GROUP, (sub + 1) * GROUP)
                for tile in range(plan.tiles):
                    ranks = token_rank[rows, tile * GROUP : (tile + 1) * GROUP]
                    for j in range(pairs):
                        to = (tile * pairs + j) * GROUP
                        lhs_ref[here, to : to + GROUP] = jnp.where(
                            ranks == pair_values(j), 1.0, 0.0
                        ).astype(BF16)
            found = dot_nn(lhs_ref[...], rhs_ref[...])
            shared_out[0, pl.ds(start, plan.chunk), :] = found[:, :DH].astype(BF16)
            value_out[0, pl.ds(start, plan.chunk), :] = found[:, DH:].astype(BF16)
            return 0

        lax.fori_loop(0, plan.tokens // plan.chunk, chunk, 0)


def backward_call(plan, scal, named, grads, slot_shared, slot_value):
    first_scatter = plan.blocks + plan.steps

    def named_at(i, scal):
        here = jnp.where(i < plan.blocks, i, jnp.maximum(i - first_scatter, 0))
        return (scal[2 + here], 0, 0)

    def table_at(i, scal):
        return (jnp.minimum(i, plan.blocks - 1), 0, 0)

    def slots_at(i, scal):
        return (jnp.clip(i - plan.blocks, 0, plan.steps - 1), 0, 0)

    def out_at(i, scal):
        return (jnp.maximum(i - first_scatter, 0), 0, 0)

    out = jax.ShapeDtypeStruct((plan.blocks, plan.tokens, DH), BF16)
    return pl.pallas_call(
        lambda *refs: backward_body(plan, *refs),
        grid_spec=pltpu.PrefetchScalarGridSpec(
            num_scalar_prefetch=1,
            grid=(plan.blocks + plan.steps + plan.blocks,),
            in_specs=[
                pl.BlockSpec((1, 8, plan.tokens), named_at),
                pl.BlockSpec((1, grads.shape[1], DH), table_at),
                pl.BlockSpec((plan.per_step, CAP, DH), slots_at),
                pl.BlockSpec((plan.per_step, CAP, DH), slots_at),
            ],
            out_specs=[
                pl.BlockSpec((1, plan.tokens, DH), out_at),
                pl.BlockSpec((1, plan.tokens, DH), out_at),
            ],
            scratch_shapes=[
                pltpu.VMEM((CAP * plan.pitch, DH), F32),
                pltpu.VMEM((CAP * plan.pitch, DH), F32),
                pltpu.VMEM((plan.rows, plan.tokens), F32),
                pltpu.VMEM((plan.tokens, plan.tiles * GROUP), F32),
                pltpu.VMEM((plan.tokens, GROUP), BF16),
                pltpu.VMEM((plan.chunk, plan.deep), BF16),
                pltpu.VMEM((plan.deep, 2 * DH), BF16),
            ],
        ),
        out_shape=[out, out],
        compiler_params=pltpu.CompilerParams(vmem_limit_bytes=VMEM_BYTES),
        name="bucket_backward",
    )(scal, named, grads, slot_shared, slot_value)


def norm_parts(row_block):
    row_mean = jnp.mean(row_block, axis=1, keepdims=True)
    centred = row_block - row_mean
    row_scale = lax.rsqrt(jnp.mean(centred * centred, axis=1, keepdims=True) + 1e-05)
    return centred * row_scale, row_scale


def norm_back(grad_norm, unit, row_scale, gain):
    grad_unit = grad_norm * gain
    first = jnp.mean(grad_unit, axis=1, keepdims=True)
    second = jnp.mean(grad_unit * unit, axis=1, keepdims=True)
    back = row_scale * (grad_unit - first - unit * second)
    return back, jnp.sum(grad_norm * unit, axis=0), jnp.sum(grad_norm, axis=0)


def smooth_gate(value_in):
    return jax.nn.gelu(value_in, approximate=True)


def head_swap(array_in, bits):
    return lax.ppermute(array_in, "head", [(i, i ^ bits) for i in range(4)])


def gather_features(shard):
    if lax.axis_size("head") != 4:
        return lax.all_gather(shard, "head", axis=1, tiled=True)
    half = shard.shape[0] // 2
    one, two = head_swap(shard, 1), head_swap(shard, 2)
    far = jnp.concatenate([head_swap(two[:half], 1), head_swap(one[half:], 2)], axis=0)
    me = lax.axis_index("head")
    by_distance = jnp.stack([shard, one, two, far])
    return jnp.concatenate(
        [lax.dynamic_index_in_dim(by_distance, me ^ n, 0, False) for n in range(4)], axis=1
    )


def sum_features(partial):
    devices = lax.axis_size("head")
    rows, width = partial.shape
    if devices != 4:
        return lax.psum_scatter(partial, "head", scatter_dimension=1, tiled=True).astype(F32)
    own = width // 4
    me = lax.axis_index("head")

    def piece(block, bits):
        return lax.dynamic_slice_in_dim(block, (me ^ bits) * own, own, 1)

    half = rows // 2
    sums = []
    for block, first, second in ((partial[:half], 1, 2), (partial[half:], 2, 1)):
        sent = jnp.concatenate([piece(block, first), piece(block, 3)], axis=1)
        got = head_swap(sent, first).astype(F32)
        passed = (piece(block, second).astype(F32) + got[:, own:]).astype(BF16)
        kept = piece(block, 0).astype(F32) + got[:, :own]
        sums.append(kept + head_swap(passed, second).astype(F32))
    return jnp.concatenate(sums, axis=0)


class Tokens:
    def __init__(self, heads_here):
        self.devices = lax.axis_size("tok")
        self.me = lax.axis_index("tok")
        self.heads = heads_here
        self.paired = self.devices == 8 and heads_here == 2
        self.group = self.devices // heads_here
        self.head = self.me // self.group
        self.quarter = self.me % self.group
        if self.paired:
            z, core = self.me // 2, self.me % 2
            chips = [z, 3 - z, z ^ 1, 3 - (z ^ 1)]
            self.order = jnp.stack(
                [c * 2 + core for c in chips] + [c * 2 + 1 - core for c in chips]
            )
        else:
            self.order = jnp.arange(self.devices)

    def swap(self, array_in, bits):
        return lax.ppermute(array_in, "tok", [(i, i ^ bits) for i in range(8)])

    def mirror(self, array_in):
        return lax.ppermute(array_in, "tok", [(i, 6 - 2 * (i // 2) + i % 2) for i in range(8)])

    def own_first(self, by_head):
        return jnp.where(self.head == 0, by_head, by_head[::-1])

    def spread(self, by_head):
        if self.paired:
            both = self.own_first(by_head)
            pair = jnp.stack([both[0], self.mirror(both[1])])
            four = jnp.concatenate([pair, self.swap(pair, 2)])
            return jnp.concatenate([four, self.swap(four, 1)])
        everyone = lax.all_gather(by_head, "tok", axis=0)
        return lax.dynamic_index_in_dim(everyone, self.head, 1, False)

    def collect(self, by_block, merge):
        if self.paired:
            four = merge([by_block[:4], self.swap(by_block[4:], 1)])
            pair = merge([four[:2], self.swap(four[2:], 2)])
            return self.own_first(jnp.stack([pair[0], self.mirror(pair[1])]))
        shares = lax.all_to_all(by_block, "tok", split_axis=0, concat_axis=0, tiled=True)
        shares = shares.reshape((self.heads, self.group) + shares.shape[1:])
        return merge([shares[:, n] for n in range(self.group)])


def add_up(parts):
    total = parts[0].astype(F32)
    for part in parts[1:]:
        total = total + part.astype(F32)
    return total.astype(BF16)


def by_head(columns):
    rows, width = columns.shape
    return jnp.stack([columns[:, n * DH : (n + 1) * DH] for n in range(width // DH)])


def to_columns(heads):
    return jnp.concatenate([heads[n] for n in range(heads.shape[0])], axis=1)


def shards(
    stream_one,
    stream_two,
    buckets,
    lengths,
    gain_attn,
    bias_attn,
    qk_weight,
    value_weight,
    out_weight,
    gain_ffn,
    bias_ffn,
    in_weight,
    in_bias,
    down_weight,
    down_bias,
    cotangent_one,
    cotangent_two,
):
    tok_rows, shard_width = stream_one.shape
    head_devices = lax.axis_size("head")
    tok_devices = lax.axis_size("tok")
    me_head, me_tok = lax.axis_index("head"), lax.axis_index("tok")
    full_width = shard_width * head_devices
    hidden_width = in_bias.shape[0]
    tokens = Tokens(shard_width // DH)
    per_device = 88
    plan = Plan(
        tok_devices, tok_rows, CAP // tok_devices, per_device * tok_devices // tokens.group
    )
    own = me_head * shard_width

    whole_qk = lax.all_gather(qk_weight, "tok", axis=0, tiled=True)
    whole_value = lax.all_gather(value_weight, "tok", axis=0, tiled=True)
    whole_out = lax.all_gather(
        lax.all_gather(out_weight, "tok", axis=1, tiled=True), "head", axis=0, tiled=True
    )
    whole_in = lax.all_gather(in_weight, "tok", axis=0, tiled=True)
    whole_down = lax.all_gather(down_weight, "tok", axis=1, tiled=True)
    vectors = lax.all_gather(
        jnp.stack([gain_attn, bias_attn, gain_ffn, bias_ffn]), "head", axis=1, tiled=True
    ).astype(F32)
    gain_one, bias_one, gain_two, bias_two = [vectors[n : n + 1] for n in range(4)]

    names = jnp.concatenate(
        [buckets.T.astype(F32), jnp.full((8 - buckets.shape[1], tok_rows), -5.0, F32)]
    )
    named = lax.all_gather(names, "tok", axis=0)
    scalars = jnp.concatenate(
        [jnp.stack([lengths[0], tokens.quarter * plan.buckets]), tokens.order]
    ).astype(jnp.int32)
    ids = (me_tok * per_device + jnp.arange(per_device)).astype(F32)
    bucket_counts = jnp.sum(
        (named[:, : buckets.shape[1]].reshape(1, -1) == ids[:, None]).astype(jnp.int32), axis=1
    )

    rows_two = gather_features(stream_two)
    unit_one, scale_one = norm_parts(rows_two.astype(F32))
    normed = (unit_one * gain_one + bias_one).astype(BF16)
    shared_tok = dot_nn(normed, whole_qk).astype(BF16)
    value_tok = dot_nn(normed, whole_value).astype(BF16)
    shared_all = tokens.spread(by_head(shared_tok))
    value_all = tokens.spread(by_head(value_tok))
    slot_shared, slot_value, shares = forward_call(plan, scalars, named, shared_all, value_all)
    mixed = tokens.collect(shares, merge_call)
    attended = gather_features(to_columns(mixed[:, :tok_rows]))

    rows_stream = gather_features(stream_one)
    rows_one = (rows_stream.astype(F32) + dot_nn(attended, whole_out)).astype(BF16)
    result_one = lax.dynamic_slice_in_dim(rows_one, own, shard_width, 1)
    unit_two, scale_two = norm_parts(rows_one.astype(F32))
    normed_two = (unit_two * gain_two + bias_two).astype(BF16)
    pre_act = dot_nn(normed_two, whole_in) + in_bias.astype(F32)
    hidden, gate_back = jax.vjp(smooth_gate, pre_act)
    hidden_low = hidden.astype(BF16)
    result_two = (
        stream_two.astype(F32)
        + sum_features(dot_nn(hidden_low, whole_down).astype(BF16))
        + down_bias.astype(F32)
    ).astype(BF16)
    rows_grad = gather_features(cotangent_two)
    grad_hidden = dot_nt(rows_grad, whole_down)
    grad_pre = gate_back(grad_hidden)[0].astype(BF16)
    back_two, gain_two_part, bias_two_part = norm_back(
        dot_nt(grad_pre, whole_in), unit_two, scale_two, gain_two
    )
    mine = (jnp.arange(full_width) // shard_width == me_head)[None, :]
    carried = (
        back_two + jnp.where(mine, jnp.tile(cotangent_one, (1, head_devices)).astype(F32), 0.0)
    ).astype(BF16)
    grad_attended = sum_features(dot_nt(carried, whole_out).astype(BF16)).astype(BF16)
    grad_one = sum_features(carried).astype(BF16)

    packed = pack_call(by_head(grad_attended), mixed)
    shared_part, value_part = backward_call(
        plan, scalars, named, tokens.spread(packed), slot_shared, slot_value
    )
    grad_shared = to_columns(tokens.collect(shared_part, add_up))
    grad_value = to_columns(tokens.collect(value_part, add_up))
    back_one, gain_one_part, bias_one_part = norm_back(
        dot_nt(grad_shared, whole_qk) + dot_nt(grad_value, whole_value),
        unit_one,
        scale_one,
        gain_one,
    )
    grad_two = (cotangent_two.astype(F32) + sum_features(back_one.astype(BF16))).astype(BF16)

    def over_tokens(part, axis):
        return lax.psum_scatter(
            part.astype(BF16), "tok", scatter_dimension=axis, tiled=True
        ).astype(F32)

    grad_down = over_tokens(dot_tn(hidden_low, rows_grad), 1)
    grad_in = over_tokens(dot_tn(normed_two, grad_pre), 0)
    out_part = dot_tn(attended, grad_one).astype(BF16)
    out_rows = lax.all_to_all(out_part, "head", split_axis=0, concat_axis=1, tiled=True)
    grad_out = over_tokens(out_rows, 1)
    grad_both = over_tokens(
        dot_tn(normed, jnp.concatenate([grad_shared, grad_value], axis=1)), 0
    )
    grad_qk, grad_v = grad_both[:, :shard_width], grad_both[:, shard_width:]

    def place(part):
        start = me_head * part.shape[0]
        whole = jnp.zeros((part.shape[0] * head_devices,), F32)
        return lax.dynamic_update_slice_in_dim(whole, part, start, 0)

    def share(whole):
        size = whole.shape[0] // (head_devices * tok_devices)
        return lax.dynamic_slice_in_dim(
            whole, (me_head * tok_devices + me_tok) * size, size, 0
        )

    early = lax.psum(
        jnp.concatenate(
            [
                gain_two_part,
                bias_two_part,
                place(jnp.sum(cotangent_two.astype(F32), axis=0)),
                place(jnp.sum(grad_pre.astype(F32), axis=0)),
            ]
        ),
        ("head", "tok"),
    )
    late = lax.psum(jnp.concatenate([gain_one_part, bias_one_part]), ("head", "tok"))
    return (
        result_one,
        result_two,
        grad_one,
        grad_two,
        share(late[:full_width]),
        share(late[full_width:]),
        grad_qk,
        grad_v,
        grad_out,
        share(early[:full_width]),
        share(early[full_width : 2 * full_width]),
        grad_in,
        share(early[3 * full_width :]),
        grad_down,
        share(early[2 * full_width : 3 * full_width]),
        bucket_counts,
    )


def solution(mesh):
    wide = P("tok", "head")
    placed = (
        wide, wide, P("tok", None), P(), P("head"), P("head"), wide, wide, P("head", "tok"),
        P("head"), P("head"), wide, P("head"), P("head", "tok"), P("head"), wide, wide,
    )
    vector = P(("head", "tok"))
    return jax.shard_map(
        shards,
        mesh=mesh,
        in_specs=placed,
        out_specs=(
            wide, wide, wide, wide, vector, vector, wide, wide, P("head", "tok"), vector, vector,
            wide, vector, P("head", "tok"), vector, P("tok"),
        ),
        check_vma=False,
    )
```

time: 2860 us -> 1250 us (0.44)
  waiting for transfers between devices: 1180 us -> 270 us
  local copies, waits for them, and re-layouts: 764 us -> 90.2 us
  Pallas kernels: 0 us -> 411 us
  blocking collectives: 488 us -> 160 us
  other arithmetic: 195 us -> 98.9 us
  starting transfers between devices: 46.6 us -> 115 us
  matrix products: 149 us -> 87.9 us
    all_to_all x9 -> x1, waiting for transfers between devices: 658 us -> 3.18 us  [shards(): lax.all_to_all(out_part, 'head', split_axis=0, concat_axis=1, tiled=True)]
    pallas_call x0 -> x5, Pallas kernels: none -> 411 us  [the longest x1 219 us: forward_call(): pl.pallas_call(lambda *refs: forward_body(plan, *refs), grid_spec=pltpu.P...]
    gather x9 -> x0, local copies, waits for them, and re-layouts: 358 us -> none  [the longest x2 89.8 us: token_slots(): padded[source_rows].reshape(bucket_total, slot_most, row_block.shape[1])]
    reduce_scatter x8 -> x2, waiting for transfers between devices: 284 us -> 0.01 us  [over_tokens(): lax.psum_scatter(part.astype(BF16), 'tok', scatter_dimension=axis, tiled=...]
    ppermute x0 -> x50, waiting for transfers between devices: none -> 266 us  [the longest x32 116 us: head_swap(): return lax.ppermute(array_in, 'head', [(i, i ^ bits) for i in range(4)])]
    all_gather x1, blocking collectives: 260 us -> 14.6 us  [shards(): lax.all_gather(out_weight, 'tok', axis=1, tiled=True)]
    all_gather x8 -> x3, waiting for transfers between devices: 239 us -> 0.02 us  [the longest x1 0.02 us: shards(): whole_in = lax.all_gather(in_weight, 'tok', axis=0, tiled=True)]
    ppermute x0 -> x50, starting transfers between devices: none -> 112 us  [the longest x12 63.7 us: swap(): return lax.ppermute(array_in, 'tok', [(i, i ^ bits) for i in range(8)])]
  transfers between devices with their start and end apart: 25 -> 58, of which waited for: 17 -> 21; matrix products, arithmetic and copies ran while one was open for 24% -> 16% of each run, Pallas kernels for 0% -> 15%
where the time goes in v1:
time: 1250 us
  Pallas kernels  411 us (33%)
  waiting for transfers between devices  270 us (22%)
  blocking collectives  160 us (13%)
  starting transfers between devices  115 us (9%)
  other arithmetic  98.9 us (8%)
  local copies, waits for them, and re-layouts  90.2 us (7%)
  matrix products  87.9 us (7%)
  between operations  16.3 us (1%)
    pallas_call x1, Pallas kernels, forward_call(): pl.pallas_call(lambda *refs: forward_body(plan, *refs), grid_spec=pltpu.P...  219 us
    pallas_call x1, Pallas kernels, backward_call(): pl.pallas_call(lambda *refs: backward_body(plan, *refs), grid_spec=pltpu....  180 us
    ppermute x32, waiting for transfers between devices, head_swap(): return lax.ppermute(array_in, 'head', [(i, i ^ bits) for i in range(4)])  116 us
    ppermute x12, waiting for transfers between devices, swap(): return lax.ppermute(array_in, 'tok', [(i, i ^ bits) for i in range(8)])  94.6 us
    ppermute x12, starting transfers between devices, swap(): return lax.ppermute(array_in, 'tok', [(i, i ^ bits) for i in range(8)])  63.7 us
    ppermute x6, waiting for transfers between devices, mirror(): lax.ppermute(array_in, 'tok', [(i, 6 - 2 * (i // 2) + i % 2) for i in ran...  55.2 us
    psum x1, blocking collectives, shards(): lax.psum(jnp.concatenate([gain_one_part, bias_one_part]), ('head', 'tok'))  50.7 us
    all_gather x1, blocking collectives, shards(): lax.all_gather(jnp.stack([gain_attn, bias_attn, gain_ffn, bias_ffn]), 'he...  45.7 us
  transfers between devices with their start and end apart: 58, of which 21 were waited for; matrix products, arithmetic and copies ran while one was open for 16% of the time, Pallas kernels for 15%

profile of v1, /device:TPU:0, one launch (start us, length us, event | category | flops | bytes accessed | tf_op | source)
XLA Modules:
  0.0 1248.6 jit_solution(4038022169144798268)
XLA Ops:
  15.0 45.7 %all_gather.29 = bf16[4,1024]{1,0:T(4,128)(2,1)S(1)} all-gather(bf16[4,256]{1,0:T(4,128)(2,1)S(1)} %pad_maximum_fusion.41), channel_id=1, replica_groups=mesh['head'=4,'tok'=8] {'head'}, dimensions={1}, use_global_device_ids=true | all-gather | bytes 10240 | tf_op jit(solution)/shard_map/all_gather | solution.py:753
  65.5 16.6 %all_gather.30 = bf16[1024,256]{1,0:T(8,128)(2,1)} all-gather(bf16[128,256]{1,0:T(8,128)(2,1)} %param.23), channel_id=1, replica_groups=mesh['head'=4,'tok'=8] {'tok'}, dimensions={0}, use_global_device_ids=true | all-gather | bytes 589824 | tf_op jit(solution)/shard_map/all_gather | solution.py:746
  82.1 16.0 %all_gather.31 = bf16[1024,256]{1,0:T(8,128)(2,1)} all-gather(bf16[128,256]{1,0:T(8,128)(2,1)} %param.24), channel_id=1, replica_groups=mesh['head'=4,'tok'=8] {'tok'}, dimensions={0}, use_global_device_ids=true | all-gather | bytes 589824 | tf_op jit(solution)/shard_map/all_gather | solution.py:747
  102.4 9.9 collective-permute-done.7
  125.1 9.1 fusion.22
  142.5 12.8 %collective-permute-done.8 = bf16[2048,128]{1,0:T(8,128)(2,1)S(1)} collective-permute-done((bf16[2048,128]{1,0:T(8,128)(2,1)S(1)}, bf16[2048,128]{1,0:T(8,128)(2,1)S(1)}, u32[]{:S(2)}, u32[]{:S(2)}) %collective-permute-start.8) | collective-permute-done | bytes 524320 | tf_op jit(solution)/shard_map/ppermute | solution.py:674
  155.4 21.4 %collective-permute-start.9 = (bf16[2,2048,128]{2,1,0:T(8,128)(2,1)S(1)}, bf16[2,2048,128]{2,1,0:T(8,128)(2,1)S(1)}, u32[]{:S(2)}, u32[]{:S(2)}) collective-permute-start(bf16[2,2048,128]{2,1,0:T(8,128)(2,1)S(1)} %pad_maximum_fusion.16), channel_id=1, source_target_pairs={{0,2},{1,3},{2,0},{3,1},{4,6},{5,7},{6,4},{7,5},{8,10},{9,11},{10,... | collective-permute-start | bytes 3145736 | tf_op jit(solution)/shard_map/ppermute | solution.py:671
  176.9 10.0 collective-permute-start.12
  186.9 13.9 %collective-permute-done.9 = bf16[2,2048,128]{2,1,0:T(8,128)(2,1)S(1)} collective-permute-done((bf16[2,2048,128]{2,1,0:T(8,128)(2,1)S(1)}, bf16[2,2048,128]{2,1,0:T(8,128)(2,1)S(1)}, u32[]{:S(2)}, u32[]{:S(2)}) %collective-permute-start.9) | collective-permute-done | bytes 1048608 | tf_op jit(solution)/shard_map/ppermute | solution.py:671
  202.4 18.1 %collective-permute-done.12 = bf16[2,2048,128]{2,1,0:T(8,128)(2,1)S(1)} collective-permute-done((bf16[2,2048,128]{2,1,0:T(8,128)(2,1)S(1)}, bf16[2,2048,128]{2,1,0:T(8,128)(2,1)S(1)}, u32[]{:S(2)}, u32[]{:S(2)}) %collective-permute-start.12) | collective-permute-done | bytes 1048608 | tf_op jit(solution)/shard_map/ppermute | solution.py:671
  223.6 16.0 %all-gather = f32[64,2048]{1,0:T(8,128)} all-gather(f32[8,2048]{1,0:T(8,128)S(1)} %concatenate.114), channel_id=2, replica_groups=mesh['head'=4,'tok'=8] {'tok'}, dimensions={0}, use_global_device_ids=true | all-gather | bytes 589824 | tf_op jit(solution)/shard_map/all_gather | solution.py:761
  246.8 218.9 %bucket_forward.1 = (bf16[176,128,128]{2,1,0:T(8,128)(2,1)}, bf16[176,128,128]{2,1,0:T(8,128)(2,1)}, bf16[8,2096,128]{2,1,0:T(8,128)(2,1)}) custom-call(s32[10]{0:T(128)} %concatenate.113.refs_0_, f32[8,8,2048]{2,1,0:T(8,128)} %bitcast.156, bf16[8,2048,128]{2,1,0:T(8,128)(2,1)} %pad_maximum_fusion.4.refs_2_, bf16[8,2048,128]{2,1,0:T(8,128)(2,1)} %pad_maximum_fusion.5.refs_3_), custom_call_target="tpu_custom_call" | custom-call | tf_op jit(solution)/shard_map/bucket_forward/pallas_call | solution.py:317
  470.7 14.6 %all_gather.32 = bf16[256,1024]{1,0:T(8,128)(2,1)} all-gather(bf16[256,128]{1,0:T(8,128)(2,1)S(1)} %copy-done.73), channel_id=1, replica_groups=mesh['head'=4,'tok'=8] {'tok'}, dimensions={1}, use_global_device_ids=true | all-gather | bytes 589824 | tf_op jit(solution)/shard_map/all_gather | solution.py:749
  495.3 25.9 %collective-permute-done.15.refs_1_ = bf16[2,2096,128]{2,1,0:T(8,128)(2,1)S(1)} collective-permute-done((bf16[2,2096,128]{2,1,0:T(8,128)(2,1)S(1)}, bf16[2,2096,128]{2,1,0:T(8,128)(2,1)S(1)}, u32[]{:S(2)}, u32[]{:S(2)}) %collective-permute-start.15) | collective-permute-done | bytes 1073184 | tf_op jit(solution)/shard_map/ppermute | solution.py:671
  530.0 21.9 %collective-permute-done.16 = bf16[2096,128]{1,0:T(8,128)(2,1)S(1)} collective-permute-done((bf16[2096,128]{1,0:T(8,128)(2,1)S(1)}, bf16[2096,128]{1,0:T(8,128)(2,1)S(1)}, u32[]{:S(2)}, u32[]{:S(2)}) %collective-permute-start.16) | collective-permute-done | bytes 536608 | tf_op jit(solution)/shard_map/ppermute | solution.py:674
  570.0 20.8 %collective-permute-done.28 = bf16[1024,256]{1,0:T(8,128)(2,1)} collective-permute-done((bf16[1024,256]{1,0:T(8,128)(2,1)}, bf16[1024,256]{1,0:T(8,128)(2,1)}, u32[]{:S(2)}, u32[]{:S(2)}) %collective-permute-start.28) | collective-permute-done | bytes 524320 | tf_op jit(solution)/shard_map/ppermute | solution.py:614
  621.8 11.1 fusion.94
  632.9 14.4 %convert_reduce_fusion.3 = (f32[1024]{0:T(1024)S(1)}, bf16[2048,1024]{1,0:T(8,128)(2,1)}) fusion(f32[2048,1024]{1,0:T(8,128)} %fusion.94, f32[1024]{0:T(1024)S(1)} %convert_element_type.284, bf16[1024,1024]{1,0:T(8,128)(2,1)} %all-gather.9.cloned.1.call-done, bf16[2048,256]{1,0:T(8,128)(2,1)} %get-tuple-element.93, ...), kind=kOutput, calls=%fused_computation.44 | convolution fusion | flops 4359977984 | bytes 18882560 | tf_op jit(solution)/shard_map/dot_general | solution.py:33
  672.5 19.1 %collective-permute-done.35 = bf16[1024,512]{1,0:T(8,128)(2,1)S(1)} collective-permute-done((bf16[1024,512]{1,0:T(8,128)(2,1)S(1)}, bf16[1024,512]{1,0:T(8,128)(2,1)S(1)}, u32[]{:S(2)}, u32[]{:S(2)}) %collective-permute-start.35) | collective-permute-done | bytes 1048608 | tf_op jit(solution)/shard_map/ppermute | solution.py:614
  694.8 19.3 %collective-permute-done.31 = bf16[1024,512]{0,1:T(8,128)(2,1)S(1)} collective-permute-done((bf16[1024,512]{0,1:T(8,128)(2,1)S(1)}, bf16[1024,512]{0,1:T(8,128)(2,1)S(1)}, u32[]{:S(2)}, u32[]{:S(2)}) %collective-permute-start.31) | collective-permute-done | bytes 1048608 | tf_op jit(solution)/shard_map/ppermute | solution.py:614
  716.8 10.4 collective-permute-done.36
  748.9 16.3 %collective-permute-start.38 = (bf16[2,2128,128]{2,1,0:T(8,128)(2,1)}, bf16[2,2128,128]{2,1,0:T(8,128)(2,1)S(1)}, u32[]{:S(2)}, u32[]{:S(2)}) collective-permute-start(bf16[2,2128,128]{2,1,0:T(8,128)(2,1)} %pad_maximum_fusion.13), channel_id=1, source_target_pairs={{0,2},{1,3},{2,0},{3,1},{4,6},{5,7},{6,4},{7,5},{8,10},{9,11},{10,... | collective-permute-start | bytes 3268616 | tf_op jit(solution)/shard_map/ppermute | solution.py:671
  783.2 10.6 convolution_convert_fusion.4
  814.4 179.7 %bucket_backward.1 = (bf16[8,2048,128]{2,1,0:T(8,128)(2,1)}, bf16[8,2048,128]{2,1,0:T(8,128)(2,1)}) custom-call(s32[10]{0:T(128)} %concatenate.113.refs_0_, f32[8,8,2048]{2,1,0:T(8,128)} %bitcast.157, bf16[8,2128,128]{2,1,0:T(8,128)(2,1)} %pad_maximum_fusion.refs_2_, bf16[176,128,128]{2,1,0:T(8,128)(2,1)} %get-tuple-element.22.refs_3_, ...), custom_call_target="tpu_custom_call" | custom-call | tf_op jit(solution)/shard_map/bucket_backward/pallas_call | solution.py:563
  1014.0 12.4 collective-permute-done.23
  1055.6 17.2 %collective-permute-done.44 = bf16[2,2048,128]{2,1,0:T(8,128)(2,1)S(1)} collective-permute-done((bf16[2,2048,128]{2,1,0:T(8,128)(2,1)S(1)}, bf16[2,2048,128]{2,1,0:T(8,128)(2,1)S(1)}, u32[]{:S(2)}, u32[]{:S(2)}) %collective-permute-start.44) | collective-permute-done | bytes 1048608 | tf_op jit(solution)/shard_map/ppermute | solution.py:671
  1075.0 19.5 %collective-permute-done.41 = bf16[2,2048,128]{2,1,0:T(8,128)(2,1)S(1)} collective-permute-done((bf16[2,2048,128]{2,1,0:T(8,128)(2,1)S(1)}, bf16[2,2048,128]{2,1,0:T(8,128)(2,1)S(1)}, u32[]{:S(2)}, u32[]{:S(2)}) %collective-permute-start.41) | collective-permute-done | bytes 1048608 | tf_op jit(solution)/shard_map/ppermute | solution.py:671
  1097.3 10.4 collective-permute-done.45
  1108.1 10.1 collective-permute-done.42
  1124.4 9.5 fusion.26
  1142.7 16.5 %collective-permute-done.48 = bf16[1024,512]{0,1:T(8,128)(2,1)} collective-permute-done((bf16[1024,512]{0,1:T(8,128)(2,1)S(1)}, bf16[1024,512]{0,1:T(8,128)(2,1)}, u32[]{:S(2)}, u32[]{:S(2)}) %collective-permute-start.48) | collective-permute-done | bytes 1048608 | tf_op jit(solution)/shard_map/ppermute | solution.py:614
  1184.1 50.7 %all-reduce.1 = (f32[2048]{0:T(1024)S(1)}, f32[7168]{0:T(1024)S(1)}) all-reduce(f32[2048]{0:T(1024)S(1)} %pad_maximum_fusion.40, f32[7168]{0:T(1024)S(1)} %pad_maximum_fusion.39), channel_id=1, replica_groups=mesh['head'=4,'tok'=8] {'head','tok'}, use_global_device_ids=true, to_apply=%region_10.11 | all-reduce | flops 9216 | bytes 73728 | tf_op jit(solution)/shard_map/psum | solution.py:858
  (463 shorter events, 313.5 us)
Async XLA Ops:
  7.2 603.2 %all-gather.5.cloned.1.call-start = ((), (), s32[]{:S(2)}) async-start(), calls=%async_computation.5 | async-start | bytes 2621440 | tf_op jit(solution)/shard_map/all_gather | solution.py:748
  7.2 53.5 %collective-permute-start.1 = (bf16[2048,256]{1,0:T(8,128)(2,1)}, bf16[2048,256]{1,0:T(8,128)(2,1)S(1)}, u32[]{:S(2)}, u32[]{:S(2)}) collective-permute-start(bf16[2048,256]{1,0:T(8,128)(2,1)} %param.17), channel_id=1, source_target_pairs={{0,16},{8,24},{16,0},{24,8},{1,17},{9,25},{17,1},{25,9},{2,18},{10... | collective-permute-start | bytes 3145736 | tf_op jit(solution)/shard_map/ppermute | solution.py:614
  10.3 51.8 %collective-permute-start = (bf16[2048,256]{1,0:T(8,128)(2,1)}, bf16[2048,256]{1,0:T(8,128)(2,1)S(1)}, u32[]{:S(2)}, u32[]{:S(2)}) collective-permute-start(bf16[2048,256]{1,0:T(8,128)(2,1)} %param.17), channel_id=1, source_target_pairs={{0,8},{8,0},{16,24},{24,16},{1,9},{9,1},{17,25},{25,17},{2,10},{10... | collective-permute-start | bytes 3145736 | tf_op jit(solution)/shard_map/ppermute | solution.py:614
  11.7 86.3 %collective-permute-start.4 = (bf16[2048,256]{1,0:T(8,128)(2,1)}, bf16[2048,256]{1,0:T(8,128)(2,1)S(1)}, u32[]{:S(2)}, u32[]{:S(2)}) collective-permute-start(bf16[2048,256]{1,0:T(8,128)(2,1)} %param.18), channel_id=1, source_target_pairs={{0,8},{8,0},{16,24},{24,16},{1,9},{9,1},{17,25},{25,17},{2,10},{10... | collective-permute-start | bytes 3145736 | tf_op jit(solution)/shard_map/ppermute | solution.py:614
  12.3 86.4 %collective-permute-start.5 = (bf16[2048,256]{1,0:T(8,128)(2,1)}, bf16[2048,256]{1,0:T(8,128)(2,1)S(1)}, u32[]{:S(2)}, u32[]{:S(2)}) collective-permute-start(bf16[2048,256]{1,0:T(8,128)(2,1)} %param.18), channel_id=1, source_target_pairs={{0,16},{8,24},{16,0},{24,8},{1,17},{9,25},{17,1},{25,9},{2,18},{10... | collective-permute-start | bytes 3145736 | tf_op jit(solution)/shard_map/ppermute | solution.py:614
  61.6 38.8 %collective-permute-start.2 = (bf16[1024,256]{1,0:T(8,128)(2,1)}, bf16[1024,256]{1,0:T(8,128)(2,1)}, u32[]{:S(2)}, u32[]{:S(2)}) collective-permute-start(bf16[1024,256]{1,0:T(8,128)(2,1)} %slice.331), channel_id=1, source_target_pairs={{0,8},{8,0},{16,24},{24,16},{1,9},{9,1},{17,25},{25,17},{2,10},{10... | collective-permute-start | bytes 1572872 | tf_op jit(solution)/shard_map/ppermute | solution.py:614
  63.9 36.4 %collective-permute-start.3 = (bf16[1024,256]{1,0:T(8,128)(2,1)}, bf16[1024,256]{1,0:T(8,128)(2,1)}, u32[]{:S(2)}, u32[]{:S(2)}) collective-permute-start(bf16[1024,256]{1,0:T(8,128)(2,1)} %slice.332), channel_id=1, source_target_pairs={{0,16},{8,24},{16,0},{24,8},{1,17},{9,25},{17,1},{25,9},{2,18},{10... | collective-permute-start | bytes 1572872 | tf_op jit(solution)/shard_map/ppermute | solution.py:614
  141.9 34.8 %collective-permute-start.11 = (bf16[2048,128]{1,0:T(8,128)(2,1)S(1)}, bf16[2048,128]{1,0:T(8,128)(2,1)S(1)}, u32[]{:S(2)}, u32[]{:S(2)}) collective-permute-start(bf16[2048,128]{1,0:T(8,128)(2,1)S(1)} %get-tuple-element.149), channel_id=1, source_target_pairs={{0,6},{1,7},{2,4},{3,5},{4,2},{5,3},{6,0},{7,1},{8,14},{9,15},{10,... | collective-permute-start | bytes 1572872 | tf_op jit(solution)/shard_map/ppermute | solution.py:674
  155.4 45.5 %collective-permute-start.9 = (bf16[2,2048,128]{2,1,0:T(8,128)(2,1)S(1)}, bf16[2,2048,128]{2,1,0:T(8,128)(2,1)S(1)}, u32[]{:S(2)}, u32[]{:S(2)}) collective-permute-start(bf16[2,2048,128]{2,1,0:T(8,128)(2,1)S(1)} %pad_maximum_fusion.16), channel_id=1, source_target_pairs={{0,2},{1,3},{2,0},{3,1},{4,6},{5,7},{6,4},{7,5},{8,10},{9,11},{10,... | collective-permute-start | bytes 3145736 | tf_op jit(solution)/shard_map/ppermute | solution.py:671
  176.9 43.6 %collective-permute-start.12 = (bf16[2,2048,128]{2,1,0:T(8,128)(2,1)S(1)}, bf16[2,2048,128]{2,1,0:T(8,128)(2,1)S(1)}, u32[]{:S(2)}, u32[]{:S(2)}) collective-permute-start(bf16[2,2048,128]{2,1,0:T(8,128)(2,1)S(1)} %pad_maximum_fusion.18), channel_id=1, source_target_pairs={{0,2},{1,3},{2,0},{3,1},{4,6},{5,7},{6,4},{7,5},{8,10},{9,11},{10,... | collective-permute-start | bytes 3145736 | tf_op jit(solution)/shard_map/ppermute | solution.py:671
  202.4 37.2 %collective-permute-start.10 = (bf16[4,2048,128]{2,1,0:T(8,128)(2,1)}, bf16[4,2048,128]{2,1,0:T(8,128)(2,1)}, u32[]{:S(2)}, u32[]{:S(2)}) collective-permute-start(bf16[4,2048,128]{2,1,0:T(8,128)(2,1)} %pad_maximum_fusion.11), channel_id=1, source_target_pairs={{0,1},{1,0},{2,3},{3,2},{4,5},{5,4},{6,7},{7,6},{8,9},{9,8},{10,11... | collective-permute-start | bytes 6291464 | tf_op jit(solution)/shard_map/ppermute | solution.py:671
  485.3 136.5 %all-gather.7.cloned.1.call-start = ((), (), s32[]{:S(2)}) async-start(), calls=%async_computation.6 | async-start | bytes 2359296 | tf_op jit(solution)/shard_map/all_gather | solution.py:751
  495.2 137.7 %all-gather.9.cloned.1.call-start = ((), (), s32[]{:S(2)}) async-start(), calls=%async_computation.7 | async-start | bytes 2359296 | tf_op jit(solution)/shard_map/all_gather | solution.py:752
  553.9 38.2 %collective-permute-start.17 = (bf16[2048,256]{1,0:T(8,128)(2,1)}, bf16[2048,256]{1,0:T(8,128)(2,1)}, u32[]{:S(2)}, u32[]{:S(2)}) collective-permute-start(bf16[2048,256]{1,0:T(8,128)(2,1)} %get-tuple-element.147), channel_id=1, source_target_pairs={{0,8},{8,0},{16,24},{24,16},{1,9},{9,1},{17,25},{25,17},{2,10},{10... | collective-permute-start | bytes 3145736 | tf_op jit(solution)/shard_map/ppermute | solution.py:614
  555.4 38.2 %collective-permute-start.18 = (bf16[2048,256]{1,0:T(8,128)(2,1)}, bf16[2048,256]{1,0:T(8,128)(2,1)}, u32[]{:S(2)}, u32[]{:S(2)}) collective-permute-start(bf16[2048,256]{1,0:T(8,128)(2,1)} %get-tuple-element.147), channel_id=1, source_target_pairs={{0,16},{8,24},{16,0},{24,8},{1,17},{9,25},{17,1},{25,9},{2,18},{10... | collective-permute-start | bytes 3145736 | tf_op jit(solution)/shard_map/ppermute | solution.py:614
  556.8 34.1 %collective-permute-start.28 = (bf16[1024,256]{1,0:T(8,128)(2,1)}, bf16[1024,256]{1,0:T(8,128)(2,1)}, u32[]{:S(2)}, u32[]{:S(2)}) collective-permute-start(bf16[1024,256]{1,0:T(8,128)(2,1)} %slice.362), channel_id=1, source_target_pairs={{0,16},{8,24},{16,0},{24,8},{1,17},{9,25},{17,1},{25,9},{2,18},{10... | collective-permute-start | bytes 1572872 | tf_op jit(solution)/shard_map/ppermute | solution.py:614
  559.5 31.4 %collective-permute-start.27 = (bf16[1024,256]{1,0:T(8,128)(2,1)}, bf16[1024,256]{1,0:T(8,128)(2,1)}, u32[]{:S(2)}, u32[]{:S(2)}) collective-permute-start(bf16[1024,256]{1,0:T(8,128)(2,1)} %slice.361), channel_id=1, source_target_pairs={{0,8},{8,0},{16,24},{24,16},{1,9},{9,1},{17,25},{25,17},{2,10},{10... | collective-permute-start | bytes 1572872 | tf_op jit(solution)/shard_map/ppermute | solution.py:614
  668.5 45.6 %collective-permute-start.31 = (bf16[1024,512]{0,1:T(8,128)(2,1)S(1)}, bf16[1024,512]{0,1:T(8,128)(2,1)S(1)}, u32[]{:S(2)}, u32[]{:S(2)}) collective-permute-start(bf16[1024,512]{0,1:T(8,128)(2,1)S(1)} %pad_maximum_fusion.23), channel_id=1, source_target_pairs={{0,16},{8,24},{16,0},{24,8},{1,17},{9,25},{17,1},{25,9},{2,18},{10... | collective-permute-start | bytes 3145736 | tf_op jit(solution)/shard_map/ppermute | solution.py:614
  671.2 71.2 %collective-permute-start.29 = (bf16[1024,512]{0,1:T(8,128)(2,1)}, bf16[1024,512]{0,1:T(8,128)(2,1)}, u32[]{:S(2)}, u32[]{:S(2)}) collective-permute-start(bf16[1024,512]{0,1:T(8,128)(2,1)} %pad_maximum_fusion.22), channel_id=1, source_target_pairs={{0,8},{8,0},{16,24},{24,16},{1,9},{9,1},{17,25},{25,17},{2,10},{10... | collective-permute-start | bytes 3145736 | tf_op jit(solution)/shard_map/ppermute | solution.py:614
  692.1 35.0 %collective-permute-start.36 = (bf16[1024,256]{1,0:T(8,128)(2,1)S(1)}, bf16[1024,256]{1,0:T(8,128)(2,1)S(1)}, u32[]{:S(2)}, u32[]{:S(2)}) collective-permute-start(bf16[1024,256]{1,0:T(8,128)(2,1)S(1)} %fusion.54), channel_id=1, source_target_pairs={{0,8},{8,0},{16,24},{24,16},{1,9},{9,1},{17,25},{25,17},{2,10},{10... | collective-permute-start | bytes 1572872 | tf_op jit(solution)/shard_map/ppermute | solution.py:614
  694.1 33.4 %collective-permute-start.34 = (bf16[1024,256]{1,0:T(8,128)(2,1)S(1)}, bf16[1024,256]{1,0:T(8,128)(2,1)S(1)}, u32[]{:S(2)}, u32[]{:S(2)}) collective-permute-start(bf16[1024,256]{1,0:T(8,128)(2,1)S(1)} %fusion.57), channel_id=1, source_target_pairs={{0,16},{8,24},{16,0},{24,8},{1,17},{9,25},{17,1},{25,9},{2,18},{10... | collective-permute-start | bytes 1572872 | tf_op jit(solution)/shard_map/ppermute | solution.py:614
  715.3 30.6 %collective-permute-start.32 = (bf16[1024,256]{0,1:T(8,128)(2,1)}, bf16[1024,256]{0,1:T(8,128)(2,1)}, u32[]{:S(2)}, u32[]{:S(2)}) collective-permute-start(bf16[1024,256]{0,1:T(8,128)(2,1)} %fusion.60), channel_id=1, source_target_pairs={{0,8},{8,0},{16,24},{24,16},{1,9},{9,1},{17,25},{25,17},{2,10},{10... | collective-permute-start | bytes 1572872 | tf_op jit(solution)/shard_map/ppermute | solution.py:614
  748.9 31.0 %collective-permute-start.38 = (bf16[2,2128,128]{2,1,0:T(8,128)(2,1)}, bf16[2,2128,128]{2,1,0:T(8,128)(2,1)S(1)}, u32[]{:S(2)}, u32[]{:S(2)}) collective-permute-start(bf16[2,2128,128]{2,1,0:T(8,128)(2,1)} %pad_maximum_fusion.13), channel_id=1, source_target_pairs={{0,2},{1,3},{2,0},{3,1},{4,6},{5,7},{6,4},{7,5},{8,10},{9,11},{10,... | collective-permute-start | bytes 3268616 | tf_op jit(solution)/shard_map/ppermute | solution.py:671
  772.2 402.8 %reduce-scatter.13.cloned.1.call-start = ((), (), s32[]{:S(2)}) async-start(), calls=%async_computation.10 | async-start | bytes 589824
  779.8 396.8 %reduce-scatter.15.cloned.1.call-start = ((), (), s32[]{:S(2)}) async-start(), calls=%async_computation.11 | async-start | bytes 2359296
  797.9 380.7 %reduce-scatter.11.cloned.1.call-start = ((), (), s32[]{:S(2)}) async-start(), calls=%async_computation.9 | async-start | bytes 2359296 | tf_op jit(solution)/shard_map/reduce_scatter | solution.py:822
  997.2 35.9 %collective-permute-start.43 = (bf16[4,2048,128]{2,1,0:T(8,128)(2,1)}, bf16[4,2048,128]{2,1,0:T(8,128)(2,1)}, u32[]{:S(2)}, u32[]{:S(2)}) collective-permute-start(bf16[4,2048,128]{2,1,0:T(8,128)(2,1)} %slice.309), channel_id=1, source_target_pairs={{0,1},{1,0},{2,3},{3,2},{4,5},{5,4},{6,7},{7,6},{8,9},{9,8},{10,11... | collective-permute-start | bytes 6291464 | tf_op jit(solution)/shard_map/ppermute | solution.py:671
  1005.1 39.4 %collective-permute-start.40 = (bf16[4,2048,128]{2,1,0:T(8,128)(2,1)}, bf16[4,2048,128]{2,1,0:T(8,128)(2,1)}, u32[]{:S(2)}, u32[]{:S(2)}) collective-permute-start(bf16[4,2048,128]{2,1,0:T(8,128)(2,1)} %slice.301), channel_id=1, source_target_pairs={{0,1},{1,0},{2,3},{3,2},{4,5},{5,4},{6,7},{7,6},{8,9},{9,8},{10,11... | collective-permute-start | bytes 6291464 | tf_op jit(solution)/shard_map/ppermute | solution.py:671
  1013.4 226.2 %reduce-scatter.9.cloned.1.call-start = ((), (), s32[]{:S(2)}) async-start(), calls=%async_computation.8 | async-start | bytes 1179648 | tf_op jit(solution)/shard_map/reduce_scatter | solution.py:822
  1035.3 37.5 %collective-permute-start.44 = (bf16[2,2048,128]{2,1,0:T(8,128)(2,1)S(1)}, bf16[2,2048,128]{2,1,0:T(8,128)(2,1)S(1)}, u32[]{:S(2)}, u32[]{:S(2)}) collective-permute-start(bf16[2,2048,128]{2,1,0:T(8,128)(2,1)S(1)} %slice.386), channel_id=1, source_target_pairs={{0,2},{1,3},{2,0},{3,1},{4,6},{5,7},{6,4},{7,5},{8,10},{9,11},{10,... | collective-permute-start | bytes 3145736 | tf_op jit(solution)/shard_map/ppermute | solution.py:671
  1046.7 47.8 %collective-permute-start.41 = (bf16[2,2048,128]{2,1,0:T(8,128)(2,1)S(1)}, bf16[2,2048,128]{2,1,0:T(8,128)(2,1)S(1)}, u32[]{:S(2)}, u32[]{:S(2)}) collective-permute-start(bf16[2,2048,128]{2,1,0:T(8,128)(2,1)S(1)} %slice.380), channel_id=1, source_target_pairs={{0,2},{1,3},{2,0},{3,1},{4,6},{5,7},{6,4},{7,5},{8,10},{9,11},{10,... | collective-permute-start | bytes 3145736 | tf_op jit(solution)/shard_map/ppermute | solution.py:671
  1073.2 34.5 %collective-permute-start.45 = (bf16[2048,128]{1,0:T(8,128)(2,1)S(1)}, bf16[2048,128]{1,0:T(8,128)(2,1)S(1)}, u32[]{:S(2)}, u32[]{:S(2)}) collective-permute-start(bf16[2048,128]{1,0:T(8,128)(2,1)S(1)} %get-tuple-element.139), channel_id=1, source_target_pairs={{0,6},{1,7},{2,4},{3,5},{4,2},{5,3},{6,0},{7,1},{8,14},{9,15},{10,... | collective-permute-start | bytes 1572872 | tf_op jit(solution)/shard_map/ppermute | solution.py:674
  (110 other events, 1400.5 us)
Sparse Core Ops, SparseCore 0:
  485.4 32.9 all-gather.4
  520.1 49.4 all-gather.6
  571.1 34.8 all-gather.8
  779.9 35.7 reduce-scatter.12
  818.0 33.9 reduce-scatter.14
  1013.5 44.4 reduce-scatter.10
  1142.8 41.4 reduce-scatter.8

commit v2 on v0

v2 whole, which is shorter than its diff:
```python
import jax
import jax.numpy as jnp
from jax import lax
from jax.experimental import pallas as pl
from jax.experimental.pallas import tpu as pltpu
from jax.sharding import PartitionSpec as P

DH = 128
CAP = 128
GROUP = 128
ROWS = 256
TILE = 16
HALVES = 2

SELF_SCORE = -10000.0
MASKED = -1000000000.0
NOTHING = -1e30
LOWEST = -3e38
PENALTY = 1048576.0
F32 = jnp.float32
BF16 = jnp.bfloat16
VMEM_BYTES = 60 * 1024 * 1024


def round_up(value, multiple):
    return -(-value // multiple) * multiple


def iota(shape, axis):
    return lax.broadcasted_iota(jnp.int32, shape, axis)


def dot_nt(left, right):
    return lax.dot_general(left, right, (((1,), (1,)), ((), ())), preferred_element_type=F32)


def dot_tn(left, right):
    return lax.dot_general(left, right, (((0,), (0,)), ((), ())), preferred_element_type=F32)


def dot_nn(left, right):
    return jnp.dot(left, right, preferred_element_type=F32)


def split_three(value):
    high = value.astype(BF16).astype(F32)
    rest = value - high
    middle = rest.astype(BF16).astype(F32)
    return [high, middle, rest - middle]


def column_to_row(column):
    spread = jnp.broadcast_to(column, (GROUP, GROUP))
    same = iota((GROUP, GROUP), 0) == iota((GROUP, GROUP), 1)
    return jnp.sum(jnp.where(same, spread, 0.0), axis=0, keepdims=True)


NO_COST = pl.CostEstimate(flops=0, bytes_accessed=0, transcendentals=0)


def params():
    return pltpu.CompilerParams(vmem_limit_bytes=VMEM_BYTES)


class Plan:
    def __init__(self, blocks, tokens, most, buckets):
        self.blocks, self.tokens, self.most, self.buckets = blocks, tokens, most, buckets
        self.rows = round_up(buckets, TILE)
        self.steps = self.rows // TILE
        self.slots = self.rows * most
        self.half = tokens // HALVES
        self.groups = self.half // GROUP
        self.lse_rows = round_up(3 * self.groups, 16)
        self.dot_rows = round_up(2 * self.groups, 16)
        self.packed = self.half + self.lse_rows
        self.full = self.packed + self.dot_rows


def slot_order(plan, scal, axis):
    slot = iota((CAP, CAP), axis)
    order = jnp.zeros((CAP, CAP), F32)
    for n in range(plan.blocks):
        first = scal[1 + n] * plan.most - n * plan.most
        order = jnp.where(slot // plan.most == n, (slot + first).astype(F32), order)
    return order


def rank_call(plan, scal, named):
    def body(scal, named_ref, rank_ref, since_ref, empty_ref, code_ref):
        step = pl.program_id(0)
        boundary, base = scal[plan.blocks + 1], scal[0]
        block = scal[1 + step]
        row = iota((plan.rows, 1), 0)
        ids = jnp.where(row < plan.buckets, (row + base).astype(F32), -100.0)
        earlier = jnp.where(iota((ROWS, ROWS), 0) < iota((ROWS, ROWS), 1), 1.0, 0.0).astype(BF16)
        count = jnp.zeros((plan.rows, 1), F32)
        below = jnp.zeros((plan.rows, 1), F32)
        for part in range(plan.tokens // ROWS):
            cols = slice(part * ROWS, (part + 1) * ROWS)
            member = ids == named_ref[0, 0:1, cols]
            for r in range(1, 4):
                member = member | (ids == named_ref[0, r : r + 1, cols])
            ones = jnp.where(member, 1.0, 0.0)
            before = dot_nn(ones.astype(BF16), earlier)
            rank_ref[0, :, cols] = jnp.where(member, before + count, -1.0).astype(BF16)
            place = block * plan.tokens + part * ROWS + iota((1, ROWS), 1)
            below = below + jnp.sum(jnp.where(place < boundary, ones, 0.0), axis=1, keepdims=True)
            count = count + jnp.sum(ones, axis=1, keepdims=True)

        @pl.when(step == 0)
        def _():
            code_ref[...] = jnp.zeros_like(code_ref)

        nth = iota((plan.rows, CAP), 1) - step * plan.most
        valid = (nth >= 0) & (nth < plan.most) & (nth.astype(F32) < count)
        code_ref[...] = jnp.where(
            valid, jnp.where(nth.astype(F32) < below, 1.0, 2.0), code_ref[...]
        )

        @pl.when(step == plan.blocks - 1)
        def _():
            code = code_ref[...]
            order = slot_order(plan, scal, 1)[0:1, :]
            change = jnp.min(jnp.where(code == 2.0, order, 1.0 * CAP), axis=1, keepdims=True)
            since_ref[...] = jnp.where(order >= change, change, 0.0)
            empty = jnp.where(code == 0.0, -PENALTY, 0.0)
            pad = round_up(plan.rows, GROUP) - plan.rows
            if pad:
                empty = jnp.concatenate([empty, jnp.zeros((pad, CAP), F32)], axis=0)
            for n in range(empty.shape[0] // GROUP):
                empty_ref[n] = jnp.transpose(empty[n * GROUP : (n + 1) * GROUP]).astype(BF16)

    sets = -(-plan.rows // GROUP)
    return pl.pallas_call(
        body,
        grid_spec=pltpu.PrefetchScalarGridSpec(
            num_scalar_prefetch=1,
            grid=(plan.blocks,),
            in_specs=[pl.BlockSpec((1, 8, plan.tokens), lambda i, scal: (i, 0, 0))],
            out_specs=[
                pl.BlockSpec((1, plan.rows, plan.tokens), lambda i, scal: (i, 0, 0)),
                pl.BlockSpec((plan.rows, CAP), lambda i, scal: (0, 0)),
                pl.BlockSpec((sets, CAP, GROUP), lambda i, scal: (0, 0, 0)),
            ],
            scratch_shapes=[pltpu.VMEM((plan.rows, CAP), F32)],
        ),
        out_shape=[
            jax.ShapeDtypeStruct((plan.blocks, plan.rows, plan.tokens), BF16),
            jax.ShapeDtypeStruct((plan.rows, CAP), F32),
            jax.ShapeDtypeStruct((sets, CAP, GROUP), BF16),
        ],
        compiler_params=params(),
        cost_estimate=NO_COST,
        name="bucket_ranks",
    )(scal, named)


def spread_rows(plan, rows):
    return jnp.concatenate(
        [
            jnp.broadcast_to(rows[n : n + 1], (plan.most, rows.shape[1]))
            for n in range(rows.shape[0])
        ],
        axis=0,
    )


def gather_rows(plan, rank_ref, table, more):
    number = (iota((plan.slots, ROWS), 0) % plan.most).astype(F32)
    picks = []
    for part in range(plan.half // ROWS):
        cols = slice(part * ROWS, (part + 1) * ROWS)
        ranks = spread_rows(plan, rank_ref[0, :, cols].astype(F32))
        picks.append(jnp.where(ranks == number, 1.0, 0.0).astype(BF16))
    found = dot_nn(jnp.concatenate(picks, axis=1), table)
    for ref in more:
        found = found + ref[0].astype(F32)
    return found.astype(BF16)


def rank_spec(plan, first, half):
    return pl.BlockSpec((1, plan.rows, plan.half), lambda i, *_: (i + first, 0, half))


def slot_spec(plan, width, first=0):
    return pl.BlockSpec((1, plan.slots, width), lambda i, *_: (i + first, 0, 0))


def gather_call(plan, ranks, rows, first, half, more):
    count = rows.shape[0]

    def body(rank_ref, rows_ref, *refs):
        refs[-1][0] = gather_rows(plan, rank_ref, rows_ref[0], refs[:-1])

    return pl.pallas_call(
        body,
        grid=(count,),
        in_specs=[
            rank_spec(plan, first, half),
            pl.BlockSpec((1, plan.half, 2 * DH), lambda i: (i, 0, 0)),
        ]
        + [slot_spec(plan, 2 * DH)] * len(more),
        out_specs=slot_spec(plan, 2 * DH),
        out_shape=jax.ShapeDtypeStruct((count, plan.slots, 2 * DH), BF16),
        compiler_params=params(),
        cost_estimate=NO_COST,
        name="gather_slots",
    )(ranks, rows, *more)


def gather_back_call(plan, scal, ranks, packed, first, half, more):
    count = packed.shape[0]

    def body(scal, rank_ref, ref, *refs):
        block = scal[1 + first + pl.program_id(0)]
        boundary = scal[plan.blocks + 1]
        lane = iota((1, GROUP), 1)
        spread = jnp.where(iota((8, GROUP), 0) == iota((8, GROUP), 1), 1.0, 0.0).astype(BF16)
        small = ref[0, plan.half : plan.full, :].astype(F32)
        extras = []
        for g in range(plan.groups):
            place = block * plan.tokens + half * plan.half + g * GROUP + lane
            rows = [small[n * plan.groups + g : n * plan.groups + g + 1, :] for n in range(3)]
            for n in range(2):
                at = plan.lse_rows + n * plan.groups + g
                rows.append(small[at : at + 1, :])
            rows.append(jnp.where(place < boundary, 1.0, 0.0))
            rows.append(jnp.zeros((2, GROUP), F32))
            extras.append(dot_tn(jnp.concatenate(rows, axis=0).astype(BF16), spread).astype(BF16))
        table = jnp.concatenate(
            [ref[0, : plan.half, :], jnp.concatenate(extras, axis=0)], axis=1
        )
        refs[-1][0] = gather_rows(plan, rank_ref, table, refs[:-1])

    return pl.pallas_call(
        body,
        grid_spec=pltpu.PrefetchScalarGridSpec(
            num_scalar_prefetch=1,
            grid=(count,),
            in_specs=[
                rank_spec(plan, first, half),
                pl.BlockSpec((1, plan.full, DH), lambda i, scal: (i, 0, 0)),
            ]
            + [slot_spec(plan, 2 * DH)] * len(more),
            out_specs=slot_spec(plan, 2 * DH),
        ),
        out_shape=jax.ShapeDtypeStruct((count, plan.slots, 2 * DH), BF16),
        compiler_params=params(),
        cost_estimate=NO_COST,
        name="gather_gradient",
    )(scal, ranks, packed, *more)


def table_of(plan, refs, bucket):
    rows = slice(bucket * plan.most, (bucket + 1) * plan.most)
    return jnp.concatenate([ref[n, rows, :] for ref in refs for n in range(ref.shape[0])], axis=0)


def tile_specs(plan, arrays):
    return [
        pl.BlockSpec((a.shape[0], TILE * plan.most, a.shape[2]), lambda i, scal: (0, i, 0))
        for a in arrays
    ]


def attention_call(plan, scal, slots, since, empty):
    count = len(slots)

    def body(scal, *refs):
        ins, since_ref, empty_ref = refs[:count], refs[count], refs[count + 1]
        out_ref, total_ref, key_order, query_order = refs[count + 2 :]
        step = pl.program_id(0)

        @pl.when(step == 0)
        def _():
            key_order[...] = slot_order(plan, scal, 0)
            query_order[...] = slot_order(plan, scal, 1)

        lane = iota((1, GROUP), 1)
        per = GROUP // TILE
        own = iota((CAP, CAP), 0) == iota((CAP, CAP), 1)
        for b in range(TILE):
            both = table_of(plan, ins, b)
            query, value = both[:, :DH], both[:, DH:]
            wide = query.astype(F32)
            inverse = lax.rsqrt(jnp.sum(wide * wide, axis=1, keepdims=True) + 1e-06)
            key = (wide * inverse).astype(BF16)
            mine = jnp.where(lane == lax.rem(step, per) * TILE + b, 1.0, 0.0)
            scores = dot_nt(
                jnp.concatenate([key, empty_ref[step // per]], axis=1),
                jnp.concatenate(
                    [query, jnp.broadcast_to(mine, (CAP, GROUP)).astype(BF16)], axis=1
                ),
            )
            allowed = (key_order[...] < query_order[...]) & (
                key_order[...] >= since_ref[b : b + 1, :]
            )
            scores = jnp.where(allowed, scores, jnp.where(own, SELF_SCORE, MASKED))
            highest = jnp.max(scores, axis=0, keepdims=True)
            raised = jnp.exp(scores - highest)
            summed = jnp.sum(raised, axis=0, keepdims=True)
            weight = (raised * (1.0 / summed)).astype(BF16)
            mixture = dot_tn(weight, value).astype(BF16)
            for n in range(plan.blocks):
                out_ref[n, b * plan.most : (b + 1) * plan.most, :] = mixture[
                    n * plan.most : (n + 1) * plan.most
                ]
            total_ref[b : b + 1, :] = highest + jnp.log(summed)

    return pl.pallas_call(
        body,
        grid_spec=pltpu.PrefetchScalarGridSpec(
            num_scalar_prefetch=1,
            grid=(plan.steps,),
            in_specs=tile_specs(plan, slots)
            + [
                pl.BlockSpec((TILE, CAP), lambda i, scal: (i, 0)),
                pl.BlockSpec(empty.shape, lambda i, scal: (0, 0, 0)),
            ],
            out_specs=[
                pl.BlockSpec((plan.blocks, TILE * plan.most, DH), lambda i, scal: (0, i, 0)),
                pl.BlockSpec((TILE, CAP), lambda i, scal: (i, 0)),
            ],
            scratch_shapes=[pltpu.VMEM((CAP, CAP), F32), pltpu.VMEM((CAP, CAP), F32)],
        ),
        out_shape=[
            jax.ShapeDtypeStruct((plan.blocks, plan.slots, DH), BF16),
            jax.ShapeDtypeStruct((plan.rows, CAP), F32),
        ],
        compiler_params=params(),
        cost_estimate=NO_COST,
        name="bucket_attention",
    )(scal, *slots, since, empty)


def attention_back_call(plan, scal, slots, grads):
    count = len(slots)

    def body(scal, *refs):
        ins, grad_ins = refs[:count], refs[count : 2 * count]
        out_ref, key_order, query_order = refs[2 * count :]

        @pl.when(pl.program_id(0) == 0)
        def _():
            key_order[...] = slot_order(plan, scal, 0)
            query_order[...] = slot_order(plan, scal, 1)

        lane = iota((1, GROUP), 1)
        itself = iota((CAP, CAP), 0) == iota((CAP, CAP), 1)
        query_scale = jnp.where(lane == 5, PENALTY, 1.0)
        query_shift = jnp.where(lane == 5, -PENALTY, 0.0)
        key_scale = jnp.where(lane == 5, 1.0, 0.0)
        key_shift = jnp.where(lane < 3, -1.0, 0.0)
        value_extra = jnp.broadcast_to(
            jnp.where((lane == 3) | (lane == 4), -1.0, 0.0), (CAP, GROUP)
        ).astype(BF16)
        minus_total = jnp.broadcast_to(key_shift, (16, GROUP)).astype(BF16)
        for b in range(TILE):
            both, grad_extra = table_of(plan, ins, b), table_of(plan, grad_ins, b)
            query, value = both[:, :DH], both[:, DH:]
            grad, extra = grad_extra[:, :DH], grad_extra[:, DH:]
            wide = query.astype(F32)
            inverse = lax.rsqrt(jnp.sum(wide * wide, axis=1, keepdims=True) + 1e-06)
            unit = wide * inverse
            key = unit.astype(BF16)
            extra_wide = extra.astype(F32)
            query_extra = (extra_wide * query_scale + query_shift).astype(BF16)
            key_extra = (extra_wide * key_scale + key_shift).astype(BF16)
            scores = dot_nt(
                jnp.concatenate([key, key_extra], axis=1),
                jnp.concatenate([query, query_extra], axis=1),
            )
            slope = dot_nt(jnp.concatenate([value, value_extra], axis=1), grad_extra)
            own = dot_nt(minus_total, extra)[0:1, :] + SELF_SCORE
            earlier = key_order[...] < query_order[...]
            scores = jnp.where(earlier, scores, jnp.where(itself, own, MASKED))
            share = jnp.exp(jnp.minimum(scores, 0.0))
            grad_value = dot_nn(share.astype(BF16), grad)
            grad_scores = jnp.where(earlier, share * slope, 0.0).astype(BF16)
            grad_key = dot_nn(grad_scores, query)
            grad_query = dot_tn(grad_scores, key)
            along = jnp.sum(unit * grad_key, axis=1, keepdims=True)
            grad_shared = (grad_query + inverse * (grad_key - unit * along)).astype(BF16)
            grad_value = grad_value.astype(BF16)
            for n in range(plan.blocks):
                to = slice(b * plan.most, (b + 1) * plan.most)
                rows = slice(n * plan.most, (n + 1) * plan.most)
                out_ref[n, to, :DH] = grad_shared[rows]
                out_ref[n, to, DH:] = grad_value[rows]

    return pl.pallas_call(
        body,
        grid_spec=pltpu.PrefetchScalarGridSpec(
            num_scalar_prefetch=1,
            grid=(plan.steps,),
            in_specs=tile_specs(plan, slots) + tile_specs(plan, grads),
            out_specs=pl.BlockSpec(
                (plan.blocks, TILE * plan.most, 2 * DH), lambda i, scal: (0, i, 0)
            ),
            scratch_shapes=[pltpu.VMEM((CAP, CAP), F32), pltpu.VMEM((CAP, CAP), F32)],
        ),
        out_shape=jax.ShapeDtypeStruct((plan.blocks, plan.slots, 2 * DH), BF16),
        compiler_params=params(),
        cost_estimate=NO_COST,
        name="bucket_attention_back",
    )(scal, *slots, *grads)


def columns_of(plan, slot_ref):
    return jnp.transpose(slot_ref[0].astype(F32)).astype(BF16)


def scatter_rows(plan, rank_ref, weight_ref, columns):
    number = (iota((TILE * plan.most, plan.half), 0) % plan.most).astype(F32)
    found = []
    for n in range(plan.steps):
        buckets = slice(n * TILE, (n + 1) * TILE)
        hit = spread_rows(plan, rank_ref[0, buckets, :].astype(F32)) == number
        weight = 1.0 if weight_ref is None else spread_rows(plan, weight_ref[buckets, :])
        found.append(jnp.where(hit, weight, 0.0).astype(BF16))
    return dot_nn(columns, jnp.concatenate(found, axis=0))


def scatter_call(plan, ranks, results, totals, first, count, half):
    def body(rank_ref, result_ref, total_ref, out_ref, found_ref, top_ref, lse_ref):
        first_slot = (first + pl.program_id(0)) * plan.most

        def totals_here(turn, tops):
            rows = pl.ds(pl.multiple_of(turn * 16, 16), 16)
            mine = total_ref[rows, :]
            new = []
            for g in range(plan.groups):
                cols = slice(g * GROUP, (g + 1) * GROUP)
                rank = rank_ref[0, rows, cols].astype(F32)
                at = jnp.maximum(rank, 0.0).astype(jnp.int32) + first_slot
                top = tops[g]
                for n in range(2):
                    part = slice(n * 8, (n + 1) * 8)
                    found = jnp.where(
                        rank[part] >= 0.0,
                        jnp.take_along_axis(mine[part], at[part], axis=1),
                        LOWEST,
                    )
                    found_ref[pl.ds(pl.multiple_of(turn * 16 + n * 8, 8), 8), cols] = found
                    top = jnp.maximum(top, found)
                new.append(top)
            return tuple(new)

        tops = lax.fori_loop(
            0,
            plan.rows // 16,
            totals_here,
            tuple(jnp.full((8, GROUP), LOWEST, F32) for _ in range(plan.groups)),
        )
        for g in range(plan.groups):
            top_ref[g] = tops[g]

        def weights(g, _):
            cols = pl.ds(pl.multiple_of(g * GROUP, GROUP), GROUP)
            top = jnp.max(top_ref[g], axis=0, keepdims=True)
            weight = jnp.exp(found_ref[:, cols] - jnp.where(top > 0.1 * LOWEST, top, 0.0))
            summed = jnp.sum(weight, axis=0, keepdims=True)
            some_here = summed > 0.0
            safe = jnp.where(some_here, summed, 1.0)
            found_ref[:, cols] = weight * (1.0 / safe)
            lse_ref[pl.ds(g, 1), :] = jnp.where(some_here, top + jnp.log(safe), NOTHING)
            return 0

        lax.fori_loop(0, plan.groups, weights, 0)
        found = scatter_rows(plan, rank_ref, found_ref, columns_of(plan, result_ref))
        out_ref[0, : plan.half, :] = jnp.transpose(found).astype(BF16)
        pieces = split_three(lse_ref[...])
        rest = plan.lse_rows - 3 * plan.groups
        if rest:
            pieces.append(jnp.zeros((rest, GROUP), F32))
        out_ref[0, plan.half :, :] = jnp.concatenate(pieces, axis=0).astype(BF16)

    return pl.pallas_call(
        body,
        grid=(count,),
        in_specs=[
            rank_spec(plan, first, half),
            slot_spec(plan, DH, first),
            pl.BlockSpec((plan.rows, CAP), lambda i: (0, 0)),
        ],
        out_specs=pl.BlockSpec((1, plan.packed, DH), lambda i: (i, 0, 0)),
        out_shape=jax.ShapeDtypeStruct((count, plan.packed, DH), BF16),
        scratch_shapes=[
            pltpu.VMEM((plan.rows, plan.half), F32),
            pltpu.VMEM((plan.groups, 8, GROUP), F32),
            pltpu.VMEM((plan.groups, GROUP), F32),
        ],
        compiler_params=params(),
        cost_estimate=NO_COST,
        name="scatter_results",
    )(ranks, results, totals)


def scatter_back_call(plan, ranks, grads, first, count, half):
    def body(rank_ref, grad_ref, out_ref):
        found = scatter_rows(plan, rank_ref, None, columns_of(plan, grad_ref))
        out_ref[0] = jnp.transpose(found).astype(BF16)

    return pl.pallas_call(
        body,
        grid=(count,),
        in_specs=[rank_spec(plan, first, half), slot_spec(plan, 2 * DH, first)],
        out_specs=pl.BlockSpec((1, plan.half, 2 * DH), lambda i: (i, 0, 0)),
        out_shape=jax.ShapeDtypeStruct((count, plan.half, 2 * DH), BF16),
        compiler_params=params(),
        cost_estimate=NO_COST,
        name="scatter_gradient",
    )(ranks, grads)


def merge_call(plan, parts):
    count = parts[0].shape[0]

    def body(*refs):
        ins, out_ref = refs[:-1], refs[-1]
        lses = []
        for ref in ins:
            small = ref[0, plan.half :, :].astype(F32)
            lses.append(
                sum(small[n * plan.groups : (n + 1) * plan.groups, :] for n in range(3))
            )
        highest = lses[0]
        for lse in lses[1:]:
            highest = jnp.maximum(highest, lse)
        raised = [jnp.exp(lse - highest) for lse in lses]
        summed = sum(raised)
        shares = [one / summed for one in raised]
        pieces = split_three(highest + jnp.log(summed))
        rest = plan.lse_rows - 3 * plan.groups
        if rest:
            pieces.append(jnp.zeros((rest, GROUP), F32))
        out_ref[0, plan.half :, :] = jnp.concatenate(pieces, axis=0).astype(BF16)
        low = [piece for share in shares for piece in split_three(share)[:2]]
        ones = [
            jnp.where(iota((8, GROUP), 0) // 2 == n, 1.0, 0.0).astype(BF16) for n in range(4)
        ]
        for g in range(plan.groups):
            rows = slice(g * GROUP, (g + 1) * GROUP)
            total = jnp.zeros((GROUP, DH), F32)
            for first in range(0, len(ins), 4):
                some = low[2 * first : 2 * first + 8]
                lines = [piece[g : g + 1, :] for piece in some]
                if len(lines) < 8:
                    lines.append(jnp.zeros((8 - len(lines), GROUP), F32))
                stack = jnp.concatenate(lines, axis=0).astype(BF16)
                for n, ref in enumerate(ins[first : first + 4]):
                    total = total + dot_tn(stack, ones[n]) * ref[0, rows, :].astype(F32)
            out_ref[0, rows, :] = total.astype(BF16)

    spec = pl.BlockSpec((1, plan.packed, DH), lambda i: (i, 0, 0))
    return pl.pallas_call(
        body,
        grid=(count,),
        in_specs=[spec] * len(parts),
        out_specs=spec,
        out_shape=jax.ShapeDtypeStruct((count, plan.packed, DH), BF16),
        compiler_params=params(),
        cost_estimate=NO_COST,
        name="merge_rounds",
    )(*parts)


def pack_call(plan, grads, mixed):
    heads = len(mixed)
    terms = [len(parts) for parts in grads]
    flat = [array for parts in grads for array in parts]

    def body(*refs):
        ins, mixed_refs, outs = refs[: len(flat)], refs[len(flat) : -heads], refs[-heads:]
        at = 0
        for n in range(heads):
            grad = ins[at][...].astype(F32)
            for ref in ins[at + 1 : at + terms[n]]:
                grad = grad + ref[...].astype(F32)
            at += terms[n]
            low = grad.astype(BF16)
            outs[n][: plan.half, :] = low
            outs[n][plan.half : plan.packed, :] = mixed_refs[n][plan.half :, :]
            wide = low.astype(F32)
            rows = []
            for g in range(plan.groups):
                here = slice(g * GROUP, (g + 1) * GROUP)
                product = wide[here] * mixed_refs[n][here, :].astype(F32)
                rows.append(column_to_row(jnp.sum(product, axis=1, keepdims=True)))
            dots = jnp.concatenate(rows, axis=0)
            high = dots.astype(BF16).astype(F32)
            pieces = [high, dots - high]
            rest = plan.dot_rows - 2 * plan.groups
            if rest:
                pieces.append(jnp.zeros((rest, GROUP), F32))
            outs[n][plan.packed :, :] = jnp.concatenate(pieces, axis=0).astype(BF16)

    return pl.pallas_call(
        body,
        out_shape=[jax.ShapeDtypeStruct((plan.full, DH), BF16)] * heads,
        compiler_params=params(),
        cost_estimate=NO_COST,
        name="pack_gradient",
    )(*flat, *mixed)


def unit_rows(wide):
    mean = jnp.mean(wide, axis=1, keepdims=True)
    centred = wide - mean
    scale = lax.rsqrt(jnp.mean(centred * centred, axis=1, keepdims=True) + 1e-05)
    return centred * scale, scale


def norm_back(grad_norm, unit, scale, gain):
    grad_unit = grad_norm * gain
    first = jnp.mean(grad_unit, axis=1, keepdims=True)
    second = jnp.mean(grad_unit * unit, axis=1, keepdims=True)
    return scale * (grad_unit - first - unit * second)


def row_spec(array, first=0):
    return pl.BlockSpec((ROWS, array.shape[1]), lambda i, *_: (i + first, 0))


def whole_spec(array):
    return pl.BlockSpec(array.shape, lambda i, *_: (0, 0))


def in_order(me, refs):
    if len(refs) == 1:
        return refs[0][...]
    parts = [ref[...] for ref in refs]
    columns = []
    for n in range(len(parts)):
        column = parts[n]
        for m in range(1, len(parts)):
            column = jnp.where(me == m, parts[n ^ m], column)
        columns.append(column)
    return jnp.concatenate(columns, axis=1)


def own_columns(me, array, width):
    mine = array[:, :width]
    for n in range(1, array.shape[1] // width):
        mine = jnp.where(me == n, array[:, n * width : (n + 1) * width], mine)
    return mine


def share_shapes(rows, width, devices):
    if devices != 4:
        return [jax.ShapeDtypeStruct((rows, width), BF16)]
    return [jax.ShapeDtypeStruct((rows, width // 2), BF16)] * 2


def put_share(me, early, refs, share):
    if len(refs) == 1:
        refs[0][...] = share.astype(BF16)
        return
    width = share.shape[1] // 4
    columns = [share[:, n * width : (n + 1) * width].astype(BF16) for n in range(4)]
    at = []
    for distance in range(4):
        column = columns[distance]
        for m in range(1, 4):
            column = jnp.where(me == m, columns[m ^ distance], column)
        at.append(column)
    sent, kept = refs
    sent[:, :width] = jnp.where(early, at[1], at[2])
    sent[:, width:] = at[3]
    kept[:, :width] = at[0]
    kept[:, width:] = jnp.where(early, at[2], at[1])


def norm_call(places, pieces, vectors, weight, heads):
    count = len(pieces)
    rows, width = pieces[0].shape[0], weight.shape[0]
    each = weight.shape[1] // heads

    def body(places, *refs):
        vectors_ref, weight_ref, rows_ref, normed_ref = refs[count : count + 4]
        outs = refs[count + 4 :]
        whole = in_order(places[0], refs[:count])
        rows_ref[...] = whole
        unit, _ = unit_rows(whole.astype(F32))
        normed = (unit * vectors_ref[0:1, :] + vectors_ref[1:2, :]).astype(BF16)
        normed_ref[...] = normed
        both = dot_nn(normed, weight_ref[...]).astype(BF16)
        parts = [both[:, n * each : (n + 1) * each] for n in range(heads)]
        if heads == 2:
            parts = [jnp.where(places[1] == n, parts[1], parts[0]) for n in (1, 0)]
        for out, part in zip(outs, parts):
            out[...] = part

    outs = [jax.ShapeDtypeStruct((rows, width), BF16)] * 2
    outs += [jax.ShapeDtypeStruct((rows, each), BF16)] * heads
    return pl.pallas_call(
        body,
        grid_spec=pltpu.PrefetchScalarGridSpec(
            num_scalar_prefetch=1,
            grid=(rows // ROWS,),
            in_specs=[row_spec(p) for p in pieces] + [whole_spec(vectors), whole_spec(weight)],
            out_specs=[row_spec(o) for o in outs],
        ),
        out_shape=outs,
        compiler_params=params(),
        cost_estimate=NO_COST,
        name="norm_project",
    )(places, *pieces, vectors, weight)


def norm_back_call(places, devices, rows, vectors, weight, grads):
    heads = len(grads)
    each = weight.shape[1] // heads

    def body(places, rows_ref, vectors_ref, weight_ref, *refs):
        outs, sums_ref = refs[heads:-1], refs[-1]
        unit, scale = unit_rows(rows_ref[...].astype(F32))
        parts = [ref[...] for ref in refs[:heads]]
        if heads == 2:
            parts = [jnp.where(places[1] == n, parts[1], parts[0]) for n in (1, 0)]
        grad = dot_nt(jnp.concatenate(parts, axis=1), weight_ref[...])
        back = norm_back(grad, unit, scale, vectors_ref[0:1, :])
        step = pl.program_id(0)
        early = pl.program_id(0) < pl.num_programs(0) // 2
        put_share(places[0], early, outs, back)

        @pl.when(step == 0)
        def _():
            sums_ref[...] = jnp.zeros_like(sums_ref)

        sums_ref[0:1, :] += jnp.sum(grad * unit, axis=0, keepdims=True)
        sums_ref[1:2, :] += jnp.sum(grad, axis=0, keepdims=True)

    outs = share_shapes(*rows.shape, devices)
    sums = jax.ShapeDtypeStruct((8, rows.shape[1]), F32)
    return pl.pallas_call(
        body,
        grid_spec=pltpu.PrefetchScalarGridSpec(
            num_scalar_prefetch=1,
            grid=(rows.shape[0] // ROWS,),
            in_specs=[row_spec(rows), whole_spec(vectors), whole_spec(weight)]
            + [row_spec(g) for g in grads],
            out_specs=[row_spec(o) for o in outs] + [whole_spec(sums)],
        ),
        out_shape=outs + [sums],
        compiler_params=params(),
        cost_estimate=NO_COST,
        name="norm_project_back",
    )(places, rows, vectors, weight, *grads)


CURVE = 0.7978845608028654
CUBIC = 0.044715


def feed_forward_call(
    places, devices, half, stream, pieces, grads, cotangent, vectors, in_bias, out_cols, in_weight,
    down_cols, before,
):
    own = cotangent.shape[1]
    count = len(pieces)
    rows, width = pieces[0].shape[0], stream.shape[1]
    deep = in_bias.shape[1]
    attended_width = out_cols.shape[1]
    widths = (attended_width, own, width, deep, deep, width, width)

    def body(places, *refs):
        piece_refs = refs[:count]
        stream_ref, grad_ref, cot_ref, vectors_ref, bias_ref, out_w, in_w, down_w = refs[
            count : count + 8
        ]
        (
            attended_ref, first_ref, normed_ref, hidden_ref, pre_ref, carried_ref, second_ref,
            sums_ref, hidden_sums,
        ) = refs[count + 8 + len(before) : count + 17 + len(before)]
        shares = refs[count + 17 + len(before) :]
        me = places[0]
        step = pl.program_id(0)
        attended = in_order(me, piece_refs)
        attended_ref[...] = attended
        result = (stream_ref[...].astype(F32) + dot_nt(attended, out_w[...])).astype(BF16)
        first_ref[...] = own_columns(me, result, own)
        unit, scale = unit_rows(result.astype(F32))
        normed = (unit * vectors_ref[2:3, :] + vectors_ref[3:4, :]).astype(BF16)
        normed_ref[...] = normed
        pre = dot_nn(normed, in_w[...]) + bias_ref[...]
        square = pre * pre
        bent = jnp.tanh(CURVE * (pre + CUBIC * square * pre))
        hidden = (0.5 * pre * (1.0 + bent)).astype(BF16)
        hidden_ref[...] = hidden
        slope = 0.5 * (1.0 + bent) + 0.5 * pre * (1.0 - bent * bent) * (
            CURVE * (1.0 + 3.0 * CUBIC * square)
        )
        grad_pre = (dot_nn(grad_ref[...], down_w[...]) * slope).astype(BF16)
        pre_ref[...] = grad_pre
        grad_norm = dot_nt(grad_pre, in_w[...])
        back = norm_back(grad_norm, unit, scale, vectors_ref[2:3, :])
        carried = jnp.concatenate(
            [
                back[:, n * own : (n + 1) * own]
                + jnp.where(me == n, cot_ref[...].astype(F32), 0.0)
                for n in range(width // own)
            ],
            axis=1,
        ).astype(BF16)
        carried_ref[...] = carried
        early = step < pl.num_programs(0) // 2
        put_share(me, early, shares, dot_nn(carried, out_w[...]))
        second_ref[...] = dot_nt(hidden, down_w[...]).astype(BF16)

        @pl.when(step == 0)
        def _():
            sums_ref[...] = jnp.zeros_like(sums_ref)
            hidden_sums[...] = jnp.zeros_like(hidden_sums)

        sums_ref[0:1, :] += jnp.sum(grad_norm * unit, axis=0, keepdims=True)
        sums_ref[1:2, :] += jnp.sum(grad_norm, axis=0, keepdims=True)
        hidden_sums[0:1, :] += jnp.sum(grad_pre.astype(F32), axis=0, keepdims=True)

    outs = [jax.ShapeDtypeStruct((stream.shape[0], w), BF16) for w in widths]
    sums = [jax.ShapeDtypeStruct((8, w), F32) for w in (width, deep)]
    shares = share_shapes(rows, attended_width, devices)
    first = half * (rows // ROWS)
    return pl.pallas_call(
        body,
        grid_spec=pltpu.PrefetchScalarGridSpec(
            num_scalar_prefetch=1,
            grid=(rows // ROWS,),
            in_specs=[row_spec(p) for p in pieces]
            + [row_spec(a, first) for a in (stream, grads, cotangent)]
            + [whole_spec(a) for a in (vectors, in_bias, out_cols)]
            + [pl.BlockSpec((width, deep), lambda i, *_: (0, 0))] * 2
            + [pl.BlockSpec(memory_space=pl.ANY)] * len(before),
            out_specs=[row_spec(o, first) for o in outs]
            + [whole_spec(o) for o in sums]
            + [row_spec(o) for o in shares],
        ),
        out_shape=outs + sums + shares,
        input_output_aliases={count + 9 + n: n for n in range(len(before))},
        compiler_params=params(),
        cost_estimate=NO_COST,
        name="feed_forward",
    )(
        places, *pieces, stream, grads, cotangent, vectors, in_bias, out_cols, in_weight, down_cols,
        *before,
    )


class Order:
    def __init__(self):
        self.last = None

    def tie(self, *arrays):
        if self.last is not None:
            arrays = lax.optimization_barrier((*arrays, self.last))[:-1]
        return arrays if len(arrays) > 1 else arrays[0]

    def mark(self, *arrays):
        self.last = arrays[0]
        return arrays if len(arrays) > 1 else arrays[0]


class Steps:
    def __init__(self, steps):
        self.steps = steps
        self.result = None

    def go(self, count=1):
        for _ in range(count):
            got = next(self.steps, None)
            self.result = self.result if got is None else got
        return self.result


def head_swap(array_in, bits):
    return lax.ppermute(array_in, "head", [(i, i ^ bits) for i in range(4)])


def gather_features(order, shard, direct=False):
    shard = order.tie(shard)
    if lax.axis_size("head") != 4:
        whole = [lax.all_gather(shard, "head", axis=1, tiled=True)]
        yield whole
        yield whole
        return
    one, two = head_swap(shard, 1), head_swap(shard, 2)
    if direct:
        far = head_swap(shard, 3)
        yield
        yield [shard, one, two, far]
        return
    yield
    half = round_up(shard.shape[0] // 2, 16)
    one, two = order.mark(*order.tie(one, two))
    far = jnp.concatenate([head_swap(two[:half], 1), head_swap(one[half:], 2)], axis=0)
    yield [shard, one, two, far]


def sum_terms(order, share):
    if len(share) == 1:
        share = order.tie(share[0])
        whole = [lax.psum_scatter(share, "head", scatter_dimension=1, tiled=True)]
        yield whole
        yield whole
        return
    sent, kept = order.tie(*share)
    half, own = sent.shape[0] // 2, sent.shape[1] // 2
    low, high = head_swap(sent[:half], 1), head_swap(sent[half:], 2)
    yield
    low, high = order.mark(*order.tie(low, high))
    passed = [
        (mine.astype(F32) + other.astype(F32)).astype(BF16)
        for mine, other in ((kept[:half, own:], low[:, own:]), (kept[half:, own:], high[:, own:]))
    ]
    last = jnp.concatenate([head_swap(passed[0], 2), head_swap(passed[1], 1)])
    yield [kept[:, :own], jnp.concatenate([low[:, :own], high[:, :own]]), last]


def add_terms(terms):
    return sum(term.astype(F32) for term in terms)


class Tokens:
    def __init__(self, heads_here):
        self.devices = lax.axis_size("tok")
        self.me = lax.axis_index("tok")
        self.heads = heads_here
        self.paired = self.devices == 8 and heads_here == 2
        self.group = self.devices // heads_here
        self.head = self.me // self.group
        self.quarter = self.me % self.group
        if self.paired:
            z, core = self.me // 2, self.me % 2
            chips = [z, 3 - z, z ^ 1, 3 - (z ^ 1)]
            self.order = jnp.stack(
                [c * 2 + core for c in chips] + [c * 2 + 1 - core for c in chips]
            )
            self.cuts = [(0, 4), (4, 4)]
            self.scatter_cuts = [(4, 4), (0, 4)]
        else:
            self.order = jnp.arange(self.devices)
            self.cuts = self.scatter_cuts = [(0, self.devices)]

    def swap(self, array_in, bits):
        return lax.ppermute(array_in, "tok", [(i, i ^ bits) for i in range(8)])

    def mirror(self, array_in):
        return lax.ppermute(array_in, "tok", [(i, 6 - 2 * (i // 2) + i % 2) for i in range(8)])

    def spread(self, order, by_head):
        by_head = order.tie(*by_head)
        if not self.paired:
            by_head = jnp.stack(by_head) if self.heads > 1 else by_head[None]
            everyone = lax.all_gather(by_head, "tok", axis=0)
            everyone = [lax.dynamic_index_in_dim(everyone, self.head, 1, False)]
            yield everyone
            yield everyone
            yield everyone
            return
        mine, other = by_head
        far, near = self.mirror(other), self.swap(mine, 2)
        yield
        last = self.swap(order.tie(far), 2)
        yield
        four = order.mark(jnp.stack(order.tie(mine, far, near, last)))
        yield [four, self.swap(four, 1)]

    def spread_same(self, array_in):
        if not self.paired:
            return lax.all_gather(array_in, "tok", axis=0)
        far = self.mirror(array_in)
        four = jnp.stack([array_in, far, self.swap(array_in, 2), self.swap(far, 2)])
        return jnp.concatenate([four, self.swap(four, 1)])

    def collect(self, order, merge):
        if not self.paired:
            blocks = order.tie((yield))
            shares = lax.all_to_all(blocks, "tok", split_axis=0, concat_axis=0, tiled=True)
            shares = shares.reshape((self.heads, self.group) + shares.shape[1:])
            yield
            merged = merge([shares[:, n] for n in range(self.group)])
            merged = [merged[n] for n in range(self.heads)]
            yield merged
            yield merged
            yield merged
            return
        got = self.swap(order.tie((yield)), 1)
        blocks = yield
        four = order.mark(merge(list(order.tie(blocks, got))))
        far = self.swap(four[3:], 2)
        yield
        far = order.mark(merge(list(order.tie(four[1:2], far))))
        far, near = self.mirror(far), self.swap(order.tie(four[2:3]), 2)
        yield
        own = order.mark(merge(list(order.tie(four[:1], near))))
        yield [own[0], far[0]]


def add_up(parts):
    total = parts[0].astype(F32)
    for part in parts[1:]:
        total = total + part.astype(F32)
    return total.astype(BF16)


def sum_everywhere(vector):
    if lax.axis_size("head") != 4 or lax.axis_size("tok") != 8:
        return lax.psum(vector, ("head", "tok"))
    for axis, count, bits in (
        ("tok", 8, 1), ("head", 4, 1), ("tok", 8, 2), ("head", 4, 2), ("tok", 8, 4),
    ):
        vector = vector + lax.ppermute(vector, axis, [(i, i ^ bits) for i in range(count)])
    return vector


def shards(
    stream_one,
    stream_two,
    buckets,
    lengths,
    gain_attn,
    bias_attn,
    qk_weight,
    value_weight,
    out_weight,
    gain_ffn,
    bias_ffn,
    in_weight,
    in_bias,
    down_weight,
    down_bias,
    cotangent_one,
    cotangent_two,
):
    tok_rows, shard_width = stream_one.shape
    head_devices = lax.axis_size("head")
    tok_devices = lax.axis_size("tok")
    me_head, me_tok = lax.axis_index("head"), lax.axis_index("tok")
    full_width = shard_width * head_devices
    hidden_width = in_bias.shape[0]
    heads = shard_width // DH
    tokens = Tokens(heads)
    per_device = 88
    plan = Plan(
        tok_devices, tok_rows, CAP // tok_devices, per_device * tok_devices // tokens.group
    )
    halves = [slice(h * plan.half, (h + 1) * plan.half) for h in range(HALVES)]

    order = Order()
    places = jnp.stack([me_head, tokens.head]).astype(jnp.int32)
    first_half, last_half = 0, HALVES - 1

    def head_columns(rows):
        if heads == 2:
            rows = [jnp.where(tokens.head == n, rows[1], rows[0]) for n in (1, 0)]
        return jnp.concatenate(rows, axis=1)

    vectors = jnp.stack([gain_attn, bias_attn, gain_ffn, bias_ffn])
    behind = jnp.concatenate([vectors, jnp.zeros((28, shard_width), BF16)])
    rows_in = [
        Steps(gather_features(order, jnp.concatenate([stream_two[halves[0]], behind]))),
        Steps(gather_features(order, stream_two[halves[1]])),
    ]
    rows_in[0].go()

    both_weights = jnp.concatenate(
        [
            weight[:, n * DH : (n + 1) * DH]
            for n in range(heads)
            for weight in (qk_weight, value_weight)
        ],
        axis=1,
    )
    whole_both = lax.all_gather(both_weights, "tok", axis=0, tiled=True)
    in_out = jnp.concatenate([in_weight, out_weight.T], axis=1)
    in_out = lax.all_gather(in_out, "tok", axis=0, tiled=True)

    names = jnp.concatenate(
        [buckets.T.astype(F32), jnp.full((8 - buckets.shape[1], tok_rows), -5.0, F32)]
    )
    named = tokens.spread_same(names)
    scalars = jnp.concatenate(
        [jnp.stack([tokens.quarter * plan.buckets]), tokens.order, lengths[:1]]
    ).astype(jnp.int32)
    ranks, since, empty = rank_call(plan, scalars, named)
    order.mark(since)
    rows_in[0].go()
    rows_in[1].go()
    ids = (me_tok * per_device + jnp.arange(per_device)).astype(F32)
    bucket_counts = order.mark(
        jnp.sum(
            (
                order.tie(named)[:, : buckets.shape[1]].reshape(1, -1) == ids[:, None]
            ).astype(jnp.int32),
            axis=1,
        )
    )

    pieces = [rows_in[0].result, None]
    by_distance = [piece[plan.half : plan.half + 8] for piece in pieces[0]]
    pieces[0] = [piece[: plan.half] for piece in pieces[0]]
    if len(by_distance) == 4:
        by_distance = jnp.stack(by_distance)
        by_distance = [
            lax.dynamic_index_in_dim(by_distance, me_head ^ n, 0, False) for n in range(4)
        ]
    vectors = jnp.concatenate(by_distance, axis=1).astype(F32)

    rows_two, normed, tables = [], [], []

    def project(h):
        one, *others = order.tie(*pieces[h]) if len(pieces[h]) > 1 else pieces[h]
        rows, normed_rows, *both = norm_call(
            places, [one, *others], vectors, whole_both, heads
        )
        rows_two.append(rows)
        normed.append(order.mark(normed_rows))
        tables.append(Steps(tokens.spread(order, both)))
        tables[h].go()

    slots = [[] for _ in tokens.cuts]

    def gather(h, n, found, call):
        found[n] = [order.mark(call(tokens.cuts[n][0], h, found[n]))]

    def gather_tables(first, h, more):
        n = [cut[0] for cut in tokens.cuts].index(first)
        return gather_call(plan, ranks, order.tie(tables[h].result[n]), first, h, more)

    rows_in[1].go()
    project(first_half)
    tables[0].go()
    pieces[1] = rows_in[1].result
    project(last_half)
    rows_stream = lax.all_gather(order.tie(stream_one), "head", axis=1, tiled=True)
    tables[0].go()
    gather(0, 0, slots, gather_tables)
    tables[1].go()
    if len(tokens.cuts) > 1:
        gather(0, 1, slots, gather_tables)
    tables[1].go()
    down_cols = lax.all_gather(order.tie(down_weight.T), "tok", axis=0, tiled=True)
    rows_grad = lax.all_gather(order.tie(cotangent_two), "head", axis=1, tiled=True)
    out_cols = lax.all_gather(
        order.tie(in_out[:, hidden_width:]), "head", axis=1, tiled=True
    )
    for n in range(len(tokens.cuts)):
        gather(1, n, slots, gather_tables)
    slots = [parts[0] for parts in slots]
    results, totals = attention_call(plan, scalars, slots, since, empty)
    order.mark(totals)

    def scatter(call, h, n):
        first, count = tokens.scatter_cuts[n]
        return order.mark(call(first, count, h))

    def scatter_forward(first, count, h):
        return scatter_call(plan, ranks, order.tie(results), totals, first, count, h)

    def collects(merge):
        made = []
        for _ in range(HALVES):
            steps = tokens.collect(order, merge)
            next(steps)
            made.append(steps)
        return made

    several = len(tokens.scatter_cuts) > 1
    mixing = collects(lambda parts: merge_call(plan, parts))
    part = scatter(scatter_forward, 0, 0)
    mixing[0].send(part)
    if several:
        part = scatter(scatter_forward, 0, 1)
        mixing[0].send(part)
    part = scatter(scatter_forward, 1, 0)
    mixing[1].send(part)
    next(mixing[0])
    if several:
        part = scatter(scatter_forward, 1, 1)
    mixed = [next(mixing[0])]

    def gather_attended(h):
        columns = head_columns([rows[: plan.half] for rows in mixed[h]])
        steps = Steps(gather_features(order, columns, h == last_half))
        steps.go()
        return steps

    attended_in = [gather_attended(0)]
    mixing[1].send(part if several else None)
    attended_in[0].go()
    next(mixing[1])
    mixed.append(next(mixing[1]))
    order.mark(*order.tie(*attended_in[0].result[::-1]))
    attended_in.append(gather_attended(1))
    attended_in[1].go()

    def feed_forward(h, before):
        pieces = attended_in[h].result
        pieces = list(order.tie(*pieces)) if len(pieces) > 1 else pieces
        kept = feed_forward_call(
            places,
            head_devices,
            h,
            rows_stream,
            pieces,
            rows_grad,
            cotangent_one,
            vectors,
            in_bias.astype(F32).reshape(1, -1),
            out_cols,
            in_out,
            down_cols,
            before,
        )
        order.mark(kept[7])
        return kept

    kept = feed_forward(0, [])
    sums, hidden_sums = kept[7:9]
    grad_sums = [Steps(sum_terms(order, kept[9:]))]
    grad_sums[0].go()
    kept = feed_forward(1, kept[:7])
    attended, result_one, normed_two, hidden, grad_pre, carried, second = kept[:7]
    sums, hidden_sums = sums + kept[7], hidden_sums + kept[8]
    grad_sums[0].go()
    grad_sums.append(Steps(sum_terms(order, kept[9:])))
    grad_sums[1].go()

    def pack(h):
        terms = grad_sums[h].result
        columns = [[t[:, n * DH : (n + 1) * DH] for t in terms] for n in range(heads)]
        if heads == 2:
            columns = [
                [jnp.where(tokens.head == n, b, a) for a, b in zip(*columns)] for n in (1, 0)
            ]
        columns[0][0] = order.tie(columns[0][0])
        packed = pack_call(plan, columns, mixed[h])
        order.mark(packed[0])
        steps = Steps(tokens.spread(order, packed))
        steps.go()
        return steps

    grad_slots = [[] for _ in tokens.cuts]

    def gather_grads(first, h, more):
        n = [cut[0] for cut in tokens.cuts].index(first)
        return gather_back_call(
            plan, scalars, ranks, order.tie(packed[h].result[n]), first, h, more
        )

    packed = [pack(0)]
    grad_down = order.mark(dot_tn(order.tie(hidden), rows_grad).astype(BF16))
    grad_sums[1].go()
    packed[0].go()
    grad_in = order.mark(dot_tn(order.tie(normed_two), grad_pre).astype(BF16))
    packed.append(pack(1))

    def over_tokens(part, axis):
        return lax.psum_scatter(
            part.astype(BF16), "tok", scatter_dimension=axis, tiled=True
        ).astype(F32)

    def over_heads(part):
        part = order.tie(part)
        return lax.psum_scatter(part, "head", scatter_dimension=1, tiled=True).astype(F32)

    packed[0].go()
    gather(0, 0, grad_slots, gather_grads)
    packed[1].go()
    grad_down, grad_in = order.tie(grad_down, grad_in)
    grad_down, grad_in = over_tokens(grad_down, 1), over_tokens(grad_in, 0)
    if len(tokens.cuts) > 1:
        gather(0, 1, grad_slots, gather_grads)
    packed[1].go()
    for n in range(len(tokens.cuts)):
        gather(1, n, grad_slots, gather_grads)
    grad_slots = [parts[0] for parts in grad_slots]
    grad_one = over_heads(carried).astype(BF16)

    slot_grads = order.mark(attention_back_call(plan, scalars, slots, grad_slots))
    second = over_heads(second)

    def scatter_back(first, count, h):
        return scatter_back_call(plan, ranks, order.tie(slot_grads), first, count, h)

    mixing = collects(add_up)
    part = scatter(scatter_back, 0, 0)
    mixing[0].send(part)
    if several:
        part = scatter(scatter_back, 0, 1)
        mixing[0].send(part)
    part = scatter(scatter_back, 1, 0)
    mixing[1].send(part)
    next(mixing[0])
    if several:
        part = scatter(scatter_back, 1, 1)
    grads = [next(mixing[0])]
    mixing[1].send(part if several else None)

    def project_back(h):
        *back_one, sums_one = norm_back_call(
            places, head_devices, rows_two[h], vectors, whole_both, list(order.tie(*grads[h]))
            if heads > 1
            else grads[h],
        )
        order.mark(sums_one)
        return back_one, sums_one

    grad_out = order.mark(dot_tn(order.tie(attended), grad_one).astype(BF16))
    if tokens.paired and head_devices == 4:
        grad_out = over_tokens(grad_out, 0).astype(BF16)
        own_part, other_part = [
            lax.ppermute(
                jnp.where(me_tok % 2 == n, grad_out[:, DH:], grad_out[:, :DH]),
                ("head", "tok"),
                [
                    (h * 8 + t, (t // 2) * 8 + 2 * h + (t + 1 - n) % 2)
                    for h in range(4)
                    for t in range(8)
                ],
            )
            for n in (1, 0)
        ]
        odd = me_tok % 2 == 1
        grad_out = jnp.concatenate(
            [jnp.where(odd, other_part, own_part), jnp.where(odd, own_part, other_part)]
        ).astype(F32)
    else:
        out_rows = lax.all_to_all(grad_out, "head", split_axis=0, concat_axis=1, tiled=True)
        grad_out = over_tokens(out_rows, 1)
    back_one, sums_one = project_back(0)
    last_steps = [Steps(sum_terms(order, back_one))]
    last_steps[0].go()
    next(mixing[1])
    grad_both = order.mark(dot_tn(normed[0], order.tie(head_columns(grads[0]))))
    last_steps[0].go()
    grads.append(next(mixing[1]))
    grad_both = grad_both + dot_tn(normed[1], order.tie(head_columns(grads[1])))
    grad_both = over_tokens(order.mark(grad_both.astype(BF16)), 0)
    back_one, sums_two = project_back(1)
    last_steps.append(Steps(sum_terms(order, back_one)))
    last_steps[1].go(2)
    grad_two = [
        (cotangent_two[rows].astype(F32) + add_terms(steps.result)).astype(BF16)
        for rows, steps in zip(halves, last_steps)
    ]
    result_two = (
        stream_two.astype(F32) + second + down_bias.astype(F32)
    ).astype(BF16)
    late = (sums_one + sums_two)[:2].reshape(-1)

    grad_qk, grad_value = [
        jnp.concatenate(
            [grad_both[:, n * DH : (n + 1) * DH] for n in range(first, 2 * heads, 2)], axis=1
        )
        for first in range(2)
    ]

    def place(part):
        whole = jnp.zeros((part.shape[0] * head_devices,), F32)
        return lax.dynamic_update_slice_in_dim(whole, part, me_head * part.shape[0], 0)

    def share(whole):
        size = whole.shape[0] // (head_devices * tok_devices)
        return lax.dynamic_slice_in_dim(whole, (me_head * tok_devices + me_tok) * size, size, 0)

    whole = sum_everywhere(
        jnp.concatenate(
            [
                sums[:2].reshape(-1),
                place(jnp.sum(cotangent_two.astype(F32), axis=0)),
                late,
                place(hidden_sums[0]),
            ]
        )
    )
    gain_two_sum, bias_two_sum, down_sum, gain_one_sum, bias_one_sum = [
        share(whole[n * full_width : (n + 1) * full_width]) for n in range(5)
    ]
    in_sum = share(whole[5 * full_width :])
    return (
        result_one,
        result_two,
        grad_one,
        jnp.concatenate(grad_two),
        gain_one_sum,
        bias_one_sum,
        grad_qk,
        grad_value,
        grad_out,
        gain_two_sum,
        bias_two_sum,
        grad_in,
        in_sum,
        grad_down,
        down_sum,
        bucket_counts,
    )


def solution(mesh):
    wide = P("tok", "head")
    placed = (
        wide, wide, P("tok", None), P(), P("head"), P("head"), wide, wide, P("head", "tok"),
        P("head"), P("head"), wide, P("head"), P("head", "tok"), P("head"), wide, wide,
    )
    vector = P(("head", "tok"))
    return jax.shard_map(
        shards,
        mesh=mesh,
        in_specs=placed,
        out_specs=(
            wide, wide, wide, wide, vector, vector, wide, wide, P("head", "tok"), vector, vector,
            wide, vector, P("head", "tok"), vector, P("tok"),
        ),
        check_vma=False,
    )
```

time: 2860 us -> 805 us (0.28)
  waiting for transfers between devices: 1180 us -> 173 us
  local copies, waits for them, and re-layouts: 764 us -> 51.1 us
  blocking collectives: 488 us -> 0 us
  Pallas kernels: 0 us -> 381 us
  other arithmetic: 195 us -> 52 us
  matrix products: 149 us -> 24.1 us
  starting transfers between devices: 46.6 us -> 97 us
    all_to_all x9 -> x0, waiting for transfers between devices: 658 us -> none  [the longest x1 239 us: shards(): lax.all_to_all(grad_shared_slots.reshape(slot_buckets, CAP, columns), 'to...]
    all_gather x7 -> x0, blocking collectives: 443 us -> none  [the longest x1 260 us: shards(): lax.all_gather(out_weight, 'tok', axis=1, tiled=True)]
    pallas_call x0 -> x33, Pallas kernels: none -> 381 us  [the longest x4 56.3 us: scatter_call(): pl.pallas_call(body, grid=(count,), in_specs=[rank_spec(plan, first, half...]
    gather x9 -> x0, local copies, waits for them, and re-layouts: 358 us -> none  [the longest x2 89.8 us: token_slots(): padded[source_rows].reshape(bucket_total, slot_most, row_block.shape[1])]
    reduce_scatter x8 -> x5, waiting for transfers between devices: 284 us -> 18.2 us  [the longest x3 18.2 us: over_tokens(): lax.psum_scatter(part.astype(BF16), 'tok', scatter_dimension=axis, tiled=...]
    all_gather x8 -> x6, waiting for transfers between devices: 239 us -> 1.39 us  [the longest x1 1.36 us: shards(): lax.all_gather(order.tie(cotangent_two), 'head', axis=1, tiled=True)]
    ppermute x0 -> x74, waiting for transfers between devices: none -> 151 us  [the longest x27 65.4 us: swap(): return lax.ppermute(array_in, 'tok', [(i, i ^ bits) for i in range(8)])]
    dot_general x169 -> x5, matrix products: 149 us -> 24.1 us  [dot_tn(): lax.dot_general(left, right, (((0,), (0,)), ((), ())), preferred_element_...]
  transfers between devices with their start and end apart: 25 -> 86, of which waited for: 17 -> 29; matrix products, arithmetic and copies ran while one was open for 24% -> 13% of each run, Pallas kernels for 0% -> 47%
where the time goes in v2:
time: 805 us; the launch traced here: 793 us
  Pallas kernels  381 us (47%)
  waiting for transfers between devices  173 us (21%)
  starting transfers between devices  97 us (12%)
  other arithmetic  52 us (6%)
  local copies, waits for them, and re-layouts  51.1 us (6%)
  matrix products  24.1 us (3%)
  between operations  15.8 us (2%)
    ppermute x27, waiting for transfers between devices, swap(): return lax.ppermute(array_in, 'tok', [(i, i ^ bits) for i in range(8)])  65.4 us
    pallas_call x4, Pallas kernels, scatter_call(): pl.pallas_call(body, grid=(count,), in_specs=[rank_spec(plan, first, half...  56.3 us
    ppermute x31, waiting for transfers between devices, head_swap(): return lax.ppermute(array_in, 'head', [(i, i ^ bits) for i in range(4)])  54.7 us
    pallas_call x2, Pallas kernels, feed_forward_call(): pl.pallas_call(body, grid_spec=pltpu.PrefetchScalarGridSpec(num_scalar_pr...  50.6 us
    pallas_call x4, Pallas kernels, scatter_back_call(): pl.pallas_call(body, grid=(count,), in_specs=[rank_spec(plan, first, half...  47.4 us
    pallas_call x1, Pallas kernels, attention_back_call(): pl.pallas_call(body, grid_spec=pltpu.PrefetchScalarGridSpec(num_scalar_pr...  46.8 us
    pallas_call x4, Pallas kernels, gather_back_call(): pl.pallas_call(body, grid_spec=pltpu.PrefetchScalarGridSpec(num_scalar_pr...  43.6 us
    ppermute x31, starting transfers between devices, head_swap(): return lax.ppermute(array_in, 'head', [(i, i ^ bits) for i in range(4)])  40.2 us
  transfers between devices with their start and end apart: 86, of which 29 were waited for; matrix products, arithmetic and copies ran while one was open for 13% of the time, Pallas kernels for 47%

profile of v2, /device:TPU:0, one launch (start us, length us, event | category | flops | bytes accessed | tf_op | source)
XLA Modules:
  0.0 793.1 jit_solution(18061838004753516911)
XLA Ops:
  32.8 9.9 %bucket_ranks.1 = (bf16[8,176,2048]{2,1,0:T(8,128)(2,1)}, f32[176,128]{1,0:T(8,128)}, bf16[2,128,128]{2,1,0:T(8,128)(2,1)}) custom-call(s32[10]{0:T(128)} %concatenate.86.scal, f32[8,8,2048]{2,1,0:T(8,128)} %copy-done.20), custom_call_target="tpu_custom_call" | custom-call | tf_op jit(solution)/shard_map/bucket_ranks/pallas_call | solution.py:134
  52.0 10.7 %collective-permute-done.11 = bf16[528,256]{1,0:T(8,128)(2,1)S(1)} collective-permute-done((bf16[528,256]{1,0:T(8,128)(2,1)S(1)}, bf16[528,256]{1,0:T(8,128)(2,1)S(1)}, u32[]{:S(2)}, u32[]{:S(2)}) %collective-permute-start.11) | collective-permute-done | bytes 270368 | tf_op jit(solution)/shard_map/ppermute | solution.py:876
  73.0 14.8 %collective-permute-done.14 = bf16[1024,256]{1,0:T(8,128)(2,1)S(1)} collective-permute-done((bf16[1024,256]{1,0:T(8,128)(2,1)}, bf16[1024,256]{1,0:T(8,128)(2,1)S(1)}, u32[]{:S(2)}, u32[]{:S(2)}) %collective-permute-start.14) | collective-permute-done | bytes 524320 | tf_op jit(solution)/shard_map/ppermute | solution.py:948
  87.8 9.4 %collective-permute-start.16 = (bf16[1024,256]{1,0:T(8,128)(2,1)S(1)}, bf16[1024,256]{1,0:T(8,128)(2,1)S(1)}, u32[]{:S(2)}, u32[]{:S(2)}) collective-permute-start(bf16[1024,256]{1,0:T(8,128)(2,1)S(1)} %collective-permute-done.14), channel_id=1, source_target_pairs={{0,2},{1,3},{2,0},{3,1},{4,6},{5,7},{6,4},{7,5},{8,10},{9,11},{10,... | collective-permute-start | bytes 1572872 | tf_op jit(solution)/shard_map/ppermute | solution.py:945
  116.3 9.0 %gather_slots.4.refs_0_ = bf16[4,2816,256]{2,1,0:T(8,128)(2,1)} custom-call(bf16[8,176,2048]{2,1,0:T(8,128)(2,1)} %get-tuple-element.203.rank_ref, bf16[4,1024,256]{2,1,0:T(8,128)(2,1)} %copy-done.3), custom_call_target="tpu_custom_call" | custom-call | tf_op jit(solution)/shard_map/gather_slots/pallas_call | solution.py:195
  131.9 9.2 %collective-permute-start.17 = (bf16[1024,256]{1,0:T(8,128)(2,1)S(1)}, bf16[1024,256]{1,0:T(8,128)(2,1)}, u32[]{:S(2)}, u32[]{:S(2)}) collective-permute-start(bf16[1024,256]{1,0:T(8,128)(2,1)S(1)} %collective-permute-done.12), channel_id=1, source_target_pairs={{0,2},{1,3},{2,0},{3,1},{4,6},{5,7},{6,4},{7,5},{8,10},{9,11},{10,... | collective-permute-start | bytes 1572872 | tf_op jit(solution)/shard_map/ppermute | solution.py:945
  143.0 9.0 %gather_slots.5.refs_0_ = bf16[4,2816,256]{2,1,0:T(8,128)(2,1)} custom-call(bf16[8,176,2048]{2,1,0:T(8,128)(2,1)} %get-tuple-element.203.rank_ref, bf16[4,1024,256]{2,1,0:T(8,128)(2,1)} %collective-permute-done.18.rows_ref), custom_call_target="tpu_custom_call" | custom-call | tf_op jit(solution)/shard_map/gather_slots/pallas_call | solution.py:195
  157.0 10.1 %gather_slots.6.refs_0_ = bf16[4,2816,256]{2,1,0:T(8,128)(2,1)} custom-call(bf16[8,176,2048]{2,1,0:T(8,128)(2,1)} %get-tuple-element.203.rank_ref, bf16[4,1024,256]{2,1,0:T(8,128)(2,1)} %copy-done.2, bf16[4,2816,256]{2,1,0:T(8,128)(2,1)} %gather_slots.4.refs_0_), custom_call_target="tpu_custom_call" | custom-call | tf_op jit(solution)/shard_map/gather_slots/pallas_call | solution.py:195
  167.1 10.1 %gather_slots.7.refs_1_ = bf16[4,2816,256]{2,1,0:T(8,128)(2,1)} custom-call(bf16[8,176,2048]{2,1,0:T(8,128)(2,1)} %get-tuple-element.203.rank_ref, bf16[4,1024,256]{2,1,0:T(8,128)(2,1)} %collective-permute-done.19.rows_ref, bf16[4,2816,256]{2,1,0:T(8,128)(2,1)} %gather_slots.5.refs_0_), custom_call_target="tpu_custom_call" | custom-call | tf_op jit(solution)/shard_map/gather_slots/pallas_call | solution.py:195
  177.2 37.4 %bucket_attention.1 = (bf16[8,2816,128]{2,1,0:T(8,128)(2,1)}, f32[176,128]{1,0:T(8,128)}) custom-call(s32[10]{0:T(128)} %concatenate.86.scal, bf16[4,2816,256]{2,1,0:T(8,128)(2,1)} %gather_slots.6.refs_0_, bf16[4,2816,256]{2,1,0:T(8,128)(2,1)} %gather_slots.7.refs_1_, f32[176,128]{1,0:T(8,128)} %get-tuple-element.204.refs_2_, ...), custom_call_target="tpu_custom_call" | custom-call | tf_op jit(solution)/shard_map/bucket_attention/pallas_call | solution.py:310
  214.7 14.1 %scatter_results.4 = bf16[4,1056,128]{2,1,0:T(8,128)(2,1)} custom-call(bf16[8,176,2048]{2,1,0:T(8,128)(2,1)} %get-tuple-element.203.rank_ref, bf16[8,2816,128]{2,1,0:T(8,128)(2,1)} %get-tuple-element.253.result_ref, f32[176,128]{1,0:T(8,128)} %get-tuple-element.245.total_ref), custom_call_target="tpu_custom_call" | custom-call | tf_op jit(solution)/shard_map/scatter_results/pallas_call | solution.py:478
  229.2 14.0 %scatter_results.5.refs_0_ = bf16[4,1056,128]{2,1,0:T(8,128)(2,1)} custom-call(bf16[8,176,2048]{2,1,0:T(8,128)(2,1)} %get-tuple-element.203.rank_ref, bf16[8,2816,128]{2,1,0:T(8,128)(2,1)} %get-tuple-element.253.result_ref, f32[176,128]{1,0:T(8,128)} %get-tuple-element.245.total_ref), custom_call_target="tpu_custom_call" | custom-call | tf_op jit(solution)/shard_map/scatter_results/pallas_call | solution.py:478
  248.5 14.1 %scatter_results.6 = bf16[4,1056,128]{2,1,0:T(8,128)(2,1)} custom-call(bf16[8,176,2048]{2,1,0:T(8,128)(2,1)} %get-tuple-element.203.rank_ref, bf16[8,2816,128]{2,1,0:T(8,128)(2,1)} %get-tuple-element.253.result_ref, f32[176,128]{1,0:T(8,128)} %get-tuple-element.245.total_ref), custom_call_target="tpu_custom_call" | custom-call | tf_op jit(solution)/shard_map/scatter_results/pallas_call | solution.py:478
  265.3 12.3 %collective-permute-done.21.refs_1_ = bf16[1,1056,128]{2,1,0:T(8,128)(2,1)S(1)} collective-permute-done((bf16[1,1056,128]{2,1,0:T(8,128)(2,1)S(1)}, bf16[1,1056,128]{2,1,0:T(8,128)(2,1)S(1)}, u32[]{:S(2)}, u32[]{:S(2)}) %collective-permute-start.21) | collective-permute-done | bytes 270368 | tf_op jit(solution)/shard_map/ppermute | solution.py:945
  284.3 14.0 %scatter_results.7.refs_0_ = bf16[4,1056,128]{2,1,0:T(8,128)(2,1)} custom-call(bf16[8,176,2048]{2,1,0:T(8,128)(2,1)} %get-tuple-element.203.rank_ref, bf16[8,2816,128]{2,1,0:T(8,128)(2,1)} %get-tuple-element.253.result_ref, f32[176,128]{1,0:T(8,128)} %get-tuple-element.245.total_ref), custom_call_target="tpu_custom_call" | custom-call | tf_op jit(solution)/shard_map/scatter_results/pallas_call | solution.py:478
  312.7 8.7 %collective-permute-done.26.refs_1_ = bf16[1024,256]{1,0:T(8,128)(2,1)S(1)} collective-permute-done((bf16[1024,256]{1,0:T(8,128)(2,1)S(1)}, bf16[1024,256]{1,0:T(8,128)(2,1)S(1)}, u32[]{:S(2)}, u32[]{:S(2)}) %collective-permute-start.26) | collective-permute-done | bytes 524320 | tf_op jit(solution)/shard_map/ppermute | solution.py:876
  347.9 25.0 %feed_forward.2 = (bf16[2048,1024]{1,0:T(8,128)(2,1)}, bf16[2048,256]{1,0:T(8,128)(2,1)}, bf16[2048,1024]{1,0:T(8,128)(2,1)}, bf16[2048,1024]{1,0:T(8,128)(2,1)}...) custom-call(s32[2]{0:T(128)} %pad_add_fusion.places, ...), custom_call_target="tpu_custom_call" | custom-call | tf_op jit(solution)/shard_map/feed_forward/pallas_call | solution.py:824
  378.7 25.6 %feed_forward.3 = (bf16[2048,1024]{1,0:T(8,128)(2,1)}, bf16[2048,256]{1,0:T(8,128)(2,1)}, bf16[2048,1024]{1,0:T(8,128)(2,1)}, bf16[2048,1024]{1,0:T(8,128)(2,1)}...) custom-call(s32[2]{0:T(128)} %pad_add_fusion.places, ...), custom_call_target="tpu_custom_call", output_to_operand_aliasing={{0}: (13, {}), {1}: (14, {}), {2}: (15, {}), {3}: (16, {}),... | custom-call | tf_op jit(solution)/shard_map/feed_forward/pallas_call | solution.py:824
  424.1 8.2 %convolution_convert_fusion.1 = bf16[1024,1024]{1,0:T(8,128)(2,1)S(1)} fusion(bf16[2048,1024]{1,0:T(8,128)(2,1)} %get-tuple-element.307, bf16[2048,1024]{1,0:T(8,128)(2,1)} %all-gather.11.cloned.1.call-done.refs_5_), kind=kOutput, calls=%fused_computation.9 | convolution fusion | flops 4296015872 | bytes 10485760 | tf_op jit(solution)/shard_map/dot_general | solution.py:38
  456.2 10.4 %gather_gradient.4.refs_0_ = bf16[4,2816,256]{2,1,0:T(8,128)(2,1)} custom-call(s32[10]{0:T(128)} %concatenate.86.scal, bf16[8,176,2048]{2,1,0:T(8,128)(2,1)} %get-tuple-element.203.rank_ref, bf16[4,1072,128]{2,1,0:T(8,128)(2,1)} %copy-done.10), custom_call_target="tpu_custom_call" | custom-call | tf_op jit(solution)/shard_map/gather_gradient/pallas_call | solution.py:235
  470.0 10.6 %gather_gradient.5.refs_0_ = bf16[4,2816,256]{2,1,0:T(8,128)(2,1)} custom-call(s32[10]{0:T(128)} %concatenate.86.scal, bf16[8,176,2048]{2,1,0:T(8,128)(2,1)} %get-tuple-element.203.rank_ref, bf16[4,1072,128]{2,1,0:T(8,128)(2,1)} %collective-permute-done.49.ref), custom_call_target="tpu_custom_call" | custom-call | tf_op jit(solution)/shard_map/gather_gradient/pallas_call | solution.py:235
  482.8 11.2 %gather_gradient.6.refs_2_ = bf16[4,2816,256]{2,1,0:T(8,128)(2,1)} custom-call(s32[10]{0:T(128)} %concatenate.86.scal, bf16[8,176,2048]{2,1,0:T(8,128)(2,1)} %get-tuple-element.203.rank_ref, bf16[4,1072,128]{2,1,0:T(8,128)(2,1)} %copy-done.11, bf16[4,2816,256]{2,1,0:T(8,128)(2,1)} %gather_gradient.4.refs_0_), custom_call_target="tpu_custom_call" | custom-call | tf_op jit(solution)/shard_map/gather_gradient/pallas_call | solution.py:235
  494.0 11.3 %gather_gradient.7.refs_3_ = bf16[4,2816,256]{2,1,0:T(8,128)(2,1)} custom-call(s32[10]{0:T(128)} %concatenate.86.scal, bf16[8,176,2048]{2,1,0:T(8,128)(2,1)} %get-tuple-element.203.rank_ref, bf16[4,1072,128]{2,1,0:T(8,128)(2,1)} %collective-permute-done.50.ref, bf16[4,2816,256]{2,1,0:T(8,128)(2,1)} %gather_gradient.5.refs_0_), custom_call_target="tpu_custom_call" | custom-call | tf_op jit(solution)/shard_map/gather_gradient/pallas_call | solution.py:235
  508.7 46.8 %bucket_attention_back.1.grad_ref = bf16[8,2816,256]{2,1,0:T(8,128)(2,1)} custom-call(s32[10]{0:T(128)} %concatenate.86.scal, bf16[4,2816,256]{2,1,0:T(8,128)(2,1)} %gather_slots.6.refs_0_, bf16[4,2816,256]{2,1,0:T(8,128)(2,1)} %gather_slots.7.refs_1_, bf16[4,2816,256]{2,1,0:T(8,128)(2,1)} %gather_gradient.6.refs_2_, ...), custom_call_target="tpu_custom_call" | custom-call | tf_op jit(solution)/shard_map/bucket_attention_back/pallas_call | solution.py:391
  555.6 11.9 %scatter_gradient.4 = bf16[4,1024,256]{2,1,0:T(8,128)(2,1)} custom-call(bf16[8,176,2048]{2,1,0:T(8,128)(2,1)} %get-tuple-element.203.rank_ref, bf16[8,2816,256]{2,1,0:T(8,128)(2,1)} %bucket_attention_back.1.grad_ref), custom_call_target="tpu_custom_call" | custom-call | tf_op jit(solution)/shard_map/scatter_gradient/pallas_call | solution.py:504
  567.5 11.7 %scatter_gradient.5 = bf16[4,1024,256]{2,1,0:T(8,128)(2,1)} custom-call(bf16[8,176,2048]{2,1,0:T(8,128)(2,1)} %get-tuple-element.203.rank_ref, bf16[8,2816,256]{2,1,0:T(8,128)(2,1)} %bucket_attention_back.1.grad_ref), custom_call_target="tpu_custom_call" | custom-call | tf_op jit(solution)/shard_map/scatter_gradient/pallas_call | solution.py:504
  581.9 11.8 %scatter_gradient.6 = bf16[4,1024,256]{2,1,0:T(8,128)(2,1)} custom-call(bf16[8,176,2048]{2,1,0:T(8,128)(2,1)} %get-tuple-element.203.rank_ref, bf16[8,2816,256]{2,1,0:T(8,128)(2,1)} %bucket_attention_back.1.grad_ref), custom_call_target="tpu_custom_call" | custom-call | tf_op jit(solution)/shard_map/scatter_gradient/pallas_call | solution.py:504
  595.3 19.8 %collective-permute-done.52 = bf16[1,1024,256]{2,1,0:T(8,128)(2,1)S(1)} collective-permute-done((bf16[1,1024,256]{2,1,0:T(8,128)(2,1)S(1)}, bf16[1,1024,256]{2,1,0:T(8,128)(2,1)S(1)}, u32[]{:S(2)}, u32[]{:S(2)}) %collective-permute-start.52) | collective-permute-done | bytes 524320 | tf_op jit(solution)/shard_map/ppermute | solution.py:945
  618.8 12.0 %scatter_gradient.7 = bf16[4,1024,256]{2,1,0:T(8,128)(2,1)} custom-call(bf16[8,176,2048]{2,1,0:T(8,128)(2,1)} %get-tuple-element.203.rank_ref, bf16[8,2816,256]{2,1,0:T(8,128)(2,1)} %bucket_attention_back.1.grad_ref), custom_call_target="tpu_custom_call" | custom-call | tf_op jit(solution)/shard_map/scatter_gradient/pallas_call | solution.py:504
  630.8 20.5 %collective-permute-done.53 = bf16[1,1024,256]{2,1,0:T(8,128)(2,1)S(1)} collective-permute-done((bf16[1,1024,256]{2,1,0:T(8,128)(2,1)}, bf16[1,1024,256]{2,1,0:T(8,128)(2,1)S(1)}, u32[]{:S(2)}, u32[]{:S(2)}) %collective-permute-start.53) | collective-permute-done | bytes 524320 | tf_op jit(solution)/shard_map/ppermute | solution.py:945
  680.9 14.5 %collective-permute-done.56 = bf16[512,512]{1,0:T(8,128)(2,1)} collective-permute-done((bf16[512,512]{1,0:T(8,128)(2,1)}, bf16[512,512]{1,0:T(8,128)(2,1)}, u32[]{:S(2)}, u32[]{:S(2)}) %collective-permute-start.56) | collective-permute-done | bytes 524320 | tf_op jit(solution)/shard_map/ppermute | solution.py:876
  768.0 15.7 %reduce-scatter.13.cloned.1.call-done = bf16[128,512]{1,0:T(8,128)(2,1)} async-done(((bf16[1024,512]{1,0:T(8,128)(2,1)}), bf16[128,512]{1,0:T(8,128)(2,1)}) %reduce-scatter.13.cloned.1.call-update) | async-done | bytes 131088 | tf_op jit(solution)/shard_map/reduce_scatter | solution.py:1259
  (442 shorter events, 303.4 us)
Async XLA Ops:
  7.2 57.0 %all-gather.7.cloned.1.call-start = ((), (), s32[]{:S(2)}) async-start(), calls=%async_computation.6 | async-start | bytes 1179648 | tf_op jit(solution)/shard_map/all_gather | solution.py:1074
  8.8 132.3 %all-gather.13.cloned.1.call-start = ((), (), s32[]{:S(2)}) async-start(), calls=%async_computation.9 | async-start | bytes 2949120 | tf_op jit(solution)/shard_map/all_gather | solution.py:1076
  23.0 323.5 %all-gather.15.cloned.1.call-start = ((), (), s32[]{:S(2)}) async-start(), calls=%async_computation.10 | async-start | bytes 2621440 | tf_op jit(solution)/shard_map/all_gather | solution.py:1144
  73.0 39.4 %collective-permute-start.15 = (bf16[1024,256]{1,0:T(8,128)(2,1)}, bf16[1024,256]{1,0:T(8,128)(2,1)S(1)}, u32[]{:S(2)}, u32[]{:S(2)}) collective-permute-start(bf16[1024,256]{1,0:T(8,128)(2,1)} %get-tuple-element.230), channel_id=1, source_target_pairs={{0,2},{1,3},{2,0},{3,1},{4,6},{5,7},{6,4},{7,5},{8,10},{9,11},{10,... | collective-permute-start | bytes 1572872 | tf_op jit(solution)/shard_map/ppermute | solution.py:945
  87.8 24.6 %collective-permute-start.16 = (bf16[1024,256]{1,0:T(8,128)(2,1)S(1)}, bf16[1024,256]{1,0:T(8,128)(2,1)S(1)}, u32[]{:S(2)}, u32[]{:S(2)}) collective-permute-start(bf16[1024,256]{1,0:T(8,128)(2,1)S(1)} %collective-permute-done.14), channel_id=1, source_target_pairs={{0,2},{1,3},{2,0},{3,1},{4,6},{5,7},{6,4},{7,5},{8,10},{9,11},{10,... | collective-permute-start | bytes 1572872 | tf_op jit(solution)/shard_map/ppermute | solution.py:945
  115.0 28.0 %collective-permute-start.18 = (bf16[4,1024,256]{2,1,0:T(8,128)(2,1)S(1)}, bf16[4,1024,256]{2,1,0:T(8,128)(2,1)}, u32[]{:S(2)}, u32[]{:S(2)}) collective-permute-start(bf16[4,1024,256]{2,1,0:T(8,128)(2,1)S(1)} %pad_maximum_fusion.rows_ref), channel_id=1, source_target_pairs={{0,1},{1,0},{2,3},{3,2},{4,5},{5,4},{6,7},{7,6},{8,9},{9,8},{10,11... | collective-permute-start | bytes 6291464 | tf_op jit(solution)/shard_map/ppermute | solution.py:945
  115.6 36.3 %collective-permute-start.13 = (bf16[1024,256]{1,0:T(8,128)(2,1)S(1)}, bf16[1024,256]{1,0:T(8,128)(2,1)}, u32[]{:S(2)}, u32[]{:S(2)}) collective-permute-start(bf16[1024,256]{1,0:T(8,128)(2,1)S(1)} %copy-done.43), channel_id=1, source_target_pairs={{0,2},{1,3},{2,0},{3,1},{4,6},{5,7},{6,4},{7,5},{8,10},{9,11},{10,... | collective-permute-start | bytes 1572872 | tf_op jit(solution)/shard_map/ppermute | solution.py:945
  154.6 192.0 %all-gather.9.cloned.1.call-start = ((), (), s32[]{:S(2)}) async-start(), calls=%async_computation.7 | async-start | bytes 5242880 | tf_op jit(solution)/shard_map/all_gather | solution.py:1135
  155.2 191.4 %all-gather.17.cloned.1.call-start = ((), (), s32[]{:S(2)}) async-start(), calls=%async_computation.11 | async-start | bytes 2359296 | tf_op jit(solution)/shard_map/all_gather | solution.py:1142
  156.1 191.8 %all-gather.11.cloned.1.call-start = ((), (), s32[]{:S(2)}) async-start(), calls=%async_computation.8 | async-start | bytes 5242880 | tf_op jit(solution)/shard_map/all_gather | solution.py:1143
  156.7 499.4 %reduce-scatter.11.cloned.1.call-start = ((), (), s32[]{:S(2)}) async-start(), calls=%async_computation.13 | async-start | bytes 5242880 | tf_op jit(solution)/shard_map/reduce_scatter | solution.py:1265
  262.6 42.5 %collective-permute-start.22 = (bf16[4,1056,128]{2,1,0:T(8,128)(2,1)}, bf16[4,1056,128]{2,1,0:T(8,128)(2,1)S(1)}, u32[]{:S(2)}, u32[]{:S(2)}) collective-permute-start(bf16[4,1056,128]{2,1,0:T(8,128)(2,1)} %scatter_results.6), channel_id=1, source_target_pairs={{0,1},{1,0},{2,3},{3,2},{4,5},{5,4},{6,7},{7,6},{8,9},{9,8},{10,11... | collective-permute-start | bytes 3244040 | tf_op jit(solution)/shard_map/ppermute | solution.py:945
  343.0 34.6 %collective-permute-start.32 = (bf16[1024,256]{1,0:T(8,128)(2,1)S(1)}, bf16[1024,256]{1,0:T(8,128)(2,1)S(1)}, u32[]{:S(2)}, u32[]{:S(2)}) collective-permute-start(bf16[1024,256]{1,0:T(8,128)(2,1)S(1)} %pad_maximum_fusion.10.refs_0_), channel_id=1, source_target_pairs={{0,8},{8,0},{16,24},{24,16},{1,9},{9,1},{17,25},{25,17},{2,10},{10... | collective-permute-start | bytes 1572872 | tf_op jit(solution)/shard_map/ppermute | solution.py:876
  345.0 32.5 %collective-permute-start.33 = (bf16[1024,256]{1,0:T(8,128)(2,1)S(1)}, bf16[1024,256]{1,0:T(8,128)(2,1)S(1)}, u32[]{:S(2)}, u32[]{:S(2)}) collective-permute-start(bf16[1024,256]{1,0:T(8,128)(2,1)S(1)} %pad_maximum_fusion.10.refs_0_), channel_id=1, source_target_pairs={{0,16},{8,24},{16,0},{24,8},{1,17},{9,25},{17,1},{25,9},{2,18},{10... | collective-permute-start | bytes 1572872 | tf_op jit(solution)/shard_map/ppermute | solution.py:876
  345.1 32.5 %collective-permute-start.34 = (bf16[1024,256]{1,0:T(8,128)(2,1)S(1)}, bf16[1024,256]{1,0:T(8,128)(2,1)S(1)}, u32[]{:S(2)}, u32[]{:S(2)}) collective-permute-start(bf16[1024,256]{1,0:T(8,128)(2,1)S(1)} %pad_maximum_fusion.10.refs_0_), channel_id=1, source_target_pairs={{0,24},{8,16},{16,8},{24,0},{1,25},{9,17},{17,9},{25,1},{2,26},{10... | collective-permute-start | bytes 1572872 | tf_op jit(solution)/shard_map/ppermute | solution.py:876
  375.2 30.0 %collective-permute-start.35 = (bf16[512,512]{1,0:T(8,128)(2,1)}, bf16[512,512]{1,0:T(8,128)(2,1)}, u32[]{:S(2)}, u32[]{:S(2)}) collective-permute-start(bf16[512,512]{1,0:T(8,128)(2,1)} %get-tuple-element.426), channel_id=1, source_target_pairs={{0,8},{8,0},{16,24},{24,16},{1,9},{9,1},{17,25},{25,17},{2,10},{10... | collective-permute-start | bytes 1572872 | tf_op jit(solution)/shard_map/ppermute | solution.py:876
  376.1 29.1 %collective-permute-start.36 = (bf16[512,512]{1,0:T(8,128)(2,1)}, bf16[512,512]{1,0:T(8,128)(2,1)}, u32[]{:S(2)}, u32[]{:S(2)}) collective-permute-start(bf16[512,512]{1,0:T(8,128)(2,1)} %get-tuple-element.425), channel_id=1, source_target_pairs={{0,16},{8,24},{16,0},{24,8},{1,17},{9,25},{17,1},{25,9},{2,18},{10... | collective-permute-start | bytes 1572872 | tf_op jit(solution)/shard_map/ppermute | solution.py:876
  424.1 25.9 %collective-permute-start.46 = (bf16[1072,128]{1,0:T(8,128)(2,1)}, bf16[1072,128]{1,0:T(8,128)(2,1)}, u32[]{:S(2)}, u32[]{:S(2)}) collective-permute-start(bf16[1072,128]{1,0:T(8,128)(2,1)} %get-tuple-element.321), channel_id=1, source_target_pairs={{0,2},{1,3},{2,0},{3,1},{4,6},{5,7},{6,4},{7,5},{8,10},{9,11},{10,... | collective-permute-start | bytes 823304 | tf_op jit(solution)/shard_map/ppermute | solution.py:945
  455.4 25.3 %collective-permute-start.44 = (bf16[1072,128]{1,0:T(8,128)(2,1)}, bf16[1072,128]{1,0:T(8,128)(2,1)S(1)}, u32[]{:S(2)}, u32[]{:S(2)}) collective-permute-start(bf16[1072,128]{1,0:T(8,128)(2,1)} %get-tuple-element.328), channel_id=1, source_target_pairs={{0,2},{1,3},{2,0},{3,1},{4,6},{5,7},{6,4},{7,5},{8,10},{9,11},{10,... | collective-permute-start | bytes 823304 | tf_op jit(solution)/shard_map/ppermute | solution.py:945
  505.3 210.3 %reduce-scatter.19.cloned.1.call-start = ((), (), s32[]{:S(2)}) async-start(), calls=%async_computation.17 | async-start | bytes 2359296
  507.9 209.6 %reduce-scatter.17.cloned.1.call-start = ((), (), s32[]{:S(2)}) async-start(), calls=%async_computation.16 | async-start | bytes 2359296 | tf_op jit(solution)/shard_map/reduce_scatter | solution.py:1259
  508.7 216.3 %reduce-scatter.9.cloned.1.call-start = ((), (), s32[]{:S(2)}) async-start(), calls=%async_computation.12 | async-start | bytes 5242880 | tf_op jit(solution)/shard_map/reduce_scatter | solution.py:1265
  555.5 194.7 %reduce-scatter.15.cloned.1.call-start = ((), (), s32[]{:S(2)}) async-start(), calls=%async_computation.15 | async-start | bytes 589824 | tf_op jit(solution)/shard_map/reduce_scatter | solution.py:1259
  593.7 58.6 %collective-permute-start.55 = (bf16[4,1024,256]{2,1,0:T(8,128)(2,1)}, bf16[4,1024,256]{2,1,0:T(8,128)(2,1)}, u32[]{:S(2)}, u32[]{:S(2)}) collective-permute-start(bf16[4,1024,256]{2,1,0:T(8,128)(2,1)} %scatter_gradient.6), channel_id=1, source_target_pairs={{0,1},{1,0},{2,3},{3,2},{4,5},{5,4},{6,7},{7,6},{8,9},{9,8},{10,11... | collective-permute-start | bytes 6291464 | tf_op jit(solution)/shard_map/ppermute | solution.py:945
  615.2 36.0 %collective-permute-start.54 = (bf16[1,1024,256]{2,1,0:T(8,128)(2,1)S(1)}, bf16[1,1024,256]{2,1,0:T(8,128)(2,1)S(1)}, u32[]{:S(2)}, u32[]{:S(2)}) collective-permute-start(bf16[1,1024,256]{2,1,0:T(8,128)(2,1)S(1)} %add_convert_fusion.9), channel_id=1, source_target_pairs={{0,6},{1,7},{2,4},{3,5},{4,2},{5,3},{6,0},{7,1},{8,14},{9,15},{10,... | collective-permute-start | bytes 1572872 | tf_op jit(solution)/shard_map/ppermute | solution.py:948
  616.4 34.9 %collective-permute-start.53 = (bf16[1,1024,256]{2,1,0:T(8,128)(2,1)}, bf16[1,1024,256]{2,1,0:T(8,128)(2,1)S(1)}, u32[]{:S(2)}, u32[]{:S(2)}) collective-permute-start(bf16[1,1024,256]{2,1,0:T(8,128)(2,1)} %get-tuple-element.346), channel_id=1, source_target_pairs={{0,2},{1,3},{2,0},{3,1},{4,6},{5,7},{6,4},{7,5},{8,10},{9,11},{10,... | collective-permute-start | bytes 1572872 | tf_op jit(solution)/shard_map/ppermute | solution.py:945
  670.5 24.8 %collective-permute-start.56 = (bf16[512,512]{1,0:T(8,128)(2,1)}, bf16[512,512]{1,0:T(8,128)(2,1)}, u32[]{:S(2)}, u32[]{:S(2)}) collective-permute-start(bf16[512,512]{1,0:T(8,128)(2,1)} %get-tuple-element.414), channel_id=1, source_target_pairs={{0,8},{8,0},{16,24},{24,16},{1,9},{9,1},{17,25},{25,17},{2,10},{10... | collective-permute-start | bytes 1572872 | tf_op jit(solution)/shard_map/ppermute | solution.py:876
  670.6 24.7 %collective-permute-start.57 = (bf16[512,512]{1,0:T(8,128)(2,1)}, bf16[512,512]{1,0:T(8,128)(2,1)S(1)}, u32[]{:S(2)}, u32[]{:S(2)}) collective-permute-start(bf16[512,512]{1,0:T(8,128)(2,1)} %get-tuple-element.413), channel_id=1, source_target_pairs={{0,16},{8,24},{16,0},{24,8},{1,17},{9,25},{17,1},{25,9},{2,18},{10... | collective-permute-start | bytes 1572872 | tf_op jit(solution)/shard_map/ppermute | solution.py:876
  673.7 25.0 %collective-permute-start.62 = (bf16[1,1024,256]{2,1,0:T(8,128)(2,1)}, bf16[1,1024,256]{2,1,0:T(8,128)(2,1)S(1)}, u32[]{:S(2)}, u32[]{:S(2)}) collective-permute-start(bf16[1,1024,256]{2,1,0:T(8,128)(2,1)} %add_convert_fusion.7), channel_id=1, source_target_pairs={{0,6},{1,7},{2,4},{3,5},{4,2},{5,3},{6,0},{7,1},{8,14},{9,15},{10,... | collective-permute-start | bytes 1572872 | tf_op jit(solution)/shard_map/ppermute | solution.py:948
  677.7 106.0 %reduce-scatter.13.cloned.1.call-start = ((), (), s32[]{:S(2)}) async-start(), calls=%async_computation.14 | async-start | bytes 1179648 | tf_op jit(solution)/shard_map/reduce_scatter | solution.py:1259
  720.9 26.7 %collective-permute-start.63 = (bf16[512,512]{1,0:T(8,128)(2,1)}, bf16[512,512]{1,0:T(8,128)(2,1)}, u32[]{:S(2)}, u32[]{:S(2)}) collective-permute-start(bf16[512,512]{1,0:T(8,128)(2,1)} %get-tuple-element.412), channel_id=1, source_target_pairs={{0,8},{8,0},{16,24},{24,16},{1,9},{9,1},{17,25},{25,17},{2,10},{10... | collective-permute-start | bytes 1572872 | tf_op jit(solution)/shard_map/ppermute | solution.py:876
  721.2 26.4 %collective-permute-start.64 = (bf16[512,512]{1,0:T(8,128)(2,1)}, bf16[512,512]{1,0:T(8,128)(2,1)}, u32[]{:S(2)}, u32[]{:S(2)}) collective-permute-start(bf16[512,512]{1,0:T(8,128)(2,1)} %get-tuple-element.411), channel_id=1, source_target_pairs={{0,16},{8,24},{16,0},{24,8},{1,17},{9,25},{17,1},{25,9},{2,18},{10... | collective-permute-start | bytes 1572872 | tf_op jit(solution)/shard_map/ppermute | solution.py:876
  (114 other events, 1400.0 us)
Sparse Core Ops, SparseCore 0:
  10.2 25.9 all-gather.6
  37.9 33.3 all-gather.12
  154.7 34.1 all-gather.14
  190.6 52.5 all-gather.8
  244.7 31.2 all-gather.16
  277.6 70.2 all-gather.10
  505.4 50.4 reduce-scatter.10
  558.4 35.8 reduce-scatter.18
  596.6 51.8 reduce-scatter.16
  651.6 65.2 reduce-scatter.8
  719.2 30.9 reduce-scatter.14
  752.4 31.2 reduce-scatter.12
